TPU v7x, 32 devices: a whole 2x2x4 slice. The times are simulated.
32 devices in a mesh: dp: 4 (over z), wide: 2 (over x), narrow: 4 (over y, core).
Axes of the slice: x: 2, y: 2, z: 4, core: 2. Of those that a mesh axis runs over, the one named last changes fastest.
Arguments:
- tokens: bfloat16 [25216, 512], P(('dp', 'wide', 'narrow')), may hold values from -6 to 6
- grad_out: bfloat16 [25216, 512], P(('dp', 'wide', 'narrow')), may hold values from -6 to 6
- gates: float32 [25216, 2], P(('dp', 'wide', 'narrow')), may hold values from 0.25 to 0.75
- routes: int32 [25216, 2], P(('dp', 'wide', 'narrow')), may hold values from 0 to 31, all different within a row; in each aligned block of 788 rows (0 to 787, 788 to 1575, ...) at most 66 rows name the same one
- ln1_gain: float32 [512], replicated, may hold values from 0.5 to 1.5
- ln1_bias: float32 [512], replicated, may hold values from -1 to 1
- ln2_gain: float32 [512], replicated, may hold values from 0.5 to 1.5
- ln2_bias: float32 [512], replicated, may hold values from -1 to 1
- w_qkv: bfloat16 [3, 512, 512], P(None, 'wide', 'narrow'), may hold values from -0.25 to 0.25
- w_attn_out: bfloat16 [512, 512], P('narrow', 'wide'), may hold values from -1 to 1
- w_expert_in: bfloat16 [32, 512, 2048], P(None, 'wide', 'narrow'), may hold values from -0.25 to 0.25
- w_expert_out: bfloat16 [32, 2048, 512], P(None, 'narrow', 'wide'), may hold values from -0.125 to 0.125
Outputs:
- mixed: bfloat16 [25216, 512], P(('dp', 'wide', 'narrow'))
- grad_input: float32 [25216, 512], P(('dp', 'wide', 'narrow'))
- grad_ln1_gain: float32 [512], replicated
- grad_ln1_bias: float32 [512], replicated
- grad_ln2_gain: float32 [512], replicated
- grad_ln2_bias: float32 [512], replicated
- grad_qkv: float32 [3, 512, 512], P(None, 'wide', 'narrow')
- grad_attn_out: float32 [512, 512], P('narrow', 'wide')
- grad_expert_in: float32 [32, 512, 2048], P(None, 'wide', 'narrow')
- grad_expert_out: float32 [32, 2048, 512], P(None, 'narrow', 'wide')
Inputs may be any that keep to these rules, and one draw needn't show every extreme that they name: `routes`: the two ids of a row differ. Within the rows of one device no expert is named more than 66 times, a bound that some block reaches.
All inputs are finite; a program needn't handle non-finite values.
Results may differ from a plain program's by a relative error of at most 0.019.
Values may be sent and summed in bfloat16 or wider, within the bound.
No kernel may reach another device: no remote copies, remote signals or barrier semaphores. Data moves between devices by JAX's collectives and lax.ppermute only.
A program may use at most 256 MiB of HBM per device.

v0:
```python
import jax
import jax.numpy as jnp
from jax import lax
from jax.sharding import PartitionSpec as P

HEAD_DIM = 64
EXPERTS = 32
TOP = 2
SEQ = 197
IMG_STEP = 4
CAP = 66


norm_eps = 1e-06


def normalize(values, norm_gain, norm_shift):
    average = jnp.mean(values, axis=-1, keepdims=True)
    centered = values - average
    scaled = centered * lax.rsqrt(jnp.mean(centered * centered, axis=-1, keepdims=True) + norm_eps)
    return scaled * norm_gain + norm_shift


def route_slots(routes):
    flat_ids = routes.reshape(-1)
    onehot = (flat_ids[:, None] == jnp.arange(EXPERTS, dtype=jnp.int32)[None, :]).astype(jnp.int32)
    order_rank = jnp.sum(
        (jnp.cumsum(onehot, axis=0, dtype=jnp.int32) - 1) * onehot, axis=1, dtype=jnp.int32
    )
    slot_ids = order_rank * EXPERTS + flat_ids
    entry_count = flat_ids.shape[0]
    sources = (
        jnp.full((CAP * EXPERTS,), entry_count, jnp.int32)
        .at[slot_ids]
        .set(jnp.arange(entry_count, dtype=jnp.int32))
    )
    return (slot_ids.reshape(routes.shape), sources)


def narrow_rows(values):
    return lax.all_gather(values, "narrow", axis=0, tiled=True)


def narrow_sums(values):
    return lax.psum_scatter(
        values.astype(jnp.bfloat16), "narrow", scatter_dimension=0, tiled=True
    ).astype(jnp.float32)


def attention_forward(query, keys, values, head_count):
    row_count = query.shape[0]
    group_count = row_count // (IMG_STEP * SEQ)
    block_shape = (group_count, IMG_STEP, SEQ, head_count, HEAD_DIM)
    score_scale = HEAD_DIM ** (-0.5)

    def one_group(block):
        query_blk, key_blk, value_blk = block
        scores = (
            jnp.einsum("ishd,ithd->ihst", query_blk, key_blk, preferred_element_type=jnp.float32)
            * score_scale
        )
        row_top = jnp.max(scores, axis=-1, keepdims=True)
        weights = jnp.exp(scores - row_top)
        row_total = jnp.sum(weights, axis=-1, keepdims=True)
        probs = weights / row_total
        output = jnp.einsum(
            "ihst,ithd->ishd",
            probs.astype(jnp.bfloat16),
            value_blk,
            preferred_element_type=jnp.float32,
        )
        return (output.astype(jnp.bfloat16), (row_top + jnp.log(row_total))[..., 0])

    output, log_total = lax.map(
        one_group,
        (query.reshape(block_shape), keys.reshape(block_shape), values.reshape(block_shape)),
    )
    return (output.reshape(row_count, head_count * HEAD_DIM), log_total)


def attention_backward(query, keys, values, grad_att, log_total, head_count):
    row_count = query.shape[0]
    group_count = row_count // (IMG_STEP * SEQ)
    block_shape = (group_count, IMG_STEP, SEQ, head_count, HEAD_DIM)
    score_scale = HEAD_DIM ** (-0.5)

    def one_group(block):
        query_blk, key_blk, value_blk, grad_blk, total_blk = block
        scores = (
            jnp.einsum("ishd,ithd->ihst", query_blk, key_blk, preferred_element_type=jnp.float32)
            * score_scale
        )
        probs = jnp.exp(scores - total_blk[..., None])
        dprobs = jnp.einsum(
            "ishd,ithd->ihst", grad_blk, value_blk, preferred_element_type=jnp.float32
        )
        inner = jnp.sum(probs * dprobs, axis=-1, keepdims=True)
        grad_scores = (probs * (dprobs - inner)).astype(jnp.bfloat16)
        grad_query = (
            jnp.einsum("ihst,ithd->ishd", grad_scores, key_blk, preferred_element_type=jnp.float32)
            * score_scale
        )
        grad_key = (
            jnp.einsum(
                "ihst,ishd->ithd", grad_scores, query_blk, preferred_element_type=jnp.float32
            )
            * score_scale
        )
        grad_value = jnp.einsum(
            "ihst,ishd->ithd",
            probs.astype(jnp.bfloat16),
            grad_blk,
            preferred_element_type=jnp.float32,
        )
        return (
            grad_query.astype(jnp.bfloat16),
            grad_key.astype(jnp.bfloat16),
            grad_value.astype(jnp.bfloat16),
        )

    pieces = lax.map(
        one_group,
        (
            query.reshape(block_shape),
            keys.reshape(block_shape),
            values.reshape(block_shape),
            grad_att.reshape(block_shape),
            log_total,
        ),
    )
    return jnp.stack([piece.reshape(row_count, head_count * HEAD_DIM) for piece in pieces])


def on_device(
    tokens,
    grad_out,
    gates,
    routes,
    ln1_gain,
    ln1_bias,
    ln2_gain,
    ln2_bias,
    w_qkv,
    w_attn_out,
    w_expert_in,
    w_expert_out,
):
    stream = tokens.astype(jnp.float32)
    feature_count = stream.shape[1]
    normed = normalize(stream, ln1_gain, ln1_bias).astype(jnp.bfloat16)
    qkv_part, out_part = (
        lax.all_gather(w_qkv, "wide", axis=1, tiled=True),
        lax.all_gather(w_attn_out, "wide", axis=1, tiled=True),
    )
    qkv_full, out_full = (qkv_part, out_part)
    att_rows = narrow_rows(normed)
    projected = jnp.einsum(
        "rd,jdc->jrc", att_rows, qkv_full, preferred_element_type=jnp.float32
    ).astype(jnp.bfloat16)
    head_count = projected.shape[2] // HEAD_DIM
    attended, log_total = attention_forward(projected[0], projected[1], projected[2], head_count)
    branch = jnp.dot(attended, out_full, preferred_element_type=jnp.float32)
    att_sum = narrow_sums(branch)
    resid = stream + att_sum
    normed_two = normalize(resid, ln2_gain, ln2_bias).astype(jnp.bfloat16)
    slot_ids, sources = route_slots(routes)
    owner_rows = sources // TOP
    padded = jnp.concatenate([normed_two, jnp.zeros((1, feature_count), jnp.bfloat16)], axis=0)
    dispatched = padded[owner_rows].reshape(CAP, EXPERTS, feature_count)
    gathered_slots = narrow_rows(dispatched)
    in_full, down_full = (
        lax.all_gather(w_expert_in, "wide", axis=1, tiled=True),
        lax.all_gather(w_expert_out, "wide", axis=2, tiled=True),
    )
    down_form = "cef,efd->ced"
    back_form = "ced,efd->cef"
    grad_down_form = "cef,ced->efd"
    preact = jnp.einsum("ced,edf->cef", gathered_slots, in_full, preferred_element_type=jnp.float32)
    activated = jax.nn.gelu(preact).astype(jnp.bfloat16)
    partial_out = jnp.einsum(down_form, activated, down_full, preferred_element_type=jnp.float32)
    expert_flat = narrow_sums(partial_out).reshape(CAP * EXPERTS, feature_count)
    mixed = (resid + jnp.sum(gates[:, :, None] * expert_flat[slot_ids], axis=1)).astype(
        jnp.bfloat16
    )
    cotangent = grad_out.astype(jnp.float32)
    gate_pad = jnp.concatenate([gates.reshape(-1), jnp.zeros((1,), jnp.float32)], axis=0)
    cot_pad = jnp.concatenate([cotangent, jnp.zeros((1, feature_count), jnp.float32)], axis=0)
    grad_disp = (
        (gate_pad[sources][:, None] * cot_pad[owner_rows])
        .astype(jnp.bfloat16)
        .reshape(CAP, EXPERTS, feature_count)
    )
    grad_slots = narrow_rows(grad_disp)
    grad_activated = jnp.einsum(
        back_form, grad_slots, down_full, preferred_element_type=jnp.float32
    )
    gelu_back = jax.vjp(jax.nn.gelu, preact)[1]
    grad_preact = gelu_back(grad_activated)[0].astype(jnp.bfloat16)
    grad_down = jnp.einsum(
        grad_down_form, activated, grad_slots, preferred_element_type=jnp.float32
    )
    grad_in = jnp.einsum(
        "ced,cef->edf", gathered_slots, grad_preact, preferred_element_type=jnp.float32
    )
    grad_partial = jnp.einsum(
        "cef,edf->ced", grad_preact, in_full, preferred_element_type=jnp.float32
    )
    grad_slot_rows = narrow_sums(grad_partial).reshape(CAP * EXPERTS, feature_count)
    grad_normed_two = jnp.sum(grad_slot_rows[slot_ids], axis=1)
    norm_two_back = jax.vjp(normalize, resid, ln2_gain, ln2_bias)[1]
    grad_resid_norm, grad_gain_two, grad_bias_two = norm_two_back(grad_normed_two)
    grad_resid = cotangent + grad_resid_norm
    grad_branch = grad_resid.astype(jnp.bfloat16)
    grad_branch_rows = narrow_rows(grad_branch)
    grad_out_weight = jnp.dot(attended.T, grad_branch_rows, preferred_element_type=jnp.float32)
    grad_att = jnp.dot(grad_branch_rows, out_full.T, preferred_element_type=jnp.float32).astype(
        jnp.bfloat16
    )
    grad_proj = attention_backward(
        projected[0], projected[1], projected[2], grad_att, log_total, head_count
    )
    grad_qkv_weight = jnp.einsum(
        "rd,jrc->jdc", att_rows, grad_proj, preferred_element_type=jnp.float32
    )
    grad_normed_part = jnp.einsum(
        "jrc,jdc->rd", grad_proj, qkv_full, preferred_element_type=jnp.float32
    )
    grad_normed = narrow_sums(grad_normed_part)
    norm_one_back = jax.vjp(normalize, stream, ln1_gain, ln1_bias)[1]
    grad_stream_norm, grad_gain_one, grad_bias_one = norm_one_back(grad_normed)
    grad_input = grad_resid + grad_stream_norm
    grad_in_block, grad_down_block = (
        lax.psum_scatter(
            grad_in.astype(jnp.bfloat16), "wide", scatter_dimension=1, tiled=True
        ).astype(jnp.float32),
        lax.psum_scatter(
            grad_down.astype(jnp.bfloat16), "wide", scatter_dimension=2, tiled=True
        ).astype(jnp.float32),
    )
    grad_qkv_block, grad_out_block = (
        lax.psum_scatter(
            grad_qkv_weight.astype(jnp.bfloat16), "wide", scatter_dimension=1, tiled=True
        ).astype(jnp.float32),
        lax.psum_scatter(
            grad_out_weight.astype(jnp.bfloat16), "wide", scatter_dimension=1, tiled=True
        ).astype(jnp.float32),
    )
    block_grads = (
        lax.psum(grad_qkv_block.astype(jnp.bfloat16), "dp").astype(jnp.float32),
        lax.psum(grad_out_block.astype(jnp.bfloat16), "dp").astype(jnp.float32),
        lax.psum(grad_in_block.astype(jnp.bfloat16), "dp").astype(jnp.float32),
        lax.psum(grad_down_block.astype(jnp.bfloat16), "dp").astype(jnp.float32),
    )
    norm_totals = lax.psum(
        (grad_gain_one, grad_bias_one, grad_gain_two, grad_bias_two), ("dp", "wide", "narrow")
    )
    return (
        mixed,
        grad_input,
        norm_totals[0],
        norm_totals[1],
        norm_totals[2],
        norm_totals[3],
        block_grads[0],
        block_grads[1],
        block_grads[2],
        block_grads[3],
    )


def solution(mesh):
    placed = (
        P(("dp", "wide", "narrow"), None),
        P(("dp", "wide", "narrow"), None),
        P(("dp", "wide", "narrow"), None),
        P(("dp", "wide", "narrow"), None),
        P(),
        P(),
        P(),
        P(),
        P(None, "wide", "narrow"),
        P("narrow", "wide"),
        P(None, "wide", "narrow"),
        P(None, "narrow", "wide"),
    )
    return jax.shard_map(
        on_device,
        mesh=mesh,
        in_specs=placed,
        out_specs=(
            P(("dp", "wide", "narrow"), None),
            P(("dp", "wide", "narrow"), None),
            P(),
            P(),
            P(),
            P(),
            P(None, "wide", "narrow"),
            P("narrow", "wide"),
            P(None, "wide", "narrow"),
            P(None, "narrow", "wide"),
        ),
        check_vma=False,
    )
```

profile of v0, /device:TPU:0, one launch (start us, length us, event | category | flops | bytes accessed | tf_op | source)
XLA Modules:
  0.0 1943.7 jit_solution(15779378259460886551)
XLA Ops:
  14.3 9.1 reduce-window.6
  24.2 8.8 scatter_custom_fusion
  69.5 15.1 while.26
  92.2 32.9 %fusion = bf16[792,512]{1,0:T(8,128)(2,1)} fusion(bf16[3152,512]{1,0:T(8,128)(2,1)} %convolution_convert_fusion.4), kind=kCustom, calls=%all-reduce-scatter | all-reduce-scatter fusion | flops 1622017 | bytes 4039168
  134.1 7.4 gather_fusion
  150.5 11.4 gather_fusion.2
  166.7 78.4 %all-gather.11.cloned.1.call-done = bf16[32,512,512]{2,1,0:T(8,128)(2,1)} async-done(((bf16[32,256,512]{2,1,0:T(8,128)(2,1)}), bf16[32,512,512]{2,1,0:T(8,128)(2,1)}) %all-gather.11.cloned.1.call-update) | async-done | bytes 16777232 | tf_op jit(solution)/shard_map/all_gather | solution.py:172
  245.0 62.0 %all-gather.9.cloned.1.call-done = bf16[264,32,512]{2,1,0:T(8,128)(2,1)} async-done(((bf16[66,32,512]{2,1,0:T(8,128)(2,1)}), bf16[264,32,512]{2,1,0:T(8,128)(2,1)}) %all-gather.9.cloned.1.call-update) | async-done | bytes 8650768 | tf_op jit(solution)/shard_map/all_gather | solution.py:41
  307.0 23.2 %fusion.57 = f32[32,264,512]{2,1,0:T(8,128)} fusion(bf16[32,512,512]{2,1,0:T(8,128)(2,1)} %all-gather.11.cloned.1.call-done, bf16[264,32,512]{2,1,0:T(8,128)(2,1)} %all-gather.9.cloned.1.call-done), kind=kOutput, calls=%fused_computation.83 | convolution fusion | flops 4429185024 | bytes 42729472 | tf_op jit(solution)/shard_map/ced,edf->cef/dot_general | solution.py:178
  330.2 38.0 %all-gather.15.cloned.1.call-done = bf16[264,32,512]{2,1,0:T(8,128)(2,1)} async-done(((bf16[66,32,512]{2,1,0:T(8,128)(2,1)}), bf16[264,32,512]{2,1,0:T(8,128)(2,1)}) %all-gather.15.cloned.1.call-update) | async-done | bytes 8650768 | tf_op jit(solution)/shard_map/all_gather | solution.py:41
  368.2 200.2 %all-gather.13.cloned.1.call-done = bf16[32,512,512]{2,1,0:T(8,128)(2,1)} async-done(((bf16[32,512,256]{2,1,0:T(8,128)(2,1)}), bf16[32,512,512]{2,1,0:T(8,128)(2,1)}) %all-gather.13.cloned.1.call-update) | async-done | bytes 16777232 | tf_op jit(solution)/shard_map/all_gather | solution.py:173
  568.5 39.8 %fusion.49 = bf16[264,32,512]{2,0,1:T(8,128)(2,1)} fusion(f32[32,264,512]{2,1,0:T(8,128)} %fusion.57, bf16[32,512,512]{2,1,0:T(8,128)(2,1)} %all-gather.13.cloned.1.call-done, bf16[264,32,512]{2,1,0:T(8,128)(2,1)} %all-gather.15.cloned.1.call-done), kind=kOutput, calls=%fused_computation.68 | convolution fusion | flops 4515692544 | bytes 51380224 | tf_op jit(solution)/shard_map/ced,efd->cef/dot_general | solution.py:194
  608.3 13.3 convert_bitcast_fusion
  621.6 9.9 copy.94
  631.6 20.6 %convert_bitcast_fusion.1 = bf16[264,32,512]{2,0,1:T(8,128)(2,1)} fusion(bf16[32,512,512]{2,1,0:T(8,128)(2,1)} %all-gather.13.cloned.1.call-done, f32[32,264,512]{2,1,0:T(8,128)} %fusion.57), kind=kOutput, calls=%fused_computation.79 | convolution fusion | flops 4472438784 | bytes 42729472 | tf_op jit(solution)/shard_map/cef,efd->ced/dot_general | solution.py:180
  652.2 10.2 copy.90
  663.8 41.3 %reduce-scatter.13.cloned.1.call-done = bf16[66,32,512]{2,1,0:T(8,128)(2,1)} async-done(((bf16[264,32,512]{2,1,0:T(8,128)(2,1)}), bf16[66,32,512]{2,1,0:T(8,128)(2,1)}) %reduce-scatter.13.cloned.1.call-update) | async-done | bytes 2162704 | tf_op jit(solution)/shard_map/reduce_scatter | solution.py:45
  709.3 8.7 gather_fusion.4
  733.6 47.4 %reduce-scatter.11.cloned.1.call-done = bf16[66,32,512]{2,1,0:T(8,128)(2,1)} async-done(((bf16[264,32,512]{2,1,0:T(8,128)(2,1)}), bf16[66,32,512]{2,1,0:T(8,128)(2,1)}) %reduce-scatter.11.cloned.1.call-update) | async-done | bytes 2162704 | tf_op jit(solution)/shard_map/reduce_scatter | solution.py:45
  785.3 8.6 gather_fusion.1
  799.0 18.5 multiply_reduce_fusion.2
  821.8 29.2 %all-gather.19.cloned.1.call-done = bf16[4,788,512]{2,1,0:T(8,128)(2,1)} async-done(((bf16[1,788,512]{2,1,0:T(8,128)(2,1)}), bf16[4,788,512]{2,1,0:T(8,128)(2,1)}) %all-gather.19.cloned.1.call-update) | async-done | bytes 3227664 | tf_op jit(solution)/shard_map/all_gather | solution.py:41
  870.0 28.8 %while.27 = (s32[]{:T(128)}, bf16[4,4,197,2,64]{2,4,3,1,0:T(8,128)(2,1)}, bf16[4,4,197,2,64]{2,4,3,1,0:T(8,128)(2,1)}, bf16[4,4,197,2,64]{2,4,3,1,0:T(8,128)(2,1...) while((s32[]{:T(128)}, ...), condition=%wide.region_21.22_spmd, body=%wide.region_19.21_spmd.sunk | while | flops 201688608 | bytes 12767257 | solution.py:121
  923.9 28.4 %convolution_convert_fusion.3 = bf16[32,512,512]{2,1,0:T(8,128)(2,1)} fusion(bf16[264,32,512]{2,0,1:T(8,128)(2,1)} %fusion.49, bf16[264,32,512]{2,1,0:T(8,128)(2,1)} %all-gather.9.cloned.1.call-done), kind=kOutput, calls=%fused_computation.77 | convolution fusion | flops 4437573632 | bytes 34078720 | tf_op jit(solution)/shard_map/ced,cef->edf/dot_general | solution.py:202
  952.4 50.9 %convolution_convert_fusion.2 = bf16[32,512,512]{2,1,0:T(8,128)(2,1)} fusion(bf16[264,32,512]{2,1,0:T(8,128)(2,1)} %all-gather.15.cloned.1.call-done, f32[32,264,512]{2,1,0:T(8,128)} %fusion.57), kind=kOutput, calls=%fused_computation.76 | convolution fusion | flops 4476502016 | bytes 42729472 | tf_op jit(solution)/shard_map/cef,ced->efd/dot_general | solution.py:199
  1003.7 138.0 %reduce-scatter.19.cloned.1.call-done = bf16[32,256,512]{2,1,0:T(8,128)(2,1)} async-done(((bf16[32,512,512]{2,1,0:T(8,128)(2,1)}), bf16[32,256,512]{2,1,0:T(8,128)(2,1)}) %reduce-scatter.19.cloned.1.call-update) | async-done | bytes 8388624 | tf_op jit(solution)/shard_map/reduce_scatter | solution.py:233
  1141.7 191.9 %reduce-scatter.21.cloned.1.call-done = bf16[32,512,256]{2,1,0:T(8,128)(2,1)} async-done(((bf16[32,512,512]{2,1,0:T(8,128)(2,1)}), bf16[32,512,256]{2,1,0:T(8,128)(2,1)}) %reduce-scatter.21.cloned.1.call-update) | async-done | bytes 8388624 | tf_op jit(solution)/shard_map/reduce_scatter | solution.py:236
  1339.8 33.2 %fusion.1 = bf16[792,512]{1,0:T(8,128)(2,1)S(1)} fusion(bf16[3152,512]{1,0:T(8,128)(2,1)} %fusion.59), kind=kCustom, calls=%all-reduce-scatter.1 | all-reduce-scatter fusion | flops 1622017 | bytes 4039168
  1382.7 45.3 %all-reduce.7 = (f32[512]{0:T(512)}, f32[512]{0:T(512)}, f32[512]{0:T(512)}, f32[512]{0:T(512)}) all-reduce(f32[512]{0:T(512)S(1)} %get-tuple-element.174, f32[512]{0:T(512)S(1)} %get-tuple-element.176, f32[512]{0:T(512)S(1)} %get-tuple-element.172, ...), channel_id=1, replica_groups=mesh['dp'=4,'wide'=2,'narrow'=4] {'dp','wide','narrow'}, use_global_device_ids=true, to_apply=%region_26.27 | all-reduce | flops 2048 | bytes 16384 | tf_op jit(solution)/shard_map/psum | solution.py:254
  1431.0 480.8 %all-reduce.11.cloned.1.call-done = (bf16[3,256,128]{1,2,0:T(8,128)(2,1)}, bf16[128,256]{1,0:T(8,128)(2,1)}, bf16[32,256,512]{2,1,0:T(8,128)(2,1)}, bf16[32,512,256]{2,1,0:T(8,128)(2,1)}) async-done(((bf16[3,256,128]{1,2,0:T(8,128)(2,1)}, bf16[128,256]{1,0:T(8,128)(2,1)}, bf16[32,256,512]{2,1,0:T(8,128)(2,1)}, bf16[32,512,256]{2,1,0:T(8,128)(2,1)}), (bf16[3,256,128]{1,2,0:T(8,128)(2,1)}, ...) | async-done | bytes 17039376 | tf_op jit(solution)/shard_map/psum | solution.py:249
  1911.8 11.8 convert_element_type.159
  1923.6 11.7 convert_element_type.161
  (252 shorter events, 217.1 us)
Async XLA Ops:
  7.2 38.7 %all-gather.17.cloned.1.call-start = ((), (), s32[]{:S(2)}) async-start(), calls=%async_computation.16 | async-start | bytes 4055040 | tf_op jit(solution)/shard_map/all_gather | solution.py:41
  12.6 232.4 %all-gather.11.cloned.1.call-start = ((), (), s32[]{:S(2)}) async-start(), calls=%async_computation.7 | async-start | bytes 25165824 | tf_op jit(solution)/shard_map/all_gather | solution.py:172
  13.4 19.6 %copy-start.25 = (bf16[128,256]{1,0:T(8,128)(2,1)S(1)}, bf16[128,256]{1,0:T(8,128)(2,1)}, u32[]{:S(2)}) copy-start(bf16[128,256]{1,0:T(8,128)(2,1)} %param.25) | copy-start | bytes 196612
  13.4 293.6 %all-gather.9.cloned.1.call-start = ((), (), s32[]{:S(2)}) async-start(), calls=%async_computation.6 | async-start | bytes 10813440 | tf_op jit(solution)/shard_map/all_gather | solution.py:41
  13.5 25.5 %copy-start.19 = (bf16[3,256,128]{2,1,0:T(8,128)(2,1)S(1)}, bf16[3,256,128]{2,1,0:T(8,128)(2,1)}, u32[]{:S(2)}) copy-start(bf16[3,256,128]{2,1,0:T(8,128)(2,1)} %param.24) | copy-start | bytes 589828
  13.7 32.2 %copy-start.12 = (s32[788,2]{1,0:T(8,128)}, s32[788,2]{1,0:T(8,128)S(1)}, u32[]{:S(2)}) copy-start(s32[788,2]{1,0:T(8,128)S(1)} %copy.85) | copy-start | bytes 18916
  24.1 8.9 copy-start.23
  69.5 18.8 copy-start.16
  84.6 7.6 copy-start.4
  92.2 34.9 %copy-start.36 = (u32[32]{0:T(128)S(1)}, u32[32]{0:T(128)}, u32[]{:S(2)}) copy-start(u32[32]{0:T(128)} %constant.122) | copy-start | bytes 388
  92.2 40.2 %copy-start = (bf16[788,512]{1,0:T(8,128)(2,1)S(1)}, bf16[788,512]{1,0:T(8,128)(2,1)}, u32[]{:S(2)}) copy-start(bf16[788,512]{1,0:T(8,128)(2,1)} %param.16) | copy-start | bytes 2420740
  125.8 2.6 collective-permute-start
  141.6 226.6 %all-gather.15.cloned.1.call-start = ((), (), s32[]{:S(2)}) async-start(), calls=%async_computation.10 | async-start | bytes 10813440 | tf_op jit(solution)/shard_map/all_gather | solution.py:41
  166.0 402.4 %all-gather.13.cloned.1.call-start = ((), (), s32[]{:S(2)}) async-start(), calls=%async_computation.8 | async-start | bytes 25165824 | tf_op jit(solution)/shard_map/all_gather | solution.py:173
  166.6 538.4 %reduce-scatter.13.cloned.1.call-start = ((), (), s32[]{:S(2)}) async-start(), calls=%async_computation.11 | async-start | bytes 10813440 | tf_op jit(solution)/shard_map/reduce_scatter | solution.py:45
  631.6 149.5 %reduce-scatter.11.cloned.1.call-start = ((), (), s32[]{:S(2)}) async-start(), calls=%async_computation.9 | async-start | bytes 10813440 | tf_op jit(solution)/shard_map/reduce_scatter | solution.py:45
  662.4 188.5 %all-gather.19.cloned.1.call-start = ((), (), s32[]{:S(2)}) async-start(), calls=%async_computation.17 | async-start | bytes 4055040 | tf_op jit(solution)/shard_map/all_gather | solution.py:41
  799.0 18.5 copy-start.7
  821.7 182.0 %reduce-scatter.17.cloned.1.call-start = ((), (), s32[]{:S(2)}) async-start(), calls=%async_computation.13 | async-start | bytes 196608 | tf_op jit(solution)/shard_map/reduce_scatter | solution.py:244
  821.8 33.1 %copy-start.17 = (bf16[128,512]{1,0:T(8,128)(2,1)S(1)}, bf16[128,512]{1,0:T(8,128)(2,1)}, u32[]{:S(2)}) copy-start(bf16[128,512]{1,0:T(8,128)(2,1)} %all_gather.26) | copy-start | bytes 393220
  860.1 9.9 copy-start.3
  860.1 9.9 copy-start.5
  916.5 87.2 %reduce-scatter.15.cloned.1.call-start = ((), (), s32[]{:S(2)}) async-start(), calls=%async_computation.12 | async-start | bytes 589824 | tf_op jit(solution)/shard_map/reduce_scatter | solution.py:241
  923.9 217.8 %reduce-scatter.19.cloned.1.call-start = ((), (), s32[]{:S(2)}) async-start(), calls=%async_computation.14 | async-start | bytes 25165824 | tf_op jit(solution)/shard_map/reduce_scatter | solution.py:233
  952.4 381.2 %reduce-scatter.21.cloned.1.call-start = ((), (), s32[]{:S(2)}) async-start(), calls=%async_computation.15 | async-start | bytes 25165824 | tf_op jit(solution)/shard_map/reduce_scatter | solution.py:236
  1003.3 908.5 %all-reduce.11.cloned.1.call-start = ((), (), s32[]{:S(2)}) async-start(), calls=%async_computation.18 | async-start | bytes 34078720 | tf_op jit(solution)/shard_map/psum | solution.py:249
  1373.1 7.8 copy-start.22
  1373.1 7.8 copy-start.31
  1373.1 3.6 collective-permute-start.1
  1376.7 51.3 %copy-start.9 = (f32[788,512]{1,0:T(8,128)S(1)}, f32[788,512]{1,0:T(8,128)}, u32[]{:S(2)}) copy-start(f32[788,512]{1,0:T(8,128)} %copy-done.8) | copy-start | bytes 4841476
  1923.6 11.7 copy-start.20
  1923.6 12.6 copy-start.26
  (20 other events, 70.6 us)
Sparse Core Ops, SparseCore 0:
  12.7 31.8 all-gather.16
  46.2 198.8 all-gather.10
  247.2 59.7 all-gather.8
  308.4 59.7 all-gather.14
  369.6 198.8 all-gather.12
  631.7 73.3 reduce-scatter.12
  707.7 73.3 reduce-scatter.10
  821.8 29.0 all-gather.18
  916.6 10.2 reduce-scatter.16
  928.9 13.1 reduce-scatter.14
  952.5 189.1 reduce-scatter.18
  1144.4 189.1 reduce-scatter.20
  1336.8 574.9 all-reduce.10
where the time goes:
time: 1950 us; the launch traced here: 1940 us
  waiting for transfers between devices  1310 us (67%)
  matrix products  230 us (12%)
  local copies, waits for them, and re-layouts  165 us (8%)
  blocking collectives  124 us (6%)
  other arithmetic  96.1 us (5%)
    psum x1, waiting for transfers between devices, on_device(): lax.psum(grad_qkv_block.astype(jnp.bfloat16), 'dp').astype(jnp.float32)  481 us
    all_gather x1, waiting for transfers between devices, on_device(): lax.all_gather(w_expert_out, 'wide', axis=2, tiled=True)  200 us
    reduce_scatter x1, waiting for transfers between devices, on_device(): lax.psum_scatter(grad_down.astype(jnp.bfloat16), 'wide', scatter_dimensio...  192 us
    reduce_scatter x1, waiting for transfers between devices, on_device(): lax.psum_scatter(grad_in.astype(jnp.bfloat16), 'wide', scatter_dimension=...  138 us
    all_gather x4, waiting for transfers between devices, narrow_rows(): return lax.all_gather(values, 'narrow', axis=0, tiled=True)  129 us
    reduce_scatter x2, waiting for transfers between devices, narrow_sums(): lax.psum_scatter(values.astype(jnp.bfloat16), 'narrow', scatter_dimension...  88.7 us
    all_gather x1, waiting for transfers between devices, on_device(): lax.all_gather(w_expert_in, 'wide', axis=1, tiled=True)  78.4 us
    unnamed x2, blocking collectives  66.1 us
  transfers between devices with their start and end apart: 15, of which 10 were waited for; matrix products, arithmetic and copies ran while one was open for 18% of the time, Pallas kernels for 0%

commit v1 on v0

--- a/solution.py
+++ b/solution.py
@@ -1,7 +1,12 @@
+import functools
+import math
+
 import jax
 import jax.numpy as jnp
 from jax import lax
-from jax.sharding import PartitionSpec as P
+from jax.experimental import pallas as pl
+from jax.experimental.pallas import tpu as pltpu
+from jax.sharding import Mesh, PartitionSpec as P
 
 HEAD_DIM = 64
 EXPERTS = 32
@@ -10,8 +15,637 @@
 IMG_STEP = 4
 CAP = 66
 
-
 norm_eps = 1e-06
+
+f32 = jnp.float32
+bf16 = jnp.bfloat16
+
+
+SLOTS = -(-CAP // 8) * 8
+IMG_ROWS = -(-SEQ // 16) * 16
+LANES = 128
+VMEM_LIMIT = 56 * 1024 * 1024
+
+
+def dot(a, b):
+    return lax.dot_general(a, b, (((1,), (0,)), ((), ())), preferred_element_type=f32)
+
+
+def dot_bt(a, b):
+    return lax.dot_general(a, b, (((1,), (1,)), ((), ())), preferred_element_type=f32)
+
+
+def dot_at(a, b):
+    return lax.dot_general(a, b, (((0,), (0,)), ((), ())), preferred_element_type=f32)
+
+
+def norm_parts(values):
+    average = jnp.mean(values, axis=-1, keepdims=True)
+    centered = values - average
+    scale = lax.rsqrt(jnp.mean(centered * centered, axis=-1, keepdims=True) + norm_eps)
+    return centered * scale, scale
+
+
+def norm_back(hat, scale, gain, grad):
+    t = grad * gain
+    return scale * (
+        t
+        - jnp.mean(t, axis=-1, keepdims=True)
+        - hat * jnp.mean(t * hat, axis=-1, keepdims=True)
+    )
+
+
+def full_spec(shape):
+    zeros = (0,) * len(shape)
+    return pl.BlockSpec(shape, lambda *_: zeros)
+
+
+def image_spec(shape):
+    rest = (0,) * (len(shape) - 1)
+    return pl.BlockSpec((1,) + shape[1:], lambda i: (i,) + rest)
+
+
+def route_kernel(rep, tile, routes_ref, routes_t_ref, gates_ref, cot_ref, slot_ref, slot_t_ref, *gd_refs):
+    rows = routes_ref.shape[0]
+    before = lax.broadcasted_iota(jnp.int32, (rows, rows), 0)
+    after = lax.broadcasted_iota(jnp.int32, (rows, rows), 1)
+    ids_t = lax.broadcasted_iota(jnp.int32, (EXPERTS, rows), 0)
+    ids = lax.broadcasted_iota(jnp.int32, (rows, EXPERTS), 1)
+    hot_t = [(ids_t == routes_t_ref[k : k + 1, :]).astype(f32) for k in range(TOP)]
+    hot = [(ids == routes_ref[:, k : k + 1]).astype(f32) for k in range(TOP)]
+    count_t = dot(sum(hot_t).astype(bf16), (before < after).astype(f32).astype(bf16))
+    count = dot((after < before).astype(f32).astype(bf16), sum(hot).astype(bf16))
+    slot_t = []
+    for k in range(TOP):
+        rank_t = jnp.sum(hot_t[k] * count_t, axis=0, keepdims=True).astype(jnp.int32)
+        slot_t.append(routes_t_ref[k : k + 1, :] * SLOTS + rank_t)
+        slot_t_ref[k : k + 1, :] = slot_t[k]
+        rank = jnp.sum(hot[k] * count, axis=1, keepdims=True).astype(jnp.int32)
+        slot_ref[:, k : k + 1] = routes_ref[:, k : k + 1] * SLOTS + rank
+    cot = cot_ref[...].astype(f32)
+    weighed = [(gates_ref[:, k : k + 1] * cot).astype(bf16) for k in range(TOP)]
+    part = gd_refs[0].shape[0] // rep
+    for g, gd_ref in enumerate(gd_refs):
+        for start in range(0, part, tile):
+            place = lax.broadcasted_iota(jnp.int32, (tile, rows), 0) + (g * part + start)
+            total = sum(
+                dot((place == slot_t[k]).astype(f32).astype(bf16), weighed[k]) for k in range(TOP)
+            ).astype(bf16)
+            for copy in range(rep):
+                gd_ref[copy * part + start : copy * part + start + tile, :] = total
+
+
+def route_and_grad_slots(routes, gates, cot, rep, groups, owners):
+    rows, features = cot.shape
+    part = owners * SLOTS
+    tile = 384 if part % 384 == 0 else part
+    shapes = [
+        jax.ShapeDtypeStruct((rows, TOP), jnp.int32),
+        jax.ShapeDtypeStruct((TOP, rows), jnp.int32),
+    ] + [jax.ShapeDtypeStruct((rep * part, features), bf16)] * groups
+    return pl.pallas_call(
+        functools.partial(route_kernel, rep, tile),
+        out_shape=shapes,
+        compiler_params=pltpu.CompilerParams(vmem_limit_bytes=VMEM_LIMIT),
+        name="route_grad_slots",
+    )(routes, routes.T, gates, cot)
+
+
+def unpack_weights(wide, narrow, weights_ref, qkv_scratch, out_scratch):
+    deep, across = qkv_scratch.shape[1] // wide, LANES
+    for x in range(wide):
+        for n in range(narrow):
+            block = x * narrow + n
+            for j in range(3):
+                qkv_scratch[j, x * deep : (x + 1) * deep, n * across : (n + 1) * across] = weights_ref[
+                    block, j * deep : (j + 1) * deep, :
+                ]
+            for c in range(deep // LANES):
+                first = 3 * deep + c * across
+                out_scratch[
+                    n * across : (n + 1) * across,
+                    x * deep + c * LANES : x * deep + (c + 1) * LANES,
+                ] = weights_ref[block, first : first + across, :]
+
+
+def head_masks():
+    lane = lax.broadcasted_iota(jnp.int32, (1, LANES), 1)
+    per = LANES // HEAD_DIM
+    return [(lane // HEAD_DIM) == h for h in range(per)]
+
+
+def masked(value, mask):
+    return jnp.where(mask, value, jnp.zeros_like(value))
+
+
+def forward_kernel(
+    wide,
+    narrow,
+    rep,
+    tile,
+    tokens_ref,
+    norms_ref,
+    weights_ref,
+    slot_t_ref,
+    proj_ref,
+    att_ref,
+    resid_ref,
+    *rest,
+):
+    x_refs, (qkv_w, out_w, norm_scratch) = rest[:-3], rest[-3:]
+    step = pl.program_id(0)
+    features = tokens_ref.shape[2]
+
+    @pl.when(step == 0)
+    def _():
+        unpack_weights(wide, narrow, weights_ref, qkv_w, out_w)
+        norm_scratch[...] = jnp.zeros_like(norm_scratch)
+
+    stream = tokens_ref[0].astype(f32)
+    hat, _ = norm_parts(stream)
+    normed = (hat * norms_ref[0:1, :] + norms_ref[1:2, :]).astype(bf16)
+    proj = [dot(normed, qkv_w[j]).astype(bf16) for j in range(3)]
+    for j in range(3):
+        proj_ref[0, :, j * features : (j + 1) * features] = proj[j]
+    masks = head_masks()
+    scale = HEAD_DIM ** (-0.5)
+    pieces = []
+    for pair in range(features // LANES):
+        cols = slice(pair * LANES, (pair + 1) * LANES)
+        q, k, v = proj[0][:, cols], proj[1][:, cols], proj[2][:, cols]
+        total = None
+        for mask in masks:
+            scores = dot_bt(masked(q, mask), k) * scale
+            weights = jnp.exp(scores - jnp.max(scores, axis=-1, keepdims=True))
+            probs = weights / jnp.sum(weights, axis=-1, keepdims=True)
+            one = dot(probs.astype(bf16), masked(v, mask))
+            total = one if total is None else total + one
+        pieces.append(total.astype(bf16))
+    attended = jnp.concatenate(pieces, axis=1)
+    att_ref[0] = attended
+    resid = stream + dot(attended, out_w[...])
+    resid_ref[0] = resid
+    hat_two, _ = norm_parts(resid)
+    norm_scratch[step, : stream.shape[0], :] = (
+        hat_two * norms_ref[2:3, :] + norms_ref[3:4, :]
+    ).astype(bf16)
+
+    @pl.when(step == pl.num_programs(0) - 1)
+    def _():
+        count = slot_t_ref.shape[1]
+        rows = norm_scratch[...].reshape(count, features)
+        part = x_refs[0].shape[0] // rep
+        for g, x_ref in enumerate(x_refs):
+            for start in range(0, part, tile):
+                place = lax.broadcasted_iota(jnp.int32, (tile, count), 0) + (g * part + start)
+                here = (place == slot_t_ref[0:1, :]) | (place == slot_t_ref[1:2, :])
+                total = dot(here.astype(f32).astype(bf16), rows).astype(bf16)
+                for copy in range(rep):
+                    x_ref[copy * part + start : copy * part + start + tile, :] = total
+
+
+def attention_and_slots(tokens, norms, weights, slot_t, wide, narrow, rep, groups, owners):
+    images, rows, features = tokens.shape
+    part = owners * SLOTS
+    tile = 384 if part % 384 == 0 else part
+    slot_shape = (rep * part, features)
+    per_image = [(images, rows, 3 * features), (images, rows, features), (images, rows, features)]
+    return pl.pallas_call(
+        functools.partial(forward_kernel, wide, narrow, rep, tile),
+        grid=(images,),
+        in_specs=[
+            image_spec(tokens.shape),
+            full_spec(norms.shape),
+            full_spec(weights.shape),
+            full_spec(slot_t.shape),
+        ],
+        out_specs=[image_spec(s) for s in per_image] + [full_spec(slot_shape)] * groups,
+        out_shape=[
+            jax.ShapeDtypeStruct(per_image[0], bf16),
+            jax.ShapeDtypeStruct(per_image[1], bf16),
+            jax.ShapeDtypeStruct(per_image[2], f32),
+        ]
+        + [jax.ShapeDtypeStruct(slot_shape, bf16)] * groups,
+        scratch_shapes=[
+            pltpu.VMEM((3, features, features), bf16),
+            pltpu.VMEM((features, features), bf16),
+            pltpu.VMEM((images, IMG_ROWS, features), bf16),
+        ],
+        compiler_params=pltpu.CompilerParams(vmem_limit_bytes=VMEM_LIMIT),
+        name="attention_forward",
+    )(tokens, norms, weights, slot_t)
+
+
+GELU_A = math.sqrt(2.0 / math.pi)
+GELU_B = 0.044715 * GELU_A
+
+
+def gelu_pair(u):
+    u2 = u * u
+    p = GELU_B * u2 + GELU_A
+    half = 0.5 * jnp.tanh(u * p) + 0.5
+    slope = half + (u * (6.0 * p - 4.0 * GELU_A)) * (half - half * half)
+    return u * half, slope
+
+
+def identity(size):
+    a = lax.broadcasted_iota(jnp.int32, (size, size), 0)
+    b = lax.broadcasted_iota(jnp.int32, (size, size), 1)
+    return (a == b).astype(f32).astype(bf16)
+
+
+def expert_kernel(
+    tile,
+    own_rows,
+    rep_ref,
+    x_ref,
+    gd_ref,
+    wi_ref,
+    wo_ref,
+    gin_ref,
+    gout_ref,
+    y_ref,
+    gx_ref,
+    x_t,
+    gd_t,
+    act,
+    gp,
+    wo_s,
+    y_acc,
+    gx_acc,
+):
+    step = pl.program_id(0)
+    rows, features = x_ref.shape
+    wide, deep, hidden = wi_ref.shape[0], wi_ref.shape[2], wi_ref.shape[3]
+
+    @pl.when(step == 0)
+    def _():
+        eye = identity(features)
+
+        def turn(t, carry):
+            at = pl.ds(pl.multiple_of(t * tile, tile), tile)
+            x_t[:, at] = dot_bt(eye, x_ref[at, :]).astype(bf16)
+            gd_t[:, at] = dot_bt(eye, gd_ref[at, :]).astype(bf16)
+            return carry
+
+        lax.fori_loop(0, rows // tile, turn, 0)
+        y_acc[...] = jnp.zeros_like(y_acc)
+        gx_acc[...] = jnp.zeros_like(gx_acc)
+
+    for x in range(wide):
+        wo_s[:, x * deep : (x + 1) * deep] = wo_ref[x, 0]
+    wi = wi_ref[:, 0].reshape(wide * deep, hidden)
+
+    def hidden_rows(t, carry):
+        at = pl.ds(pl.multiple_of(t * tile, tile), tile)
+        value, slope = gelu_pair(dot(x_ref[at, :], wi))
+        act[at, :] = value.astype(bf16)
+        gp[at, :] = (dot_bt(gd_ref[at, :], wo_s[...]) * slope).astype(bf16)
+        return carry
+
+    lax.fori_loop(0, rows // tile, hidden_rows, 0)
+
+    gin = dot(x_t[...], gp[...]).astype(bf16)
+    for x in range(wide):
+        gin_ref[x, 0] = gin[x * deep : (x + 1) * deep, :]
+    gout = dot_bt(identity(hidden), dot(gd_t[...], act[...]).astype(bf16)).astype(bf16)
+    for x in range(wide):
+        gout_ref[x, 0] = gout[:, x * deep : (x + 1) * deep]
+
+    first = rep_ref[0] * own_rows
+
+    def own(t, carry):
+        at = pl.ds(pl.multiple_of(t * tile, tile), tile)
+        here = pl.ds(pl.multiple_of(first + t * tile, tile), tile)
+        y_acc[at, :] += dot(act[here, :], wo_s[...])
+        gx_acc[at, :] += dot_bt(gp[here, :], wi)
+        return carry
+
+    lax.fori_loop(0, own_rows // tile, own, 0)
+
+    @pl.when(step == pl.num_programs(0) - 1)
+    def _():
+        y_ref[...] = y_acc[...].astype(bf16)
+        gx_ref[...] = gx_acc[...].astype(bf16)
+
+
+def expert(rep_index, x, gd, w_in, w_out, own_rows, wide, narrow):
+    rows, features = x.shape
+    deep, hidden = w_in.shape[1], w_in.shape[2]
+    w_in = w_in.reshape(wide, narrow, deep, hidden)
+    w_out = w_out.reshape(wide, narrow, hidden, deep)
+    tile = 384 if own_rows % 384 == 0 else math.gcd(own_rows, 128)
+    in_spec = pl.BlockSpec((wide, 1, deep, hidden), lambda n, r: (0, n, 0, 0))
+    out_spec = pl.BlockSpec((wide, 1, hidden, deep), lambda n, r: (0, n, 0, 0))
+    whole = lambda shape: pl.BlockSpec(shape, lambda n, r: (0, 0))
+    gin, gout, y, gx = pl.pallas_call(
+        functools.partial(expert_kernel, tile, own_rows),
+        grid_spec=pltpu.PrefetchScalarGridSpec(
+            num_scalar_prefetch=1,
+            grid=(narrow,),
+            in_specs=[whole(x.shape), whole(gd.shape), in_spec, out_spec],
+            out_specs=[in_spec, out_spec, whole((own_rows, features)), whole((own_rows, features))],
+            scratch_shapes=[
+                pltpu.VMEM((features, rows), bf16),
+                pltpu.VMEM((features, rows), bf16),
+                pltpu.VMEM((rows, hidden), bf16),
+                pltpu.VMEM((rows, hidden), bf16),
+                pltpu.VMEM((hidden, features), bf16),
+                pltpu.VMEM((own_rows, features), f32),
+                pltpu.VMEM((own_rows, features), f32),
+            ],
+        ),
+        out_shape=[
+            jax.ShapeDtypeStruct(w_in.shape, bf16),
+            jax.ShapeDtypeStruct(w_out.shape, bf16),
+            jax.ShapeDtypeStruct((own_rows, features), bf16),
+            jax.ShapeDtypeStruct((own_rows, features), bf16),
+        ],
+        compiler_params=pltpu.CompilerParams(vmem_limit_bytes=VMEM_LIMIT),
+        cost_estimate=pl.CostEstimate(
+            flops=2 * narrow * features * hidden * (4 * rows + 2 * own_rows),
+            bytes_accessed=20_000_000,
+            transcendentals=rows * hidden * narrow,
+        ),
+        name="expert",
+    )(rep_index, x, gd, w_in, w_out)
+    return gin.reshape(-1, deep, hidden), gout.reshape(-1, hidden, deep), y, gx
+
+
+def mixed_kernel(resid_ref, slot_ref, gates_ref, *rest):
+    y_refs, mixed_ref = rest[:-1], rest[-1]
+    total = resid_ref[0]
+    rows = total.shape[0]
+    part = y_refs[0].shape[0]
+    for k in range(TOP):
+        picked = None
+        for g, y_ref in enumerate(y_refs):
+            place = lax.broadcasted_iota(jnp.int32, (rows, part), 1) + g * part
+            one = dot((place == slot_ref[0, :, k : k + 1]).astype(f32).astype(bf16), y_ref[...])
+            picked = one if picked is None else picked + one
+        total = total + gates_ref[0, :, k : k + 1] * picked
+    mixed_ref[0] = total.astype(bf16)
+
+
+def mix(resid, slots, gates, ys):
+    return pl.pallas_call(
+        mixed_kernel,
+        grid=(resid.shape[0],),
+        in_specs=[image_spec(resid.shape), image_spec(slots.shape), image_spec(gates.shape)]
+        + [full_spec(y.shape) for y in ys],
+        out_specs=image_spec(resid.shape),
+        out_shape=jax.ShapeDtypeStruct(resid.shape, bf16),
+        compiler_params=pltpu.CompilerParams(vmem_limit_bytes=VMEM_LIMIT),
+        name="mix",
+    )(resid, slots, gates, *ys)
+
+
+def backward_kernel(wide, narrow, groups, *refs):
+    (tokens_ref, cot_ref, norms_ref, weights_ref, slot_ref, proj_ref, att_ref, resid_ref) = refs[:8]
+    gx_refs = refs[8 : 8 + groups]
+    (grad_ref, grads_w_ref, grads_n_ref) = refs[8 + groups : 11 + groups]
+    (qkv_w, out_w, normed_s, att_s, branch_s, proj_s) = refs[11 + groups :]
+    step = pl.program_id(0)
+    rows, features = tokens_ref.shape[1], tokens_ref.shape[2]
+
+    @pl.when(step == 0)
+    def _():
+        unpack_weights(wide, narrow, weights_ref, qkv_w, out_w)
+        normed_s[...] = jnp.zeros_like(normed_s)
+        att_s[...] = jnp.zeros_like(att_s)
+        branch_s[...] = jnp.zeros_like(branch_s)
+        proj_s[...] = jnp.zeros_like(proj_s)
+        grads_n_ref[...] = jnp.zeros_like(grads_n_ref)
+
+    part = gx_refs[0].shape[0]
+    grad_normed = None
+    for g, gx_ref in enumerate(gx_refs):
+        place = lax.broadcasted_iota(jnp.int32, (rows, part), 1) + g * part
+        here = (place == slot_ref[0, :, 0:1]) | (place == slot_ref[0, :, 1:2])
+        one = dot(here.astype(f32).astype(bf16), gx_ref[...])
+        grad_normed = one if grad_normed is None else grad_normed + one
+    hat_two, scale_two = norm_parts(resid_ref[0])
+    grads_n_ref[2:3, :] += jnp.sum(grad_normed * hat_two, axis=0, keepdims=True)
+    grads_n_ref[3:4, :] += jnp.sum(grad_normed, axis=0, keepdims=True)
+    grad_resid = cot_ref[0].astype(f32) + norm_back(
+        hat_two, scale_two, norms_ref[2:3, :], grad_normed
+    )
+    branch = grad_resid.astype(bf16)
+    branch_s[step, :rows, :] = branch
+    att_s[step, :rows, :] = att_ref[0]
+    grad_att = dot_bt(branch, out_w[...]).astype(bf16)
+
+    masks = head_masks()
+    scale = HEAD_DIM ** (-0.5)
+    pairs = features // LANES
+    pieces = [[None] * pairs for _ in range(3)]
+    for pair in range(pairs):
+        at = [j * features + pair * LANES for j in range(3)]
+        q, k, v = [proj_ref[0, :, a : a + LANES] for a in at]
+        ga = grad_att[:, pair * LANES : (pair + 1) * LANES]
+        sums = [None] * 3
+        for mask in masks:
+            scores = dot_bt(masked(k, mask), q) * scale
+            weights = jnp.exp(scores - jnp.max(scores, axis=0, keepdims=True))
+            probs = weights / jnp.sum(weights, axis=0, keepdims=True)
+            ga_h = masked(ga, mask)
+            dprobs = dot_bt(v, ga_h)
+            inner = jnp.sum(probs * dprobs, axis=0, keepdims=True)
+            grad_scores = (probs * (dprobs - inner)).astype(bf16)
+            parts = (
+                dot_at(grad_scores, masked(k, mask)),
+                dot(grad_scores, masked(q, mask)),
+                dot(probs.astype(bf16), ga_h),
+            )
+            for j in range(3):
+                sums[j] = parts[j] if sums[j] is None else sums[j] + parts[j]
+        pieces[0][pair] = (sums[0] * scale).astype(bf16)
+        pieces[1][pair] = (sums[1] * scale).astype(bf16)
+        pieces[2][pair] = sums[2].astype(bf16)
+
+    stream = tokens_ref[0].astype(f32)
+    hat, scale_one = norm_parts(stream)
+    normed_s[step, :rows, :] = (hat * norms_ref[0:1, :] + norms_ref[1:2, :]).astype(bf16)
+    grad_first = None
+    for j in range(3):
+        grad_proj = jnp.concatenate(pieces[j], axis=1)
+        proj_s[j, step, :rows, :] = grad_proj
+        one = dot_bt(grad_proj, qkv_w[j])
+        grad_first = one if grad_first is None else grad_first + one
+    grads_n_ref[0:1, :] += jnp.sum(grad_first * hat, axis=0, keepdims=True)
+    grads_n_ref[1:2, :] += jnp.sum(grad_first, axis=0, keepdims=True)
+    grad_ref[0] = grad_resid + norm_back(hat, scale_one, norms_ref[0:1, :], grad_first)
+
+    @pl.when(step == pl.num_programs(0) - 1)
+    def _():
+        count = normed_s.shape[0] * normed_s.shape[1]
+        deep = features // wide
+        flat = lambda value: value.reshape(count, features)
+        normed_t = flat(normed_s[...])
+        for j in range(3):
+            grad = dot_at(normed_t, flat(proj_s[j])).astype(bf16)
+            for x in range(wide):
+                for n in range(narrow):
+                    grads_w_ref[x * narrow + n, j * deep : (j + 1) * deep, :] = grad[
+                        x * deep : (x + 1) * deep, n * LANES : (n + 1) * LANES
+                    ]
+        grad = dot_at(flat(att_s[...]), flat(branch_s[...])).astype(bf16)
+        for x in range(wide):
+            for n in range(narrow):
+                for c in range(deep // LANES):
+                    first = 3 * deep + c * LANES
+                    grads_w_ref[x * narrow + n, first : first + LANES, :] = grad[
+                        n * LANES : (n + 1) * LANES,
+                        x * deep + c * LANES : x * deep + (c + 1) * LANES,
+                    ]
+
+
+def attention_back(tokens, cot, norms, weights, slots, proj, att, resid, gxs, wide, narrow):
+    images, rows, features = tokens.shape
+    stash = (images, IMG_ROWS, features)
+    return pl.pallas_call(
+        functools.partial(backward_kernel, wide, narrow, len(gxs)),
+        grid=(images,),
+        in_specs=[
+            image_spec(tokens.shape),
+            image_spec(cot.shape),
+            full_spec(norms.shape),
+            full_spec(weights.shape),
+            image_spec(slots.shape),
+            image_spec(proj.shape),
+            image_spec(att.shape),
+            image_spec(resid.shape),
+        ]
+        + [full_spec(gx.shape) for gx in gxs],
+        out_specs=[image_spec(tokens.shape), full_spec(weights.shape), full_spec((4, features))],
+        out_shape=[
+            jax.ShapeDtypeStruct(tokens.shape, f32),
+            jax.ShapeDtypeStruct(weights.shape, bf16),
+            jax.ShapeDtypeStruct((4, features), f32),
+        ],
+        scratch_shapes=[
+            pltpu.VMEM((3, features, features), bf16),
+            pltpu.VMEM((features, features), bf16),
+            pltpu.VMEM(stash, bf16),
+            pltpu.VMEM(stash, bf16),
+            pltpu.VMEM(stash, bf16),
+            pltpu.VMEM((3,) + stash, bf16),
+        ],
+        compiler_params=pltpu.CompilerParams(vmem_limit_bytes=VMEM_LIMIT),
+        name="attention_backward",
+    )(tokens, cot, norms, weights, slots, proj, att, resid, *gxs)
+
+
+def owned_on_device(
+    sizes,
+    tokens,
+    grad_out,
+    gates,
+    routes,
+    ln1_gain,
+    ln1_bias,
+    ln2_gain,
+    ln2_bias,
+    w_qkv,
+    w_attn_out,
+    w_expert_in,
+    w_expert_out,
+):
+    rep, own_planes, wide, narrow = sizes
+    plane = wide * narrow
+    owners = own_planes * plane
+    groups = EXPERTS // owners
+    everyone = ("rep", "own", "wide", "narrow")
+    rows, features = tokens.shape
+    images = rows // SEQ
+    deep = w_qkv.shape[1]
+    rep_index = lax.axis_index("rep").astype(jnp.int32).reshape(1)
+    own_index = lax.axis_index("own")
+
+    def in_plane(values):
+        return lax.all_to_all(values, ("wide", "narrow"), 0, 0, tiled=True)
+
+    small = jnp.concatenate(
+        [w_qkv.reshape(3 * deep, LANES)]
+        + [w_attn_out[:, c * LANES : (c + 1) * LANES] for c in range(deep // LANES)],
+        axis=0,
+    )
+    weights = in_plane(jnp.broadcast_to(small[None], (plane,) + small.shape))
+
+    slots, slot_t, *gds = route_and_grad_slots(routes, gates, grad_out, rep, groups, owners)
+
+    def to_owners(values):
+        return lax.all_to_all(
+            values.reshape(-1, SLOTS, features), everyone, 0, 0, tiled=True
+        ).reshape(-1, features)
+
+    def to_tokens(values):
+        return lax.all_to_all(
+            values.reshape(-1, SLOTS, features), ("own", "wide", "narrow"), 0, 0, tiled=True
+        ).reshape(-1, features)
+
+    def owned(values, g):
+        return in_plane(
+            lax.dynamic_slice_in_dim(values, g * owners + own_index * plane, plane, axis=0)
+        )
+
+    w_in = [owned(w_expert_in, g) for g in range(groups)]
+    w_out = [owned(w_expert_out, g) for g in range(groups)]
+
+    norms = jnp.stack([ln1_gain, ln1_bias, ln2_gain, ln2_bias])
+    per_image = lambda values: values.reshape((images, SEQ) + values.shape[1:])
+    slot_wide = jnp.pad(
+        slot_t.reshape(TOP, images, SEQ), ((0, 0), (0, 0), (0, IMG_ROWS - SEQ)), constant_values=-1
+    ).reshape(TOP, images * IMG_ROWS)
+    tokens3, cot3, slots3, gates3 = map(per_image, (tokens, grad_out, slots, gates))
+    proj, att, resid, *xs = attention_and_slots(
+        tokens3, norms, weights, slot_wide, wide, narrow, rep, groups, owners
+    )
+
+    gd_all = [to_owners(v) for v in gds]
+    x_all = [to_owners(v) for v in xs]
+    grads_in, grads_out, ys, gxs = zip(
+        *[
+            expert(rep_index, x_all[g], gd_all[g], w_in[g], w_out[g], owners * SLOTS, wide, narrow)
+            for g in range(groups)
+        ]
+    )
+    gx_back = [to_tokens(v) for v in gxs]
+    y_back = [to_tokens(v) for v in ys]
+
+    def to_blocks(parts):
+        pieces = [lax.all_gather(in_plane(v), "own", axis=0, tiled=True) for v in parts]
+        return jnp.concatenate(pieces, axis=0).astype(f32)
+
+    out_in, out_out = to_blocks(grads_in), to_blocks(grads_out)
+
+    mixed = mix(resid, slots3, gates3, y_back).reshape(rows, features)
+    grad_input, grads_w, grads_n = attention_back(
+        tokens3, cot3, norms, weights, slots3, proj, att, resid, gx_back, wide, narrow
+    )
+    grads_n = lax.psum(grads_n, everyone)
+    block = jnp.sum(in_plane(grads_w).astype(f32), axis=0).astype(bf16)
+    block = lax.psum(block, ("rep", "own")).astype(f32)
+    grad_qkv = block[: 3 * deep].reshape(3, deep, LANES)
+    grad_attn_out = jnp.concatenate(
+        [
+            block[3 * deep + c * LANES : 3 * deep + (c + 1) * LANES]
+            for c in range(deep // LANES)
+        ],
+        axis=1,
+    )
+    return (
+        mixed,
+        grad_input.reshape(rows, features),
+        grads_n[0],
+        grads_n[1],
+        grads_n[2],
+        grads_n[3],
+        grad_qkv,
+        grad_attn_out,
+        out_in,
+        out_out,
+    )
 
 
 def normalize(values, norm_gain, norm_shift):
@@ -269,11 +903,22 @@
 
 
 def solution(mesh):
-    placed = (
-        P(("dp", "wide", "narrow"), None),
-        P(("dp", "wide", "narrow"), None),
-        P(("dp", "wide", "narrow"), None),
-        P(("dp", "wide", "narrow"), None),
+    dp, wide, narrow = (mesh.shape[name] for name in ("dp", "wide", "narrow"))
+    for rep in (2, 1):
+        if dp % rep == 0 and EXPERTS % ((dp // rep) * wide * narrow) == 0:
+            sizes = (rep, dp // rep, wide, narrow)
+            split = Mesh(mesh.devices.reshape(sizes), ("rep", "own", "wide", "narrow"))
+            return placed(functools.partial(owned_on_device, sizes), split, ("rep", "own"))
+    return placed(on_device, mesh, ("dp",))
+
+
+def placed(function, mesh, dp_axes):
+    rows = P(dp_axes + ("wide", "narrow"), None)
+    specs_in = (
+        rows,
+        rows,
+        rows,
+        rows,
         P(),
         P(),
         P(),
@@ -283,21 +928,18 @@
         P(None, "wide", "narrow"),
         P(None, "narrow", "wide"),
     )
+    specs_out = (
+        rows,
+        rows,
+        P(),
+        P(),
+        P(),
+        P(),
+        P(None, "wide", "narrow"),
+        P("narrow", "wide"),
+        P(None, "wide", "narrow"),
+        P(None, "narrow", "wide"),
+    )
     return jax.shard_map(
-        on_device,
-        mesh=mesh,
-        in_specs=placed,
-        out_specs=(
-            P(("dp", "wide", "narrow"), None),
-            P(("dp", "wide", "narrow"), None),
-            P(),
-            P(),
-            P(),
-            P(),
-            P(None, "wide", "narrow"),
-            P("narrow", "wide"),
-            P(None, "wide", "narrow"),
-            P(None, "narrow", "wide"),
-        ),
-        check_vma=False,
-    )
+        function, mesh=mesh, in_specs=specs_in, out_specs=specs_out, check_vma=False
+    )

time: 1950 us -> 823 us (0.42)
  waiting for transfers between devices: 1310 us -> 223 us
  matrix products: 230 us -> 0 us
  blocking collectives: 124 us -> 336 us
  Pallas kernels: 0 us -> 150 us
  local copies, waits for them, and re-layouts: 165 us -> 32 us
  other arithmetic: 96.1 us -> 24.7 us
  starting transfers between devices: 3.7 us -> 40.2 us
    psum x1, waiting for transfers between devices: 481 us -> 0.01 us  [owned_on_device(): block = lax.psum(block, ('rep', 'own')).astype(f32)]
    reduce_scatter x6 -> x0, waiting for transfers between devices: 419 us -> none  [the longest x1 192 us: on_device(): lax.psum_scatter(grad_down.astype(jnp.bfloat16), 'wide', scatter_dimensio...]
    all_gather x6 -> x4, waiting for transfers between devices: 408 us -> 32.2 us  [to_blocks(): lax.all_gather(in_plane(v), 'own', axis=0, tiled=True)]
    all_to_all x0 -> x8, blocking collectives: none -> 297 us  [the longest x6 176 us: in_plane(): return lax.all_to_all(values, ('wide', 'narrow'), 0, 0, tiled=True)]
    dot_general x40 -> x0, matrix products: 230 us -> none  [the longest x1 50.9 us: on_device(): jnp.einsum(grad_down_form, activated, grad_slots, preferred_element_type=...]
    all_to_all x0 -> x10, waiting for transfers between devices: none -> 190 us  [the longest x4 82.4 us: in_plane(): return lax.all_to_all(values, ('wide', 'narrow'), 0, 0, tiled=True)]
    pallas_call x0 -> x6, Pallas kernels: none -> 150 us  [the longest x2 93.2 us: expert(): pl.pallas_call(functools.partial(expert_kernel, tile, own_rows), grid_spe...]
    unnamed x2 -> x0, blocking collectives: 66.1 us -> none
  transfers between devices with their start and end apart: 15 -> 15, of which waited for: 10 -> 10; matrix products, arithmetic and copies ran while one was open for 18% -> 5% of each run, Pallas kernels for 0% -> 15%
where the time goes in v1:
time: 823 us; the launch traced here: 822 us
  blocking collectives  336 us (41%)
  waiting for transfers between devices  223 us (27%)
  Pallas kernels  150 us (18%)
  starting transfers between devices  40.2 us (5%)
  local copies, waits for them, and re-layouts  32 us (4%)
  other arithmetic  24.7 us (3%)
  between operations  15.9 us (2%)
    all_to_all x6, blocking collectives, in_plane(): return lax.all_to_all(values, ('wide', 'narrow'), 0, 0, tiled=True)  176 us
    all_to_all x2, blocking collectives, to_owners(): lax.all_to_all(values.reshape(-1, SLOTS, features), everyone, 0, 0, tiled...  121 us
    pallas_call x2, Pallas kernels, expert(): pl.pallas_call(functools.partial(expert_kernel, tile, own_rows), grid_spe...  93.2 us
    all_to_all x4, waiting for transfers between devices, in_plane(): return lax.all_to_all(values, ('wide', 'narrow'), 0, 0, tiled=True)  82.4 us
    all_to_all x4, waiting for transfers between devices, to_tokens(): lax.all_to_all(values.reshape(-1, SLOTS, features), ('own', 'wide', 'narr...  63.5 us
    all_to_all x2, waiting for transfers between devices, to_owners(): lax.all_to_all(values.reshape(-1, SLOTS, features), everyone, 0, 0, tiled...  43.7 us
    psum x1, blocking collectives, owned_on_device(): grads_n = lax.psum(grads_n, everyone)  39.2 us
    all_gather x4, waiting for transfers between devices, to_blocks(): lax.all_gather(in_plane(v), 'own', axis=0, tiled=True)  32.2 us
  transfers between devices with their start and end apart: 15, of which 10 were waited for; matrix products, arithmetic and copies ran while one was open for 5% of the time, Pallas kernels for 15%

profile of v1, /device:TPU:0, one launch (start us, length us, event | category | flops | bytes accessed | tf_op | source)
XLA Modules:
  0.0 821.6 jit_solution(3303888667101795606)
XLA Ops:
  11.3 5.2 all-to-all-start
  16.5 4.6 constant_dynamic-slice_fusion.1
  21.1 21.1 %all-to-all-done.weights_ref.refs_3_ = bf16[8,1024,128]{2,1,0:T(8,128)(2,1)S(1)} async-done(((bf16[8,1024,128]{2,1,0:T(8,128)(2,1)}), bf16[8,1024,128]{2,1,0:T(8,128)(2,1)S(1)}, u32[]{:S(2)}, u32[]{:S(2)}) %all-to-all-start) | async-done | bytes 2097184 | tf_op jit(solution)/shard_map/all_to_all | solution.py:566
  42.2 30.3 %all_to_all.90 = bf16[8,256,512]{2,1,0:T(8,128)(2,1)} all-to-all(bf16[8,256,512]{2,1,0:T(8,128)(2,1)} %get-tuple-element.52), channel_id=1, replica_groups=mesh['rep'=2,'own'=2,'wide'=2,'narrow'=4] {'wide','narrow'}, dimensions={0} | all-to-all | bytes 4194304 | tf_op jit(solution)/shard_map/all_to_all | solution.py:566
  72.5 4.4 all-to-all-start.3
  80.8 21.8 %all-to-all-done.3 = bf16[8,256,512]{2,1,0:T(8,128)(2,1)} async-done(((bf16[8,256,512]{2,1,0:T(8,128)(2,1)}), bf16[8,256,512]{2,1,0:T(8,128)(2,1)}, u32[]{:S(2)}, u32[]{:S(2)}) %all-to-all-start.3) | async-done | bytes 2097184 | tf_op jit(solution)/shard_map/all_to_all | solution.py:566
  102.6 29.1 %all_to_all.91 = bf16[8,512,256]{2,1,0:T(8,128)(2,1)} all-to-all(bf16[8,512,256]{2,1,0:T(8,128)(2,1)S(1)} %get-tuple-element.50), channel_id=1, replica_groups=mesh['rep'=2,'own'=2,'wide'=2,'narrow'=4] {'wide','narrow'}, dimensions={0} | all-to-all | bytes 4194304 | tf_op jit(solution)/shard_map/all_to_all | solution.py:566
  137.4 8.7 %route_grad_slots.1 = (s32[788,2]{1,0:T(8,128)}, s32[2,788]{1,0:T(2,128)}, bf16[2304,512]{1,0:T(8,128)(2,1)}, bf16[2304,512]{1,0:T(8,128)(2,1)}) custom-call(s32[788,2]{1,0:T(8,128)} %copy.31.routes_ref, s32[2,788]{1,0:T(2,128)} %bitcast.61, f32[788,2]{1,0:T(8,128)} %copy.32.gates_ref, bf16[788,512]{1,0:T(8,128)(2,1)} %cot_ref.1), custom_call_target="tpu_custom_call" | custom-call | tf_op jit(solution)/shard_map/route_grad_slots/pallas_call | solution.py:106
  146.0 15.0 %all-to-all-done.4 = bf16[8,512,256]{2,1,0:T(8,128)(2,1)S(1)} async-done(((bf16[8,512,256]{2,1,0:T(8,128)(2,1)}), bf16[8,512,256]{2,1,0:T(8,128)(2,1)S(1)}, u32[]{:S(2)}, u32[]{:S(2)}) %all-to-all-start.4) | async-done | bytes 2097184 | tf_op jit(solution)/shard_map/all_to_all | solution.py:566
  161.1 60.7 %all_to_all.92 = bf16[32,72,512]{2,1,0:T(8,128)(2,1)} all-to-all(bf16[32,72,512]{2,1,0:T(8,128)(2,1)} %bitcast.48), channel_id=1, replica_groups=mesh['rep'=2,'own'=2,'wide'=2,'narrow'=4] {'rep','own','wide','narrow'}, dimensions={0} | all-to-all | bytes 4718592 | tf_op jit(solution)/shard_map/all_to_all | solution.py:578
  227.5 15.9 %attention_forward.1 = (bf16[4,197,1536]{2,1,0:T(8,128)(2,1)}, bf16[4,197,512]{2,1,0:T(8,128)(2,1)}, f32[4,197,512]{2,1,0:T(8,128)}, bf16[2304,512]{1,0:T(8,128)(2,1)}, bf16[2304,512]{1,0:T(8,128)(2,1)}) custom-call(bf16[4,197,512]{2,1,0:T(8,128)(2,1)} %reshape.126.tokens_ref.refs_0_, f32[4,512]{1,0:T(4,128)} %pad_maximum_fusion.2.norms_ref.refs_2_, ...), custom_call_target="tpu_custom_call" | custom-call | tf_op jit(solution)/shard_map/attention_forward/pallas_call | solution.py:213
  243.4 35.8 %all-to-all-done.7 = bf16[32,72,512]{2,1,0:T(8,128)(2,1)S(1)} async-done(((bf16[32,72,512]{2,1,0:T(8,128)(2,1)}), bf16[32,72,512]{2,1,0:T(8,128)(2,1)S(1)}, u32[]{:S(2)}, u32[]{:S(2)}) %all-to-all-start.7) | async-done | bytes 2359328 | tf_op jit(solution)/shard_map/all_to_all | solution.py:578
  279.2 60.0 %all_to_all.93 = bf16[32,72,512]{2,1,0:T(8,128)(2,1)} all-to-all(bf16[32,72,512]{2,1,0:T(8,128)(2,1)} %bitcast.49), channel_id=1, replica_groups=mesh['rep'=2,'own'=2,'wide'=2,'narrow'=4] {'rep','own','wide','narrow'}, dimensions={0} | all-to-all | bytes 4718592 | tf_op jit(solution)/shard_map/all_to_all | solution.py:578
  342.0 46.6 %expert.3 = (bf16[2,4,256,512]{3,2,1,0:T(8,128)(2,1)}, bf16[2,4,512,256]{3,2,1,0:T(8,128)(2,1)}, bf16[1152,512]{1,0:T(8,128)(2,1)}, bf16[1152,512]{1,0:T(8,128)(2,1)}) custom-call(s32[1]{0:T(128)} %bitcast.6.rep_ref, bf16[2304,512]{1,0:T(8,128)(2,1)} %bitcast.47, bf16[2304,512]{1,0:T(8,128)(2,1)} %bitcast.43, bf16[2,4,256,512]{3,2,1,0:T(8,128)(2,1)} %bitcast.52, ...), custom_call_target="tpu_custom_call" | custom-call | flops 24159191040 | bytes 20000000 | tf_op jit(solution)/shard_map/expert/pallas_call | solution.py:341
  388.6 7.9 all-to-all-done.1
  400.4 46.6 %expert.2 = (bf16[2,4,256,512]{3,2,1,0:T(8,128)(2,1)}, bf16[2,4,512,256]{3,2,1,0:T(8,128)(2,1)}, bf16[1152,512]{1,0:T(8,128)(2,1)}, bf16[1152,512]{1,0:T(8,128)(2,1)}) custom-call(s32[1]{0:T(128)} %bitcast.6.rep_ref, bf16[2304,512]{1,0:T(8,128)(2,1)} %bitcast.44, bf16[2304,512]{1,0:T(8,128)(2,1)} %bitcast.42, bf16[2,4,256,512]{3,2,1,0:T(8,128)(2,1)} %bitcast.11.wi_ref, ...), custom_call_target="tpu_custom_call" | custom-call | flops 24159191040 | bytes 20000000 | tf_op jit(solution)/shard_map/expert/pallas_call | solution.py:341
  447.0 5.0 all-to-all-start.11
  454.9 14.9 %all-to-all-done.11 = bf16[16,72,512]{2,1,0:T(8,128)(2,1)S(1)} async-done(((bf16[16,72,512]{2,1,0:T(8,128)(2,1)}), bf16[16,72,512]{2,1,0:T(8,128)(2,1)S(1)}, u32[]{:S(2)}, u32[]{:S(2)}) %all-to-all-start.11) | async-done | bytes 1179680 | tf_op jit(solution)/shard_map/all_to_all | solution.py:583
  470.8 24.1 %attention_backward.1 = (f32[4,197,512]{2,1,0:T(8,128)}, bf16[8,1024,128]{2,1,0:T(8,128)(2,1)}, f32[4,512]{1,0:T(4,128)}) custom-call(bf16[4,197,512]{2,1,0:T(8,128)(2,1)} %reshape.126.tokens_ref.refs_0_, bf16[4,197,512]{2,1,0:T(8,128)(2,1)} %reshape.150.refs_1_, f32[4,512]{1,0:T(4,128)} %pad_maximum_fusion.2.norms_ref.refs_2_, ...), custom_call_target="tpu_custom_call" | custom-call | tf_op jit(solution)/shard_map/attention_backward/pallas_call | solution.py:506
  494.9 29.5 %all_to_all.94 = bf16[8,1024,128]{2,1,0:T(8,128)(2,1)S(1)} all-to-all(bf16[8,1024,128]{2,1,0:T(8,128)(2,1)} %get-tuple-element.45), channel_id=1, replica_groups=mesh['rep'=2,'own'=2,'wide'=2,'narrow'=4] {'wide','narrow'}, dimensions={0} | all-to-all | bytes 4194304 | tf_op jit(solution)/shard_map/all_to_all | solution.py:566
  524.4 4.4 all-to-all-start.17
  530.0 24.5 %all-to-all-done.17 = bf16[8,512,256]{2,1,0:T(8,128)(2,1)} async-done(((bf16[8,512,256]{2,1,0:T(8,128)(2,1)}), bf16[8,512,256]{2,1,0:T(8,128)(2,1)}, u32[]{:S(2)}, u32[]{:S(2)}) %all-to-all-start.17) | async-done | bytes 2097184 | tf_op jit(solution)/shard_map/all_to_all | solution.py:566
  554.6 29.2 %all_to_all.95 = bf16[8,512,256]{2,1,0:T(8,128)(2,1)} all-to-all(bf16[8,512,256]{2,1,0:T(8,128)(2,1)S(1)} %bitcast.55), channel_id=1, replica_groups=mesh['rep'=2,'own'=2,'wide'=2,'narrow'=4] {'wide','narrow'}, dimensions={0} | all-to-all | bytes 4194304 | tf_op jit(solution)/shard_map/all_to_all | solution.py:566
  585.4 29.1 %all_to_all.96 = bf16[8,256,512]{2,1,0:T(8,128)(2,1)} all-to-all(bf16[8,256,512]{2,1,0:T(8,128)(2,1)S(1)} %bitcast.50), channel_id=1, replica_groups=mesh['rep'=2,'own'=2,'wide'=2,'narrow'=4] {'wide','narrow'}, dimensions={0} | all-to-all | bytes 4194304 | tf_op jit(solution)/shard_map/all_to_all | solution.py:566
  616.1 29.1 %all_to_all.97 = bf16[8,256,512]{2,1,0:T(8,128)(2,1)} all-to-all(bf16[8,256,512]{2,1,0:T(8,128)(2,1)S(1)} %bitcast.51), channel_id=1, replica_groups=mesh['rep'=2,'own'=2,'wide'=2,'narrow'=4] {'wide','narrow'}, dimensions={0} | all-to-all | bytes 4194304 | tf_op jit(solution)/shard_map/all_to_all | solution.py:566
  649.7 29.8 %all-to-all-done.10 = bf16[16,72,512]{2,1,0:T(8,128)(2,1)S(1)} async-done(((bf16[16,72,512]{2,1,0:T(8,128)(2,1)}), bf16[16,72,512]{2,1,0:T(8,128)(2,1)S(1)}, u32[]{:S(2)}, u32[]{:S(2)}) %all-to-all-start.10) | async-done | bytes 1179680 | tf_op jit(solution)/shard_map/all_to_all | solution.py:583
  687.3 18.9 %all-to-all-done.5 = bf16[16,72,512]{2,1,0:T(8,128)(2,1)S(1)} async-done(((bf16[16,72,512]{2,1,0:T(8,128)(2,1)}), bf16[16,72,512]{2,1,0:T(8,128)(2,1)S(1)}, u32[]{:S(2)}, u32[]{:S(2)}) %all-to-all-start.5) | async-done | bytes 1179680 | tf_op jit(solution)/shard_map/all_to_all | solution.py:583
  707.2 7.9 mix.1
  717.4 39.2 %psum.14 = f32[4,512]{1,0:T(4,128)S(1)} all-reduce(f32[4,512]{1,0:T(4,128)S(1)} %copy-done.15), channel_id=1, replica_groups=mesh['rep'=2,'own'=2,'wide'=2,'narrow'=4] {'rep','own','wide','narrow'}, use_global_device_ids=true, to_apply=%region_0.1 | all-reduce | flops 2048 | bytes 16384 | tf_op jit(solution)/shard_map/psum | solution.py:626
  760.4 10.7 %maximum_convert_fusion.1 = f32[32,512,256]{2,1,0:T(8,128)} fusion(bf16[16,512,256]{2,1,0:T(8,128)(2,1)} %all-gather.11.cloned.1.call-done, bf16[16,512,256]{2,1,0:T(8,128)(2,1)} %all-gather.9.cloned.1.call-done), kind=kLoop, calls=%fused_computation.1 | loop fusion | flops 8388608 | bytes 25165824 | tf_op jit(solution)/shard_map/convert_element_type | solution.py:618
  771.1 32.2 %all-gather.5.cloned.1.call-done = bf16[16,256,512]{2,1,0:T(8,128)(2,1)} async-done(((bf16[8,256,512]{2,1,0:T(8,128)(2,1)}), bf16[16,256,512]{2,1,0:T(8,128)(2,1)}) %all-gather.5.cloned.1.call-update) | async-done | bytes 4194320 | tf_op jit(solution)/shard_map/all_gather | solution.py:617
  803.3 10.7 %maximum_convert_fusion = f32[32,256,512]{2,1,0:T(8,128)} fusion(bf16[16,256,512]{2,1,0:T(8,128)(2,1)} %all-gather.7.cloned.1.call-done, bf16[16,256,512]{2,1,0:T(8,128)(2,1)} %all-gather.5.cloned.1.call-done), kind=kLoop, calls=%fused_computation | loop fusion | flops 8388608 | bytes 25165824 | tf_op jit(solution)/shard_map/convert_element_type | solution.py:618
  (85 shorter events, 52.8 us)
Async XLA Ops:
  11.3 30.9 %all-to-all-start = ((bf16[8,1024,128]{2,1,0:T(8,128)(2,1)}), bf16[8,1024,128]{2,1,0:T(8,128)(2,1)S(1)}, u32[]{:S(2)}, u32[]{:S(2)}) async-start(bf16[8,1024,128]{2,1,0:T(8,128)(2,1)} %broadcast_in_dim.2), calls=%async_computation | async-start | bytes 4194304 | tf_op jit(solution)/shard_map/all_to_all | solution.py:566
  42.2 30.3 %copy-start = (bf16[8,1024,128]{2,1,0:T(8,128)(2,1)}, bf16[8,1024,128]{2,1,0:T(8,128)(2,1)S(1)}, u32[]{:S(2)}) copy-start(bf16[8,1024,128]{2,1,0:T(8,128)(2,1)S(1)} %all-to-all-done.weights_ref.refs_3_) | copy-start | bytes 6291460
  72.5 30.1 %all-to-all-start.3 = ((bf16[8,256,512]{2,1,0:T(8,128)(2,1)}), bf16[8,256,512]{2,1,0:T(8,128)(2,1)}, u32[]{:S(2)}, u32[]{:S(2)}) async-start(bf16[8,256,512]{2,1,0:T(8,128)(2,1)} %get-tuple-element.53), calls=%async_computation.3 | async-start | bytes 4194304 | tf_op jit(solution)/shard_map/all_to_all | solution.py:566
  131.7 3.7 copy-start.13
  131.7 4.7 copy-start.14
  131.7 29.4 %all-to-all-start.4 = ((bf16[8,512,256]{2,1,0:T(8,128)(2,1)}), bf16[8,512,256]{2,1,0:T(8,128)(2,1)S(1)}, u32[]{:S(2)}, u32[]{:S(2)}) async-start(bf16[8,512,256]{2,1,0:T(8,128)(2,1)} %get-tuple-element.51), calls=%async_computation.4 | async-start | bytes 4194304 | tf_op jit(solution)/shard_map/all_to_all | solution.py:566
  161.1 60.7 %copy-start.10 = (bf16[8,512,256]{2,1,0:T(8,128)(2,1)}, bf16[8,512,256]{2,1,0:T(8,128)(2,1)S(1)}, u32[]{:S(2)}) copy-start(bf16[8,512,256]{2,1,0:T(8,128)(2,1)S(1)} %all-to-all-done.4) | copy-start | bytes 6291460
  221.8 3.2 copy-start.12
  221.8 4.3 copy-start.16
  221.8 5.1 copy-start.17
  221.8 5.1 copy-start.18
  221.8 5.1 copy-start.19
  221.8 5.1 copy-start.20
  221.8 57.4 %all-to-all-start.7 = ((bf16[32,72,512]{2,1,0:T(8,128)(2,1)}), bf16[32,72,512]{2,1,0:T(8,128)(2,1)S(1)}, u32[]{:S(2)}, u32[]{:S(2)}) async-start(bf16[32,72,512]{2,1,0:T(8,128)(2,1)} %bitcast.46), calls=%async_computation.7 | async-start | bytes 4718592 | tf_op jit(solution)/shard_map/all_to_all | solution.py:578
  279.2 60.0 %copy-start.6 = (bf16[32,72,512]{2,1,0:T(8,128)(2,1)}, bf16[32,72,512]{2,1,0:T(8,128)(2,1)S(1)}, u32[]{:S(2)}) copy-start(bf16[32,72,512]{2,1,0:T(8,128)(2,1)S(1)} %all-to-all-done.7) | copy-start | bytes 7077892
  339.2 57.3 %all-to-all-start.1 = ((bf16[32,72,512]{2,1,0:T(8,128)(2,1)}), bf16[32,72,512]{2,1,0:T(8,128)(2,1)S(1)}, u32[]{:S(2)}, u32[]{:S(2)}) async-start(bf16[32,72,512]{2,1,0:T(8,128)(2,1)} %bitcast.45), calls=%async_computation.1 | async-start | bytes 4718592 | tf_op jit(solution)/shard_map/all_to_all | solution.py:578
  396.5 3.9 copy-start.7
  396.5 50.5 %all-to-all-start.12 = ((bf16[16,72,512]{2,1,0:T(8,128)(2,1)}), bf16[16,72,512]{2,1,0:T(8,128)(2,1)S(1)}, u32[]{:S(2)}, u32[]{:S(2)}) async-start(bf16[16,72,512]{2,1,0:T(8,128)(2,1)} %bitcast.57), calls=%async_computation.12 | async-start | bytes 2359296 | tf_op jit(solution)/shard_map/all_to_all | solution.py:583
  447.0 5.0 copy-start.5
  447.0 7.9 copy-start.1
  447.0 22.7 %all-to-all-start.11 = ((bf16[16,72,512]{2,1,0:T(8,128)(2,1)}), bf16[16,72,512]{2,1,0:T(8,128)(2,1)S(1)}, u32[]{:S(2)}, u32[]{:S(2)}) async-start(bf16[16,72,512]{2,1,0:T(8,128)(2,1)} %bitcast.58), calls=%async_computation.11 | async-start | bytes 2359296 | tf_op jit(solution)/shard_map/all_to_all | solution.py:583
  524.4 30.1 %all-to-all-start.17 = ((bf16[8,512,256]{2,1,0:T(8,128)(2,1)}), bf16[8,512,256]{2,1,0:T(8,128)(2,1)}, u32[]{:S(2)}, u32[]{:S(2)}) async-start(bf16[8,512,256]{2,1,0:T(8,128)(2,1)} %bitcast.54), calls=%async_computation.17 | async-start | bytes 4194304 | tf_op jit(solution)/shard_map/all_to_all | solution.py:566
  528.8 228.4 %all-reduce.3.cloned.1.call-start = ((), (), s32[]{:S(2)}) async-start(), calls=%async_computation.18 | async-start | bytes 524288 | tf_op jit(solution)/shard_map/psum | solution.py:628
  529.9 24.7 %copy-start.11 = (bf16[2,4,512,256]{3,2,1,0:T(8,128)(2,1)S(1)}, bf16[2,4,512,256]{3,2,1,0:T(8,128)(2,1)}, u32[]{:S(2)}) copy-start(bf16[2,4,512,256]{3,2,1,0:T(8,128)(2,1)} %get-tuple-element.48) | copy-start | bytes 6291460
  529.9 230.4 %all-gather.11.cloned.1.call-start = ((), (), s32[]{:S(2)}) async-start(), calls=%async_computation.22 | async-start | bytes 6291456 | tf_op jit(solution)/shard_map/all_gather | solution.py:617
  554.5 205.8 %all-gather.9.cloned.1.call-start = ((), (), s32[]{:S(2)}) async-start(), calls=%async_computation.21 | async-start | bytes 6291456 | tf_op jit(solution)/shard_map/all_gather | solution.py:617
  583.8 187.3 %all-gather.7.cloned.1.call-start = ((), (), s32[]{:S(2)}) async-start(), calls=%async_computation.20 | async-start | bytes 6291456 | tf_op jit(solution)/shard_map/all_gather | solution.py:617
  645.2 34.2 %all-to-all-start.10 = ((bf16[16,72,512]{2,1,0:T(8,128)(2,1)}), bf16[16,72,512]{2,1,0:T(8,128)(2,1)S(1)}, u32[]{:S(2)}, u32[]{:S(2)}) async-start(bf16[16,72,512]{2,1,0:T(8,128)(2,1)} %bitcast.21), calls=%async_computation.10 | async-start | bytes 2359296 | tf_op jit(solution)/shard_map/all_to_all | solution.py:583
  649.0 154.3 %all-gather.5.cloned.1.call-start = ((), (), s32[]{:S(2)}) async-start(), calls=%async_computation.19 | async-start | bytes 6291456 | tf_op jit(solution)/shard_map/all_gather | solution.py:617
  679.4 7.8 copy-start.3
  679.4 26.7 %all-to-all-start.5 = ((bf16[16,72,512]{2,1,0:T(8,128)(2,1)}), bf16[16,72,512]{2,1,0:T(8,128)(2,1)S(1)}, u32[]{:S(2)}, u32[]{:S(2)}) async-start(bf16[16,72,512]{2,1,0:T(8,128)(2,1)} %bitcast.13), calls=%async_computation.5 | async-start | bytes 2359296 | tf_op jit(solution)/shard_map/all_to_all | solution.py:583
  707.2 10.2 %copy-start.15 = (f32[4,512]{1,0:T(4,128)S(1)}, f32[4,512]{1,0:T(4,128)}, u32[]{:S(2)}) copy-start(f32[4,512]{1,0:T(4,128)} %get-tuple-element.44) | copy-start | bytes 24580
  (4 other events, 5.2 us)
Sparse Core Ops, SparseCore 0:
  532.5 78.7 all-reduce.2
Sparse Core Ops, SparseCore 1:
  554.6 56.4 all-gather.10
  612.6 68.9 all-gather.8
  683.0 62.2 all-gather.6
  746.9 56.3 all-gather.4

commit v2 on v1

--- a/solution.py
+++ b/solution.py
@@ -24,6 +24,7 @@
 SLOTS = -(-CAP // 8) * 8
 IMG_ROWS = -(-SEQ // 16) * 16
 LANES = 128
+TAIL = 16
 VMEM_LIMIT = 56 * 1024 * 1024
 
 
@@ -65,67 +66,145 @@
     return pl.BlockSpec((1,) + shape[1:], lambda i: (i,) + rest)
 
 
-def route_kernel(rep, tile, routes_ref, routes_t_ref, gates_ref, cot_ref, slot_ref, slot_t_ref, *gd_refs):
+def back_rows(slot_ref, k, group, wide, offset):
+    first = TOP + k if wide else k
+    here = slot_ref[0, :, 2 * TOP + k : 2 * TOP + k + 1] == group
+    return jnp.where(here, slot_ref[0, :, first : first + 1] + offset, -1)
+
+
+def one_hot(mask):
+    return mask.astype(f32).astype(bf16)
+
+
+def route_kernel(plane, own_ref, routes_ref, routes_t_ref, back_ref, slot_t_ref):
     rows = routes_ref.shape[0]
+    quarters = EXPERTS // plane
+    groups = quarters // 2
     before = lax.broadcasted_iota(jnp.int32, (rows, rows), 0)
     after = lax.broadcasted_iota(jnp.int32, (rows, rows), 1)
     ids_t = lax.broadcasted_iota(jnp.int32, (EXPERTS, rows), 0)
     ids = lax.broadcasted_iota(jnp.int32, (rows, EXPERTS), 1)
     hot_t = [(ids_t == routes_t_ref[k : k + 1, :]).astype(f32) for k in range(TOP)]
     hot = [(ids == routes_ref[:, k : k + 1]).astype(f32) for k in range(TOP)]
-    count_t = dot(sum(hot_t).astype(bf16), (before < after).astype(f32).astype(bf16))
-    count = dot((after < before).astype(f32).astype(bf16), sum(hot).astype(bf16))
-    slot_t = []
+    count_t = dot(sum(hot_t).astype(bf16), one_hot(before < after))
+    count = dot(one_hot(after < before), sum(hot).astype(bf16))
+
+    def place_of(ids):
+        group, parity = ids // (2 * plane), ids // plane % 2
+        return ids % plane, jnp.where(parity == own_ref[0], group, groups + group)
+
     for k in range(TOP):
         rank_t = jnp.sum(hot_t[k] * count_t, axis=0, keepdims=True).astype(jnp.int32)
-        slot_t.append(routes_t_ref[k : k + 1, :] * SLOTS + rank_t)
-        slot_t_ref[k : k + 1, :] = slot_t[k]
+        place, q = place_of(routes_t_ref[k : k + 1, :])
+        slot_t_ref[k : k + 1, :] = (place * quarters + q) * SLOTS + rank_t
         rank = jnp.sum(hot[k] * count, axis=1, keepdims=True).astype(jnp.int32)
-        slot_ref[:, k : k + 1] = routes_ref[:, k : k + 1] * SLOTS + rank
-    cot = cot_ref[...].astype(f32)
-    weighed = [(gates_ref[:, k : k + 1] * cot).astype(bf16) for k in range(TOP)]
-    part = gd_refs[0].shape[0] // rep
+        chosen = routes_ref[:, k : k + 1]
+        item = chosen % (2 * plane)
+        back_ref[:, k : k + 1] = item * SLOTS + rank
+        back_ref[:, TOP + k : TOP + k + 1] = item * 2 * SLOTS + rank
+        back_ref[:, 2 * TOP + k : 2 * TOP + k + 1] = chosen // (2 * plane)
+
+
+def route(own, routes, plane):
+    rows = routes.shape[0]
+    return pl.pallas_call(
+        functools.partial(route_kernel, plane),
+        in_specs=[pl.BlockSpec(memory_space=pltpu.SMEM)] + [pl.BlockSpec(memory_space=pltpu.VMEM)] * 2,
+        out_shape=[
+            jax.ShapeDtypeStruct((rows, 3 * TOP), jnp.int32),
+            jax.ShapeDtypeStruct((TOP, rows), jnp.int32),
+        ],
+        compiler_params=pltpu.CompilerParams(vmem_limit_bytes=VMEM_LIMIT),
+        cost_estimate=pl.CostEstimate(flops=60_000_000, bytes_accessed=100_000, transcendentals=0),
+        name="route",
+    )(own, routes, routes.T)
+
+
+def grad_slots_kernel(plane, own_ref, sent_ref, *gd_refs):
+    rows = sent_ref.shape[1] - 2 * HEADER
+    features = sent_ref.shape[2]
+    header = jnp.concatenate(
+        [sent_ref[0, i * HEADER : (i + 1) * HEADER, :].astype(f32) for i in range(2)], axis=1
+    )[:, :rows]
+    before = lax.broadcasted_iota(jnp.int32, (rows, rows), 0)
+    after = lax.broadcasted_iota(jnp.int32, (rows, rows), 1)
+    ids_t = lax.broadcasted_iota(jnp.int32, (EXPERTS, rows), 0)
+    routes = [header[k : k + 1, :].astype(jnp.int32) for k in range(TOP)]
+    gates = [
+        (header[2 + k : 3 + k, :] + header[4 + k : 5 + k, :]) + header[6 + k : 7 + k, :]
+        for k in range(TOP)
+    ]
+    hot = [(ids_t == routes[k]).astype(f32) for k in range(TOP)]
+    count = dot(sum(hot).astype(bf16), one_hot(before < after))
+    slots = []
+    for k in range(TOP):
+        rank = jnp.sum(hot[k] * count, axis=0, keepdims=True).astype(jnp.int32)
+        q = routes[k] // plane
+        slot = ((q // 2) * plane + routes[k] % plane) * SLOTS + rank
+        slots.append(jnp.where(q % 2 == own_ref[0], slot, -1))
+    cot = sent_ref[0, 2 * HEADER :, :]
+    per = plane * SLOTS
     for g, gd_ref in enumerate(gd_refs):
-        for start in range(0, part, tile):
-            place = lax.broadcasted_iota(jnp.int32, (tile, rows), 0) + (g * part + start)
-            total = sum(
-                dot((place == slot_t[k]).astype(f32).astype(bf16), weighed[k]) for k in range(TOP)
-            ).astype(bf16)
-            for copy in range(rep):
-                gd_ref[copy * part + start : copy * part + start + tile, :] = total
-
-
-def route_and_grad_slots(routes, gates, cot, rep, groups, owners):
+        place = lax.broadcasted_iota(jnp.int32, (per, rows), 0) + g * per
+        here = [place == slot for slot in slots]
+        gate = sum(jnp.where(here[k], gates[k], 0.0) for k in range(TOP))
+        picked = dot(one_hot(here[0] | here[1]), cot)
+        weighed = jnp.sum(gate, axis=1, keepdims=True) * picked
+        for p in range(plane):
+            gd_ref[p, 0] = weighed[p * SLOTS : (p + 1) * SLOTS, :].astype(bf16)
+
+
+HEADER = 8
+
+
+def with_header(routes, gates, cot):
     rows, features = cot.shape
-    part = owners * SLOTS
-    tile = 384 if part % 384 == 0 else part
-    shapes = [
-        jax.ShapeDtypeStruct((rows, TOP), jnp.int32),
-        jax.ShapeDtypeStruct((TOP, rows), jnp.int32),
-    ] + [jax.ShapeDtypeStruct((rep * part, features), bf16)] * groups
+    high = lax.reduce_precision(gates, 8, 7)
+    middle = lax.reduce_precision(gates - high, 8, 7)
+    low = (gates - high) - middle
+    lines = jnp.concatenate([v.T for v in (routes.astype(f32), high, middle, low)], axis=0)
+    lines = jnp.pad(lines, ((0, 0), (0, 2 * features - rows))).astype(bf16)
+    return jnp.concatenate([lines[:, :features], lines[:, features:], cot], axis=0)
+
+
+def grad_slots(own, sent, plane, groups):
+    chunks, rows, features = sent.shape
+    shape = (plane, chunks, SLOTS, features)
     return pl.pallas_call(
-        functools.partial(route_kernel, rep, tile),
-        out_shape=shapes,
+        functools.partial(grad_slots_kernel, plane),
+        grid_spec=pltpu.PrefetchScalarGridSpec(
+            num_scalar_prefetch=1,
+            grid=(chunks,),
+            in_specs=[pl.BlockSpec((1, rows, features), lambda i, own: (own[1] ^ i, 0, 0))],
+            out_specs=[
+                pl.BlockSpec((plane, 1, SLOTS, features), lambda i, own: (0, i, 0, 0))
+            ]
+            * groups,
+        ),
+        out_shape=[jax.ShapeDtypeStruct(shape, bf16)] * groups,
         compiler_params=pltpu.CompilerParams(vmem_limit_bytes=VMEM_LIMIT),
-        name="route_grad_slots",
-    )(routes, routes.T, gates, cot)
-
-
-def unpack_weights(wide, narrow, weights_ref, qkv_scratch, out_scratch):
+        cost_estimate=pl.CostEstimate(flops=8_000_000_000, bytes_accessed=10_000_000, transcendentals=0),
+        name="grad_slots",
+    )(own, sent)
+
+
+def unpack_weights(wide, narrow, spot_ref, weights_refs, qkv_scratch, out_scratch):
     deep, across = qkv_scratch.shape[1] // wide, LANES
-    for x in range(wide):
-        for n in range(narrow):
-            block = x * narrow + n
-            for j in range(3):
-                qkv_scratch[j, x * deep : (x + 1) * deep, n * across : (n + 1) * across] = weights_ref[
-                    block, j * deep : (j + 1) * deep, :
-                ]
-            for c in range(deep // LANES):
-                first = 3 * deep + c * across
-                out_scratch[
-                    n * across : (n + 1) * across,
-                    x * deep + c * LANES : x * deep + (c + 1) * LANES,
-                ] = weights_ref[block, first : first + across, :]
+    for k in range(wide * narrow):
+        block_ref = weights_refs[k % 2].at[k // 2]
+        x = spot_ref[0] ^ (k // narrow)
+        n = spot_ref[1] ^ (k % narrow)
+        x_at = pl.multiple_of(x * deep, deep)
+        n_at = pl.multiple_of(n * across, across)
+        for j in range(3):
+            qkv_scratch[j, pl.ds(x_at, deep), pl.ds(n_at, across)] = block_ref[
+                j * deep : (j + 1) * deep, :
+            ]
+        for c in range(deep // LANES):
+            first = 3 * deep + c * across
+            out_scratch[
+                pl.ds(n_at, across), pl.ds(pl.multiple_of(x_at + c * LANES, LANES), LANES)
+            ] = block_ref[first : first + across, :]
 
 
 def head_masks():
@@ -141,24 +220,27 @@
 def forward_kernel(
     wide,
     narrow,
-    rep,
     tile,
+    spot_ref,
     tokens_ref,
     norms_ref,
-    weights_ref,
+    weights_a_ref,
+    weights_b_ref,
     slot_t_ref,
     proj_ref,
     att_ref,
     resid_ref,
-    *rest,
+    x_ref,
+    qkv_w,
+    out_w,
+    norm_scratch,
 ):
-    x_refs, (qkv_w, out_w, norm_scratch) = rest[:-3], rest[-3:]
     step = pl.program_id(0)
     features = tokens_ref.shape[2]
 
     @pl.when(step == 0)
     def _():
-        unpack_weights(wide, narrow, weights_ref, qkv_w, out_w)
+        unpack_weights(wide, narrow, spot_ref, (weights_a_ref, weights_b_ref), qkv_w, out_w)
         norm_scratch[...] = jnp.zeros_like(norm_scratch)
 
     stream = tokens_ref[0].astype(f32)
@@ -194,46 +276,73 @@
     def _():
         count = slot_t_ref.shape[1]
         rows = norm_scratch[...].reshape(count, features)
-        part = x_refs[0].shape[0] // rep
-        for g, x_ref in enumerate(x_refs):
-            for start in range(0, part, tile):
-                place = lax.broadcasted_iota(jnp.int32, (tile, count), 0) + (g * part + start)
-                here = (place == slot_t_ref[0:1, :]) | (place == slot_t_ref[1:2, :])
-                total = dot(here.astype(f32).astype(bf16), rows).astype(bf16)
-                for copy in range(rep):
-                    x_ref[copy * part + start : copy * part + start + tile, :] = total
-
-
-def attention_and_slots(tokens, norms, weights, slot_t, wide, narrow, rep, groups, owners):
+        for start in range(0, x_ref.shape[0], tile):
+            place = lax.broadcasted_iota(jnp.int32, (tile, count), 0) + start
+            here = (place == slot_t_ref[0:1, :]) | (place == slot_t_ref[1:2, :])
+            x_ref[start : start + tile, :] = dot(one_hot(here), rows).astype(bf16)
+
+
+def attention_and_slots(spot, tokens, norms, weights, slot_t, wide, narrow):
     images, rows, features = tokens.shape
-    part = owners * SLOTS
-    tile = 384 if part % 384 == 0 else part
-    slot_shape = (rep * part, features)
+    total = EXPERTS * SLOTS
+    tile = 384 if total % 384 == 0 else SLOTS * wide * narrow
     per_image = [(images, rows, 3 * features), (images, rows, features), (images, rows, features)]
     return pl.pallas_call(
-        functools.partial(forward_kernel, wide, narrow, rep, tile),
+        functools.partial(forward_kernel, wide, narrow, tile),
         grid=(images,),
         in_specs=[
+            pl.BlockSpec(memory_space=pltpu.SMEM),
             image_spec(tokens.shape),
             full_spec(norms.shape),
-            full_spec(weights.shape),
+            full_spec(weights[0].shape),
+            full_spec(weights[1].shape),
             full_spec(slot_t.shape),
         ],
-        out_specs=[image_spec(s) for s in per_image] + [full_spec(slot_shape)] * groups,
+        out_specs=[image_spec(s) for s in per_image] + [full_spec((total, features))],
         out_shape=[
             jax.ShapeDtypeStruct(per_image[0], bf16),
             jax.ShapeDtypeStruct(per_image[1], bf16),
             jax.ShapeDtypeStruct(per_image[2], f32),
-        ]
-        + [jax.ShapeDtypeStruct(slot_shape, bf16)] * groups,
+            jax.ShapeDtypeStruct((total, features), bf16),
+        ],
         scratch_shapes=[
             pltpu.VMEM((3, features, features), bf16),
             pltpu.VMEM((features, features), bf16),
             pltpu.VMEM((images, IMG_ROWS, features), bf16),
         ],
         compiler_params=pltpu.CompilerParams(vmem_limit_bytes=VMEM_LIMIT),
+        cost_estimate=pl.CostEstimate(flops=6_000_000_000, bytes_accessed=9_000_000, transcendentals=2_000_000),
         name="attention_forward",
-    )(tokens, norms, weights, slot_t)
+    )(spot, tokens, norms, *weights, slot_t)
+
+
+def pack_kernel(first_ref, w_in_ref, w_out_ref, *out_refs):
+    deep, hidden = w_in_ref.shape[1], w_in_ref.shape[2]
+    base = deep * (hidden // LANES) if len(out_refs) == 1 else 0
+    for c in range(hidden // LANES):
+        out_refs[0][0, c * deep : (c + 1) * deep, :] = w_in_ref[0, :, c * LANES : (c + 1) * LANES]
+    for c in range(deep // LANES):
+        out_refs[-1][0, base + c * hidden : base + (c + 1) * hidden, :] = w_out_ref[
+            0, :, c * LANES : (c + 1) * LANES
+        ]
+
+
+def pack(first, w_in, w_out, plane, arrays):
+    deep, hidden = w_in.shape[1], w_in.shape[2]
+    rows = 2 * deep * hidden // LANES // arrays
+    at = lambda i, first: (first[0] + i, 0, 0)
+    return pl.pallas_call(
+        pack_kernel,
+        grid_spec=pltpu.PrefetchScalarGridSpec(
+            num_scalar_prefetch=1,
+            grid=(plane,),
+            in_specs=[pl.BlockSpec((1, deep, hidden), at), pl.BlockSpec((1, hidden, deep), at)],
+            out_specs=[pl.BlockSpec((1, rows, LANES), lambda i, first: (i, 0, 0))] * arrays,
+        ),
+        out_shape=[jax.ShapeDtypeStruct((plane, rows, LANES), bf16)] * arrays,
+        cost_estimate=pl.CostEstimate(flops=0, bytes_accessed=9_000_000, transcendentals=0),
+        name="pack_weights",
+    )(first, w_in, w_out)
 
 
 GELU_A = math.sqrt(2.0 / math.pi)
@@ -254,113 +363,106 @@
     return (a == b).astype(f32).astype(bf16)
 
 
-def expert_kernel(
-    tile,
-    own_rows,
-    rep_ref,
-    x_ref,
-    gd_ref,
-    wi_ref,
-    wo_ref,
-    gin_ref,
-    gout_ref,
-    y_ref,
-    gx_ref,
-    x_t,
-    gd_t,
-    act,
-    gp,
-    wo_s,
-    y_acc,
-    gx_acc,
-):
+def expert_kernel(deep, hidden, parts, tile, where_ref, *refs):
+    x_refs, (gd_ref, wi_ref, wo_ref, gi_ref, go_ref) = refs[:parts], refs[parts : parts + 5]
+    gx_ref, y_ref = refs[parts + 5 : parts + 7]
+    (x_s, gd_s, act, gp, wi_s, wo_s, y_acc, gx_acc, sem) = refs[parts + 7 :]
     step = pl.program_id(0)
-    rows, features = x_ref.shape
-    wide, deep, hidden = wi_ref.shape[0], wi_ref.shape[2], wi_ref.shape[3]
+    wide = wi_ref.shape[0]
+    rows, features = x_s.shape
+    own_rows = rows // 2
+    chunk = own_rows // 2
 
     @pl.when(step == 0)
     def _():
-        eye = identity(features)
-
-        def turn(t, carry):
-            at = pl.ds(pl.multiple_of(t * tile, tile), tile)
-            x_t[:, at] = dot_bt(eye, x_ref[at, :]).astype(bf16)
-            gd_t[:, at] = dot_bt(eye, gd_ref[at, :]).astype(bf16)
-            return carry
-
-        lax.fori_loop(0, rows // tile, turn, 0)
+        copies = [pltpu.make_async_copy(gd_ref, gd_s, sem.at[parts])]
+        first = 0
+        for i, x_ref in enumerate(x_refs):
+            part = x_ref if len(x_ref.shape) == 2 else x_ref.at[where_ref[0]]
+            count = part.shape[0]
+            copies.append(pltpu.make_async_copy(part, x_s.at[pl.ds(first, count), :], sem.at[i]))
+            first += count
+        for copy in copies:
+            copy.start()
         y_acc[...] = jnp.zeros_like(y_acc)
         gx_acc[...] = jnp.zeros_like(gx_acc)
+        for copy in copies:
+            copy.wait()
+
 
     for x in range(wide):
-        wo_s[:, x * deep : (x + 1) * deep] = wo_ref[x, 0]
-    wi = wi_ref[:, 0].reshape(wide * deep, hidden)
-
-    def hidden_rows(t, carry):
-        at = pl.ds(pl.multiple_of(t * tile, tile), tile)
-        value, slope = gelu_pair(dot(x_ref[at, :], wi))
-        act[at, :] = value.astype(bf16)
-        gp[at, :] = (dot_bt(gd_ref[at, :], wo_s[...]) * slope).astype(bf16)
-        return carry
-
-    lax.fori_loop(0, rows // tile, hidden_rows, 0)
-
-    gin = dot(x_t[...], gp[...]).astype(bf16)
+        for c in range(hidden // LANES):
+            wi_s[x * deep : (x + 1) * deep, c * LANES : (c + 1) * LANES] = wi_ref[
+                x, 0, c * deep : (c + 1) * deep, :
+            ]
+        for c in range(deep // LANES):
+            first = x * deep + c * LANES
+            wo_s[:, first : first + LANES] = wo_ref[x, 0, c * hidden : (c + 1) * hidden, :]
+
+    for t in range(rows // tile):
+        at = slice(t * tile, (t + 1) * tile)
+        value, slope = gelu_pair(dot(x_s[at, :], wi_s[...]))
+        value = value.astype(bf16)
+        act[at, :] = value
+        back = (dot_bt(gd_s[at, :], wo_s[...]) * slope).astype(bf16)
+        gp[at, :] = back
+        if t < own_rows // tile:
+            y_acc[at, :] += dot(value, wo_s[...])
+            gx_acc[at, :] += dot_bt(back, wi_s[...])
+    gin = dot_at(x_s[...], gp[...]).astype(bf16)
     for x in range(wide):
-        gin_ref[x, 0] = gin[x * deep : (x + 1) * deep, :]
-    gout = dot_bt(identity(hidden), dot(gd_t[...], act[...]).astype(bf16)).astype(bf16)
+        for c in range(hidden // LANES):
+            gi_ref[x, 0, c * deep : (c + 1) * deep, :] = gin[
+                x * deep : (x + 1) * deep, c * LANES : (c + 1) * LANES
+            ]
+    gout = dot_at(act[...], gd_s[...]).astype(bf16)
     for x in range(wide):
-        gout_ref[x, 0] = gout[:, x * deep : (x + 1) * deep]
-
-    first = rep_ref[0] * own_rows
-
-    def own(t, carry):
-        at = pl.ds(pl.multiple_of(t * tile, tile), tile)
-        here = pl.ds(pl.multiple_of(first + t * tile, tile), tile)
-        y_acc[at, :] += dot(act[here, :], wo_s[...])
-        gx_acc[at, :] += dot_bt(gp[here, :], wi)
-        return carry
-
-    lax.fori_loop(0, own_rows // tile, own, 0)
+        for c in range(deep // LANES):
+            first = x * deep + c * LANES
+            go_ref[x, 0, c * hidden : (c + 1) * hidden, :] = gout[:, first : first + LANES]
 
     @pl.when(step == pl.num_programs(0) - 1)
     def _():
-        y_ref[...] = y_acc[...].astype(bf16)
-        gx_ref[...] = gx_acc[...].astype(bf16)
-
-
-def expert(rep_index, x, gd, w_in, w_out, own_rows, wide, narrow):
-    rows, features = x.shape
-    deep, hidden = w_in.shape[1], w_in.shape[2]
-    w_in = w_in.reshape(wide, narrow, deep, hidden)
-    w_out = w_out.reshape(wide, narrow, hidden, deep)
-    tile = 384 if own_rows % 384 == 0 else math.gcd(own_rows, 128)
-    in_spec = pl.BlockSpec((wide, 1, deep, hidden), lambda n, r: (0, n, 0, 0))
-    out_spec = pl.BlockSpec((wide, 1, hidden, deep), lambda n, r: (0, n, 0, 0))
-    whole = lambda shape: pl.BlockSpec(shape, lambda n, r: (0, 0))
-    gin, gout, y, gx = pl.pallas_call(
-        functools.partial(expert_kernel, tile, own_rows),
-        grid_spec=pltpu.PrefetchScalarGridSpec(
-            num_scalar_prefetch=1,
-            grid=(narrow,),
-            in_specs=[whole(x.shape), whole(gd.shape), in_spec, out_spec],
-            out_specs=[in_spec, out_spec, whole((own_rows, features)), whole((own_rows, features))],
-            scratch_shapes=[
-                pltpu.VMEM((features, rows), bf16),
-                pltpu.VMEM((features, rows), bf16),
-                pltpu.VMEM((rows, hidden), bf16),
-                pltpu.VMEM((rows, hidden), bf16),
-                pltpu.VMEM((hidden, features), bf16),
-                pltpu.VMEM((own_rows, features), f32),
-                pltpu.VMEM((own_rows, features), f32),
-            ],
-        ),
+        for i in range(2):
+            at = slice(i * chunk, (i + 1) * chunk)
+            to = pl.ds(pl.multiple_of((where_ref[1] ^ i) * chunk, chunk), chunk)
+            gx_ref[to, :] = gx_acc[at, :].astype(bf16)
+            y_ref[to, :] = y_acc[at, :].astype(bf16)
+
+
+def expert(where, xs, gd, weights, wide, narrow, deep, hidden):
+    rows, features = gd.shape
+    own_rows = rows // 2
+    chunk = own_rows // 2
+    packed = deep * hidden // LANES
+    last = len(weights) - 1
+    tile = 384 if own_rows % 384 == 0 else SLOTS * 2
+    anywhere = pl.BlockSpec(memory_space=pl.ANY)
+    whole = lambda shape: pl.BlockSpec(shape, lambda s: (0,) * len(shape))
+    per_step = pl.BlockSpec((wide, 1, packed, LANES), lambda s: (0, s, 0, 0))
+    blocks = (wide, narrow, packed, LANES)
+    g_in, g_out, gx, y = pl.pallas_call(
+        functools.partial(expert_kernel, deep, hidden, len(xs), tile),
+        grid=(narrow,),
+        in_specs=[pl.BlockSpec(memory_space=pltpu.SMEM)] + [anywhere] * (len(xs) + 1)
+        + [per_step, pl.BlockSpec((wide, 1, packed, LANES), lambda s: (0, s, 1 - last, 0))],
+        out_specs=[per_step] * 2 + [whole((own_rows, features))] * 2,
+        scratch_shapes=[
+            pltpu.VMEM((rows, features), bf16),
+            pltpu.VMEM((rows, features), bf16),
+            pltpu.VMEM((rows, hidden), bf16),
+            pltpu.VMEM((rows, hidden), bf16),
+            pltpu.VMEM((features, hidden), bf16),
+            pltpu.VMEM((hidden, features), bf16),
+            pltpu.VMEM((own_rows, features), f32),
+            pltpu.VMEM((own_rows, features), f32),
+            pltpu.SemaphoreType.DMA((len(xs) + 1,)),
+        ],
         out_shape=[
-            jax.ShapeDtypeStruct(w_in.shape, bf16),
-            jax.ShapeDtypeStruct(w_out.shape, bf16),
-            jax.ShapeDtypeStruct((own_rows, features), bf16),
-            jax.ShapeDtypeStruct((own_rows, features), bf16),
-        ],
+            jax.ShapeDtypeStruct(blocks, bf16),
+            jax.ShapeDtypeStruct(blocks, bf16),
+        ]
+        + [jax.ShapeDtypeStruct((own_rows, features), bf16)] * 2,
         compiler_params=pltpu.CompilerParams(vmem_limit_bytes=VMEM_LIMIT),
         cost_estimate=pl.CostEstimate(
             flops=2 * narrow * features * hidden * (4 * rows + 2 * own_rows),
@@ -368,61 +470,99 @@
             transcendentals=rows * hidden * narrow,
         ),
         name="expert",
-    )(rep_index, x, gd, w_in, w_out)
-    return gin.reshape(-1, deep, hidden), gout.reshape(-1, hidden, deep), y, gx
+    )(where, *xs, gd, *[w.reshape((wide, narrow) + w.shape[1:]) for w in (weights[0], weights[last])])
+    return [g.reshape(wide * narrow, packed, LANES) for g in (g_in, g_out)], gx, y
+
+
+def place_kernel(where_ref, g_ref, *refs):
+    out_ref = refs[-1]
+    rows = out_ref.shape[1]
+    for i in range(out_ref.shape[0]):
+        for c in range(out_ref.shape[2] // LANES):
+            out_ref[i, :, c * LANES : (c + 1) * LANES] = g_ref[
+                0, i, c * rows : (c + 1) * rows, :
+            ].astype(f32)
+
+
+def place(where, g, so_far, rows, columns):
+    g = g.reshape((-1,) + g.shape[-3:])
+    parts, plane, packed, _ = g.shape
+    each = math.gcd(plane, 4)
+    anywhere = pl.BlockSpec(memory_space=pl.ANY)
+    part = (lambda where: where[0]) if parts > 1 else (lambda where: 0)
+    return pl.pallas_call(
+        place_kernel,
+        grid_spec=pltpu.PrefetchScalarGridSpec(
+            num_scalar_prefetch=1,
+            grid=(plane // each,),
+            in_specs=[pl.BlockSpec((1, each, packed, LANES), lambda i, where: (part(where), i, 0, 0))]
+            + [anywhere] * len(so_far),
+            out_specs=pl.BlockSpec(
+                (each, rows, columns), lambda i, where: (where[1] // each + i, 0, 0)
+            ),
+        ),
+        out_shape=jax.ShapeDtypeStruct((EXPERTS, rows, columns), f32),
+        input_output_aliases={2 + i: i for i in range(len(so_far))},
+        compiler_params=pltpu.CompilerParams(vmem_limit_bytes=VMEM_LIMIT),
+        cost_estimate=pl.CostEstimate(flops=0, bytes_accessed=6_000_000, transcendentals=0),
+        name="place_grads",
+    )(where, g, *so_far)
 
 
 def mixed_kernel(resid_ref, slot_ref, gates_ref, *rest):
-    y_refs, mixed_ref = rest[:-1], rest[-1]
+    back_refs, mixed_ref = rest[:-1], rest[-1]
     total = resid_ref[0]
     rows = total.shape[0]
-    part = y_refs[0].shape[0]
     for k in range(TOP):
         picked = None
-        for g, y_ref in enumerate(y_refs):
-            place = lax.broadcasted_iota(jnp.int32, (rows, part), 1) + g * part
-            one = dot((place == slot_ref[0, :, k : k + 1]).astype(f32).astype(bf16), y_ref[...])
+        for g, back_ref in enumerate(back_refs):
+            wide = g < len(back_refs) - 1
+            place = lax.broadcasted_iota(jnp.int32, (rows, back_ref.shape[0]), 1)
+            here = place == back_rows(slot_ref, k, g, wide, SLOTS if wide else 0)
+            one = dot(one_hot(here), back_ref[...])
             picked = one if picked is None else picked + one
         total = total + gates_ref[0, :, k : k + 1] * picked
     mixed_ref[0] = total.astype(bf16)
 
 
-def mix(resid, slots, gates, ys):
+def mix(resid, slots, gates, backs):
     return pl.pallas_call(
         mixed_kernel,
         grid=(resid.shape[0],),
         in_specs=[image_spec(resid.shape), image_spec(slots.shape), image_spec(gates.shape)]
-        + [full_spec(y.shape) for y in ys],
+        + [full_spec(y.shape) for y in backs],
         out_specs=image_spec(resid.shape),
         out_shape=jax.ShapeDtypeStruct(resid.shape, bf16),
         compiler_params=pltpu.CompilerParams(vmem_limit_bytes=VMEM_LIMIT),
+        cost_estimate=pl.CostEstimate(flops=6_000_000_000, bytes_accessed=6_000_000, transcendentals=0),
         name="mix",
-    )(resid, slots, gates, *ys)
-
-
-def backward_kernel(wide, narrow, groups, *refs):
-    (tokens_ref, cot_ref, norms_ref, weights_ref, slot_ref, proj_ref, att_ref, resid_ref) = refs[:8]
-    gx_refs = refs[8 : 8 + groups]
-    (grad_ref, grads_w_ref, grads_n_ref) = refs[8 + groups : 11 + groups]
-    (qkv_w, out_w, normed_s, att_s, branch_s, proj_s) = refs[11 + groups :]
+    )(resid, slots, gates, *backs)
+
+
+def backward_kernel(wide, narrow, parts, *refs):
+    (spot_ref, tokens_ref, cot_ref, norms_ref, weights_a_ref, weights_b_ref) = refs[:6]
+    (slot_ref, proj_ref, att_ref, resid_ref) = refs[6:10]
+    back_refs = refs[10 : 10 + parts]
+    (grad_ref, grads_w_ref) = refs[10 + parts : 12 + parts]
+    (qkv_w, out_w, normed_s, att_s, branch_s, proj_s, grads_n_ref) = refs[12 + parts :]
     step = pl.program_id(0)
     rows, features = tokens_ref.shape[1], tokens_ref.shape[2]
 
     @pl.when(step == 0)
     def _():
-        unpack_weights(wide, narrow, weights_ref, qkv_w, out_w)
+        unpack_weights(wide, narrow, spot_ref, (weights_a_ref, weights_b_ref), qkv_w, out_w)
         normed_s[...] = jnp.zeros_like(normed_s)
         att_s[...] = jnp.zeros_like(att_s)
         branch_s[...] = jnp.zeros_like(branch_s)
         proj_s[...] = jnp.zeros_like(proj_s)
         grads_n_ref[...] = jnp.zeros_like(grads_n_ref)
 
-    part = gx_refs[0].shape[0]
     grad_normed = None
-    for g, gx_ref in enumerate(gx_refs):
-        place = lax.broadcasted_iota(jnp.int32, (rows, part), 1) + g * part
-        here = (place == slot_ref[0, :, 0:1]) | (place == slot_ref[0, :, 1:2])
-        one = dot(here.astype(f32).astype(bf16), gx_ref[...])
+    for g, back_ref in enumerate(back_refs):
+        place = lax.broadcasted_iota(jnp.int32, (rows, back_ref.shape[0]), 1)
+        own = [back_rows(slot_ref, k, g, g < parts - 1, 0) for k in range(TOP)]
+        here = (place == own[0]) | (place == own[1])
+        one = dot(one_hot(here), back_ref[...])
         grad_normed = one if grad_normed is None else grad_normed + one
     hat_two, scale_two = norm_parts(resid_ref[0])
     grads_n_ref[2:3, :] += jnp.sum(grad_normed * hat_two, axis=0, keepdims=True)
@@ -452,13 +592,13 @@
             dprobs = dot_bt(v, ga_h)
             inner = jnp.sum(probs * dprobs, axis=0, keepdims=True)
             grad_scores = (probs * (dprobs - inner)).astype(bf16)
-            parts = (
+            parts_h = (
                 dot_at(grad_scores, masked(k, mask)),
                 dot(grad_scores, masked(q, mask)),
                 dot(probs.astype(bf16), ga_h),
             )
             for j in range(3):
-                sums[j] = parts[j] if sums[j] is None else sums[j] + parts[j]
+                sums[j] = parts_h[j] if sums[j] is None else sums[j] + parts_h[j]
         pieces[0][pair] = (sums[0] * scale).astype(bf16)
         pieces[1][pair] = (sums[1] * scale).astype(bf16)
         pieces[2][pair] = sums[2].astype(bf16)
@@ -489,6 +629,19 @@
                     grads_w_ref[x * narrow + n, j * deep : (j + 1) * deep, :] = grad[
                         x * deep : (x + 1) * deep, n * LANES : (n + 1) * LANES
                     ]
+        per = features // LANES
+        tail = jnp.concatenate(
+            [
+                grads_n_ref[i : i + 1, c * LANES : (c + 1) * LANES]
+                for i in range(4)
+                for c in range(per)
+            ],
+            axis=0,
+        )
+        high = tail.astype(bf16)
+        both = jnp.concatenate([high, (tail - high.astype(f32)).astype(bf16)], axis=0)
+        for d in range(wide * narrow):
+            grads_w_ref[d, grads_w_ref.shape[1] - 2 * TAIL :, :] = both
         grad = dot_at(flat(att_s[...]), flat(branch_s[...])).astype(bf16)
         for x in range(wide):
             for n in range(narrow):
@@ -500,28 +653,30 @@
                     ]
 
 
-def attention_back(tokens, cot, norms, weights, slots, proj, att, resid, gxs, wide, narrow):
+def attention_back(spot, tokens, cot, norms, weights, slots, proj, att, resid, backs, wide, narrow):
     images, rows, features = tokens.shape
     stash = (images, IMG_ROWS, features)
+    small = (wide * narrow, weights[0].shape[1] + 2 * TAIL, LANES)
     return pl.pallas_call(
-        functools.partial(backward_kernel, wide, narrow, len(gxs)),
+        functools.partial(backward_kernel, wide, narrow, len(backs)),
         grid=(images,),
         in_specs=[
+            pl.BlockSpec(memory_space=pltpu.SMEM),
             image_spec(tokens.shape),
             image_spec(cot.shape),
             full_spec(norms.shape),
-            full_spec(weights.shape),
+            full_spec(weights[0].shape),
+            full_spec(weights[1].shape),
             image_spec(slots.shape),
             image_spec(proj.shape),
             image_spec(att.shape),
             image_spec(resid.shape),
         ]
-        + [full_spec(gx.shape) for gx in gxs],
-        out_specs=[image_spec(tokens.shape), full_spec(weights.shape), full_spec((4, features))],
+        + [full_spec(back.shape) for back in backs],
+        out_specs=[image_spec(tokens.shape), full_spec(small)],
         out_shape=[
             jax.ShapeDtypeStruct(tokens.shape, f32),
-            jax.ShapeDtypeStruct(weights.shape, bf16),
-            jax.ShapeDtypeStruct((4, features), f32),
+            jax.ShapeDtypeStruct(small, bf16),
         ],
         scratch_shapes=[
             pltpu.VMEM((3, features, features), bf16),
@@ -530,10 +685,12 @@
             pltpu.VMEM(stash, bf16),
             pltpu.VMEM(stash, bf16),
             pltpu.VMEM((3,) + stash, bf16),
+            pltpu.VMEM((4, features), f32),
         ],
         compiler_params=pltpu.CompilerParams(vmem_limit_bytes=VMEM_LIMIT),
+        cost_estimate=pl.CostEstimate(flops=9_000_000_000, bytes_accessed=12_000_000, transcendentals=2_000_000),
         name="attention_backward",
-    )(tokens, cot, norms, weights, slots, proj, att, resid, *gxs)
+    )(spot, tokens, cot, norms, *weights, slots, proj, att, resid, *backs)
 
 
 def owned_on_device(
@@ -551,86 +708,174 @@
     w_expert_in,
     w_expert_out,
 ):
-    rep, own_planes, wide, narrow = sizes
-    plane = wide * narrow
-    owners = own_planes * plane
-    groups = EXPERTS // owners
-    everyone = ("rep", "own", "wide", "narrow")
+    pairs, wide, narrow = sizes
+    planes, plane = 2 * pairs, wide * narrow
+    groups = EXPERTS // (2 * plane)
     rows, features = tokens.shape
     images = rows // SEQ
-    deep = w_qkv.shape[1]
-    rep_index = lax.axis_index("rep").astype(jnp.int32).reshape(1)
-    own_index = lax.axis_index("own")
+    qkv_deep = w_qkv.shape[1]
+    deep, hidden = w_expert_in.shape[1], w_expert_in.shape[2]
+    pair_index, parity = lax.axis_index("pair"), lax.axis_index("parity")
+    x_index, n_index = lax.axis_index("wide"), lax.axis_index("narrow")
+    own = parity.astype(jnp.int32).reshape(1)
+    own_and_plane = jnp.stack([parity, 2 * pair_index + parity]).astype(jnp.int32)
+    far_and_own = jnp.stack([1 - pair_index, parity]).astype(jnp.int32)
+    spot = jnp.stack([x_index, n_index, x_index * narrow + n_index]).astype(jnp.int32)
 
     def in_plane(values):
         return lax.all_to_all(values, ("wide", "narrow"), 0, 0, tiled=True)
 
+    def in_pair(values):
+        return lax.all_to_all(values, ("parity", "wide", "narrow"), 0, 0, tiled=True)
+
+    def across(values, k):
+        return lax.ppermute(values, ("wide", "narrow"), [(i, i ^ k) for i in range(plane)])
+
+    def along(values, k):
+        return lax.ppermute(values, ("pair", "parity"), [(i, i ^ k) for i in range(planes)])
+
+    def with_near(values):
+        return lax.all_gather(values, "parity", axis=0)
+
+    def after(values, first):
+        return lax.optimization_barrier((values, first))[0]
+
     small = jnp.concatenate(
-        [w_qkv.reshape(3 * deep, LANES)]
-        + [w_attn_out[:, c * LANES : (c + 1) * LANES] for c in range(deep // LANES)],
+        [w_qkv.reshape(3 * qkv_deep, LANES)]
+        + [w_attn_out[:, c * LANES : (c + 1) * LANES] for c in range(qkv_deep // LANES)],
         axis=0,
     )
-    weights = in_plane(jnp.broadcast_to(small[None], (plane,) + small.shape))
-
-    slots, slot_t, *gds = route_and_grad_slots(routes, gates, grad_out, rep, groups, owners)
-
-    def to_owners(values):
-        return lax.all_to_all(
-            values.reshape(-1, SLOTS, features), everyone, 0, 0, tiled=True
-        ).reshape(-1, features)
-
-    def to_tokens(values):
-        return lax.all_to_all(
-            values.reshape(-1, SLOTS, features), ("own", "wide", "narrow"), 0, 0, tiled=True
-        ).reshape(-1, features)
-
-    def owned(values, g):
-        return in_plane(
-            lax.dynamic_slice_in_dim(values, g * owners + own_index * plane, plane, axis=0)
+    same_core = jnp.stack([small] + [across(small, k) for k in range(2, plane, 2)])
+    weights = (same_core, across(same_core, 1))
+
+    sent_all = lax.all_gather(with_header(routes, gates, grad_out), ("pair", "parity"), axis=0)
+
+    back_slots, slot_t = route(own, routes, plane)
+    packed = [
+        pack(
+            (g * 2 * plane + parity * plane).astype(jnp.int32).reshape(1),
+            w_expert_in,
+            w_expert_out,
+            plane,
+            1 if g else 2,
         )
-
-    w_in = [owned(w_expert_in, g) for g in range(groups)]
-    w_out = [owned(w_expert_out, g) for g in range(groups)]
+        for g in range(groups)
+    ]
 
     norms = jnp.stack([ln1_gain, ln1_bias, ln2_gain, ln2_bias])
     per_image = lambda values: values.reshape((images, SEQ) + values.shape[1:])
     slot_wide = jnp.pad(
         slot_t.reshape(TOP, images, SEQ), ((0, 0), (0, 0), (0, IMG_ROWS - SEQ)), constant_values=-1
     ).reshape(TOP, images * IMG_ROWS)
-    tokens3, cot3, slots3, gates3 = map(per_image, (tokens, grad_out, slots, gates))
-    proj, att, resid, *xs = attention_and_slots(
-        tokens3, norms, weights, slot_wide, wide, narrow, rep, groups, owners
-    )
-
-    gd_all = [to_owners(v) for v in gds]
-    x_all = [to_owners(v) for v in xs]
-    grads_in, grads_out, ys, gxs = zip(
-        *[
-            expert(rep_index, x_all[g], gd_all[g], w_in[g], w_out[g], owners * SLOTS, wide, narrow)
-            for g in range(groups)
-        ]
-    )
-    gx_back = [to_tokens(v) for v in gxs]
-    y_back = [to_tokens(v) for v in ys]
-
-    def to_blocks(parts):
-        pieces = [lax.all_gather(in_plane(v), "own", axis=0, tiled=True) for v in parts]
-        return jnp.concatenate(pieces, axis=0).astype(f32)
-
-    out_in, out_out = to_blocks(grads_in), to_blocks(grads_out)
-
-    mixed = mix(resid, slots3, gates3, y_back).reshape(rows, features)
-    grad_input, grads_w, grads_n = attention_back(
-        tokens3, cot3, norms, weights, slots3, proj, att, resid, gx_back, wide, narrow
-    )
-    grads_n = lax.psum(grads_n, everyone)
-    block = jnp.sum(in_plane(grads_w).astype(f32), axis=0).astype(bf16)
-    block = lax.psum(block, ("rep", "own")).astype(f32)
-    grad_qkv = block[: 3 * deep].reshape(3, deep, LANES)
+    tokens3, cot3, slots3, gates3 = map(per_image, (tokens, grad_out, back_slots, gates))
+    proj, att, resid, x = attention_and_slots(
+        spot, tokens3, norms, weights, slot_wide, wide, narrow
+    )
+
+    def quarter(moved, q):
+        return moved[:, q * SLOTS : (q + 1) * SLOTS].reshape(plane * SLOTS, features)
+
+    def by_plane(values):
+        return jnp.moveaxis(values.reshape(plane, planes, SLOTS, features), 1, 0).reshape(
+            planes * plane * SLOTS, features
+        )
+
+    gd_sent = grad_slots(own_and_plane, sent_all, plane, groups)
+    first_in = in_plane(after(packed[0][0], same_core))
+    moved = in_plane(after(x, first_in).reshape(plane, -1, features))
+    first_out = in_plane(after(packed[0][1], (moved, gd_sent)))
+    mine, other = quarter(moved, 0), quarter(moved, groups)
+    nearest, far_mine = along(other, 1), along(mine, 2)
+    xs = [[mine, nearest, far_mine, along(other, 3)]]
+    gd_parts = [v.reshape(plane, planes * SLOTS, features) for v in gd_sent]
+    gds = [by_plane(in_plane(after(gd_parts[0], (first_out, nearest, far_mine, packed[1:]))))]
+    nears = [
+        jnp.concatenate([quarter(moved, g), along(quarter(moved, groups + g), 1)], axis=0)
+        for g in range(1, groups)
+    ]
+    xs += [
+        [near, lax.all_gather(after(near, xs[0]), "pair", axis=0)] for near in nears
+    ]
+
+    def to_tokens(parts, before):
+        sent = jnp.concatenate([v.reshape(2 * plane, SLOTS, features) for v in parts], axis=1)
+        return in_pair(after(sent, before)).reshape(-1, features)
+
+    shapes = ((deep, hidden), (hidden, deep))
+    out_blocks = [(), ()]
+
+    def put(i, g, own_part, before):
+        which = parity if own_part else 1 - parity
+        where = jnp.stack([which, g * 2 * plane + which * plane]).astype(jnp.int32)
+        part = after((grads if own_part else swaps)[g][i], before)
+        out_blocks[i] = (place(where, part, out_blocks[i], *shapes[i]),)
+
+    def after_blocks(values):
+        values, out_blocks[:] = lax.optimization_barrier((values, out_blocks))
+        return values
+
+    held = (first_in, first_out)
+    before = (gds[0], xs[0], nears)
+    grads, swaps, gx_back, y_back = [], [], [], []
+    for g in range(groups):
+        grad, gx, y = expert(far_and_own, xs[g], gds[g], held, wide, narrow, deep, hidden)
+        grads.append([])
+        swaps.append([])
+        if g < groups - 1:
+            held = tuple(in_plane(after(v, before)) for v in packed[g + 1])
+            grads[g].append(in_plane(after(grad[0], held)))
+            swaps[g].append(with_near(grads[g][0]))
+            gds.append(by_plane(in_plane(after(gd_parts[g + 1], (grads[g][0], xs[g + 1])))))
+            put(0, g, True, ())
+            grads[g].append(in_plane(after_blocks(after(grad[1], gds[g + 1]))))
+            swaps[g].append(with_near(grads[g][1]))
+            gds[g + 1] = after(gds[g + 1], grads[g][1])
+            before = to_tokens([gx, y], grads[g][1])
+            y_back.append(before)
+            gx_back.append(before)
+        else:
+            grads[g].append(in_plane(after(grad[0], before)))
+            swaps[g].append(with_near(grads[g][0]))
+            if g:
+                put(1, g - 1, True, ())
+                put(0, g - 1, False, ())
+            before = to_tokens([after_blocks(gx)], grads[g][0])
+            gx_back.append(before)
+            grads[g].append(in_plane(after(grad[1], before)))
+            before = grads[g][1]
+            last_y = y
+
+    last = groups - 1
+    grad_input, grads_w = attention_back(
+        spot, tokens3, cot3, norms, weights, slots3, proj, att, resid, gx_back, wide, narrow
+    )
+    count = grads_w.shape[1] - 2 * TAIL
+    swaps[last].append(with_near(after(grads[last][1], grads_w)))
+    grads_w = in_plane(after(grads_w, before))
+    y_back.append(to_tokens([last_y], grads_w))
+    for g in range(last):
+        put(1, g, False, ())
+    put(0, last, True, ())
+    put(1, last, True, ())
+    put(0, last, False, ())
+    mixed = mix(after_blocks(resid), slots3, gates3, y_back).reshape(rows, features)
+    put(1, last, False, mixed)
+    (out_in,), (out_out,) = out_blocks
+    summed = jnp.sum(grads_w.astype(f32), axis=0)
+    tail = summed[count : count + TAIL] + summed[count + TAIL :]
+    high = lax.reduce_precision(tail, 8, 7)
+    block = jnp.concatenate(
+        [summed[:count].astype(bf16), high.astype(bf16), (tail - high).astype(bf16)], axis=0
+    )
+    terms = after([block] + [along(block, k) for k in range(1, planes)], mixed)
+    terms = [v.astype(f32) for v in terms]
+    block = (terms[0] + terms[1]) + (terms[2] + terms[3])
+    grads_n = (block[count : count + TAIL] + block[count + TAIL :]).reshape(4, features)
+    grad_qkv = block[: 3 * qkv_deep].reshape(3, qkv_deep, LANES)
     grad_attn_out = jnp.concatenate(
         [
-            block[3 * deep + c * LANES : 3 * deep + (c + 1) * LANES]
-            for c in range(deep // LANES)
+            block[3 * qkv_deep + c * LANES : 3 * qkv_deep + (c + 1) * LANES]
+            for c in range(qkv_deep // LANES)
         ],
         axis=1,
     )
@@ -903,17 +1148,21 @@
 
 
 def solution(mesh):
-    dp, wide, narrow = (mesh.shape[name] for name in ("dp", "wide", "narrow"))
-    for rep in (2, 1):
-        if dp % rep == 0 and EXPERTS % ((dp // rep) * wide * narrow) == 0:
-            sizes = (rep, dp // rep, wide, narrow)
-            split = Mesh(mesh.devices.reshape(sizes), ("rep", "own", "wide", "narrow"))
-            return placed(functools.partial(owned_on_device, sizes), split, ("rep", "own"))
-    return placed(on_device, mesh, ("dp",))
-
-
-def placed(function, mesh, dp_axes):
-    rows = P(dp_axes + ("wide", "narrow"), None)
+    planes, wide, narrow = (mesh.shape[name] for name in ("dp", "wide", "narrow"))
+    plane = wide * narrow
+    if planes == 4 and EXPERTS % (2 * plane) == 0 and plane & (plane - 1) == 0 and narrow % 2 == 0:
+        sizes = (planes // 2, 2, wide, narrow)
+        split = Mesh(mesh.devices.reshape(sizes), ("pair", "parity", "wide", "narrow"))
+        return placed(
+            functools.partial(owned_on_device, (planes // 2, wide, narrow)),
+            split,
+            ("pair", "parity", "wide", "narrow"),
+        )
+    return placed(on_device, mesh, ("dp", "wide", "narrow"))
+
+
+def placed(function, mesh, row_axes):
+    rows = P(row_axes, None)
     specs_in = (
         rows,
         rows,

time: 823 us -> 572 us (0.70)
  the two profiles are of different devices: /device:TPU:0 before, /device:TPU:10 now
where the time goes in v2:
time: 572 us; the launch traced here: 561 us
  waiting for transfers between devices  235 us (41%)
  Pallas kernels  184 us (32%)
  starting transfers between devices  86.5 us (15%)
  local copies, waits for them, and re-layouts  24.8 us (4%)
  between operations  16 us (3%)
  other arithmetic  15.2 us (3%)
    all_to_all x11, waiting for transfers between devices, in_plane(): return lax.all_to_all(values, ('wide', 'narrow'), 0, 0, tiled=True)  126 us
    pallas_call x2, Pallas kernels, expert(): pl.pallas_call(functools.partial(expert_kernel, deep, hidden, len(xs), ti...  69.4 us
    all_to_all x11, starting transfers between devices, in_plane(): return lax.all_to_all(values, ('wide', 'narrow'), 0, 0, tiled=True)  55.1 us
    ppermute x7, waiting for transfers between devices, along(): lax.ppermute(values, ('pair', 'parity'), [(i, i ^ k) for i in range(plane...  53.1 us
    pallas_call x8, Pallas kernels, place(): pl.pallas_call(place_kernel, grid_spec=pltpu.PrefetchScalarGridSpec(num_s...  33 us
    pallas_call x1, Pallas kernels, attention_back(): pl.pallas_call(functools.partial(backward_kernel, wide, narrow, len(backs...  25.7 us
    all_to_all x3, waiting for transfers between devices, in_pair(): lax.all_to_all(values, ('parity', 'wide', 'narrow'), 0, 0, tiled=True)  24.4 us
    all_to_all x3, starting transfers between devices, in_pair(): lax.all_to_all(values, ('parity', 'wide', 'narrow'), 0, 0, tiled=True)  17.6 us
  transfers between devices with their start and end apart: 31, of which 22 were waited for; matrix products, arithmetic and copies ran while one was open for 5% of the time, Pallas kernels for 32%

profile of v2, /device:TPU:10, one launch (start us, length us, event | category | flops | bytes accessed | tf_op | source)
XLA Modules:
  0.0 561.4 jit_solution(25172766858929750)
XLA Ops:
  15.3 6.9 %pack_weights.2 = (bf16[8,1024,128]{2,1,0:T(8,128)(2,1)}, bf16[8,1024,128]{2,1,0:T(8,128)(2,1)}) custom-call(s32[1]{0:T(128)} %bitcast.17.first_ref, bf16[32,256,512]{2,1,0:T(8,128)(2,1)} %w_in_ref.3, bf16[32,512,256]{2,1,0:T(8,128)(2,1)} %w_out_ref.3), custom_call_target="tpu_custom_call" | custom-call | bytes 9000000 | tf_op jit(solution)/shard_map/pack_weights/pallas_call | solution.py:334
  22.2 4.3 collective-permute-done.2
  41.8 15.1 %attention_forward.1 = (bf16[4,197,1536]{2,1,0:T(8,128)(2,1)}, bf16[4,197,512]{2,1,0:T(8,128)(2,1)}, f32[4,197,512]{2,1,0:T(8,128)}, bf16[2304,512]{1,0:T(8,128)(2,1)}) custom-call(s32[3]{0:T(128)} %pad_add_fusion.spot_ref.refs_0_, bf16[4,197,512]{2,1,0:T(8,128)(2,1)} %reshape.156.tokens_ref.refs_1_, f32[4,512]{1,0:T(4,128)} %pad_maximum_fusion.7.norms_ref.refs_3_, ...), custom_call_target="tpu_custom_call" | custom-call | flops 6000000000 | bytes 9000000 | tf_op jit(solution)/shard_map/attention_forward/pallas_call | solution.py:290
  63.5 13.3 %all-gather.24.cloned.1.call-done.sent_ref = bf16[4,804,512]{2,1,0:T(8,128)(2,1)} async-done(((bf16[1,804,512]{2,1,0:T(8,128)(2,1)}), bf16[4,804,512]{2,1,0:T(8,128)(2,1)}) %all-gather.24.cloned.1.call-update) | async-done | bytes 3293200 | tf_op jit(solution)/shard_map/all_gather | solution.py:751
  76.8 13.5 %grad_slots.1 = (bf16[8,4,72,512]{3,2,1,0:T(8,128)(2,1)}, bf16[8,4,72,512]{3,2,1,0:T(8,128)(2,1)}) custom-call(s32[2]{0:T(128)} %pad_add_fusion.3.own_ref, bf16[4,804,512]{2,1,0:T(8,128)(2,1)} %all-gather.24.cloned.1.call-done.sent_ref), custom_call_target="tpu_custom_call" | custom-call | flops 8000000000 | bytes 10000000 | tf_op jit(solution)/shard_map/grad_slots/pallas_call | solution.py:173
  90.9 4.8 all-to-all-start.2
  100.3 6.7 %pack_weights.3 = bf16[8,2048,128]{2,1,0:T(8,128)(2,1)} custom-call(s32[1]{0:T(128)} %bitcast.32.first_ref, bf16[32,256,512]{2,1,0:T(8,128)(2,1)} %w_in_ref.3, bf16[32,512,256]{2,1,0:T(8,128)(2,1)} %w_out_ref.3), custom_call_target="tpu_custom_call" | custom-call | bytes 9000000 | tf_op jit(solution)/shard_map/pack_weights/pallas_call | solution.py:334
  107.0 18.0 %collective-permute-done.6.refs_2_ = bf16[576,512]{1,0:T(8,128)(2,1)S(1)} collective-permute-done((bf16[576,512]{1,0:T(8,128)(2,1)S(1)}, bf16[576,512]{1,0:T(8,128)(2,1)S(1)}, u32[]{:S(2)}, u32[]{:S(2)}) %collective-permute-start.6) | collective-permute-done | bytes 589856 | tf_op jit(solution)/shard_map/ppermute | solution.py:735
  134.2 13.3 %collective-permute-done.4 = bf16[576,512]{1,0:T(8,128)(2,1)S(1)} collective-permute-done((bf16[576,512]{1,0:T(8,128)(2,1)S(1)}, bf16[576,512]{1,0:T(8,128)(2,1)S(1)}, u32[]{:S(2)}, u32[]{:S(2)}) %collective-permute-start.4) | collective-permute-done | bytes 589856 | tf_op jit(solution)/shard_map/ppermute | solution.py:735
  148.6 10.7 %all-to-all-done.3 = bf16[8,288,512]{2,1,0:T(8,128)(2,1)S(1)} async-done(((bf16[8,288,512]{2,1,0:T(8,128)(2,1)}), bf16[8,288,512]{2,1,0:T(8,128)(2,1)S(1)}, u32[]{:S(2)}, u32[]{:S(2)}) %all-to-all-start.3) | async-done | bytes 2359328 | tf_op jit(solution)/shard_map/all_to_all | solution.py:726
  161.3 5.0 all-to-all-start.4
  167.0 34.7 %expert.2 = (bf16[2,4,1024,128]{3,2,1,0:T(8,128)(2,1)}, bf16[2,4,1024,128]{3,2,1,0:T(8,128)(2,1)}, bf16[1152,512]{1,0:T(8,128)(2,1)}, bf16[1152,512]{1,0:T(8,128)(2,1)}) custom-call(s32[2]{0:T(128)} %pad_add_fusion.2.where_ref, bf16[576,512]{1,0:T(8,128)(2,1)} %bitcast.105, bf16[576,512]{1,0:T(8,128)(2,1)} %copy-done.22, bf16[576,512]{1,0:T(8,128)(2,1)} %copy-done.21, ...), custom_call_target="tpu_custom_call" | custom-call | flops 24159191040 | bytes 20000000 | tf_op jit(solution)/shard_map/expert/pallas_call | solution.py:444
  201.7 12.4 %all-to-all-done.4 = bf16[8,2048,128]{2,1,0:T(8,128)(2,1)} async-done(((bf16[8,2048,128]{2,1,0:T(8,128)(2,1)}), bf16[8,2048,128]{2,1,0:T(8,128)(2,1)}, u32[]{:S(2)}, u32[]{:S(2)}) %all-to-all-start.4) | async-done | bytes 4194336 | tf_op jit(solution)/shard_map/all_to_all | solution.py:726
  218.1 9.9 %all-gather.14.cloned.1.call-done = bf16[2304,512]{1,0:T(8,128)(2,1)} async-done(((bf16[1152,512]{1,0:T(8,128)(2,1)}), bf16[2304,512]{1,0:T(8,128)(2,1)}) %all-gather.14.cloned.1.call-update) | async-done | bytes 2359312 | tf_op jit(solution)/shard_map/all_gather | solution.py:797
  228.1 15.2 %all-to-all-done.5 = bf16[8,1024,128]{2,1,0:T(8,128)(2,1)S(1)} async-done(((bf16[8,1024,128]{2,1,0:T(8,128)(2,1)}), bf16[8,1024,128]{2,1,0:T(8,128)(2,1)S(1)}, u32[]{:S(2)}, u32[]{:S(2)}) %all-to-all-start.5) | async-done | bytes 2097184 | tf_op jit(solution)/shard_map/all_to_all | solution.py:726
  244.7 4.8 all-to-all-start.6
  255.0 22.6 %all-to-all-done.6 = bf16[8,288,512]{2,1,0:T(8,128)(2,1)} async-done(((bf16[8,288,512]{2,1,0:T(8,128)(2,1)}), bf16[8,288,512]{2,1,0:T(8,128)(2,1)}, u32[]{:S(2)}, u32[]{:S(2)}) %all-to-all-start.6) | async-done | bytes 2359328 | tf_op jit(solution)/shard_map/all_to_all | solution.py:726
  288.0 22.3 %all-to-all-done.7 = bf16[8,1024,128]{2,1,0:T(8,128)(2,1)S(1)} async-done(((bf16[8,1024,128]{2,1,0:T(8,128)(2,1)}), bf16[8,1024,128]{2,1,0:T(8,128)(2,1)S(1)}, u32[]{:S(2)}, u32[]{:S(2)}) %all-to-all-start.7) | async-done | bytes 2097184 | tf_op jit(solution)/shard_map/all_to_all | solution.py:726
  311.6 6.0 %all-to-all-start.8 = ((bf16[16,144,512]{2,1,0:T(8,128)(2,1)}), bf16[16,144,512]{2,1,0:T(8,128)(2,1)}, u32[]{:S(2)}, u32[]{:S(2)}) async-start(bf16[16,144,512]{2,1,0:T(8,128)(2,1)} %pad_maximum_fusion), calls=%async_computation.8 | async-start | bytes 4718592 | tf_op jit(solution)/shard_map/all_to_all | solution.py:729
  318.3 34.7 %expert.3 = (bf16[2,4,1024,128]{3,2,1,0:T(8,128)(2,1)}, bf16[2,4,1024,128]{3,2,1,0:T(8,128)(2,1)}, bf16[1152,512]{1,0:T(8,128)(2,1)}, bf16[1152,512]{1,0:T(8,128)(2,1)}) custom-call(s32[2]{0:T(128)} %pad_add_fusion.2.where_ref, bf16[1152,512]{1,0:T(8,128)(2,1)} %pad_maximum_fusion.1.refs_0_, bf16[2,1152,512]{2,1,0:T(8,128)(2,1)} %bitcast.117, ...), custom_call_target="tpu_custom_call" | custom-call | flops 24159191040 | bytes 20000000 | tf_op jit(solution)/shard_map/expert/pallas_call | solution.py:444
  353.1 7.2 %all-to-all-done.8 = bf16[16,144,512]{2,1,0:T(8,128)(2,1)} async-done(((bf16[16,144,512]{2,1,0:T(8,128)(2,1)}), bf16[16,144,512]{2,1,0:T(8,128)(2,1)}, u32[]{:S(2)}, u32[]{:S(2)}) %all-to-all-start.8) | async-done | bytes 2359328 | tf_op jit(solution)/shard_map/all_to_all | solution.py:729
  360.3 8.2 %all-to-all-start.9 = ((bf16[8,1024,128]{2,1,0:T(8,128)(2,1)}), bf16[8,1024,128]{2,1,0:T(8,128)(2,1)S(1)}, u32[]{:S(2)}, u32[]{:S(2)}) async-start(bf16[8,1024,128]{2,1,0:T(8,128)(2,1)} %bitcast.99), calls=%async_computation.9 | async-start | bytes 4194304 | tf_op jit(solution)/shard_map/all_to_all | solution.py:726
  377.3 16.4 %all-to-all-done.9 = bf16[8,1024,128]{2,1,0:T(8,128)(2,1)S(1)} async-done(((bf16[8,1024,128]{2,1,0:T(8,128)(2,1)}), bf16[8,1024,128]{2,1,0:T(8,128)(2,1)S(1)}, u32[]{:S(2)}, u32[]{:S(2)}) %all-to-all-start.9) | async-done | bytes 2097184 | tf_op jit(solution)/shard_map/all_to_all | solution.py:726
  393.6 6.3 %all-to-all-start.10 = ((bf16[16,72,512]{2,1,0:T(8,128)(2,1)}), bf16[16,72,512]{2,1,0:T(8,128)(2,1)}, u32[]{:S(2)}, u32[]{:S(2)}) async-start(bf16[16,72,512]{2,1,0:T(8,128)(2,1)} %bitcast.55), calls=%async_computation.10 | async-start | bytes 2359296 | tf_op jit(solution)/shard_map/all_to_all | solution.py:729
  400.5 16.0 %all-to-all-done.10 = bf16[16,72,512]{2,1,0:T(8,128)(2,1)} async-done(((bf16[16,72,512]{2,1,0:T(8,128)(2,1)}), bf16[16,72,512]{2,1,0:T(8,128)(2,1)}, u32[]{:S(2)}, u32[]{:S(2)}) %all-to-all-start.10) | async-done | bytes 1179680 | tf_op jit(solution)/shard_map/all_to_all | solution.py:729
  416.5 7.1 %all-to-all-start.11 = ((bf16[8,1024,128]{2,1,0:T(8,128)(2,1)}), bf16[8,1024,128]{2,1,0:T(8,128)(2,1)S(1)}, u32[]{:S(2)}, u32[]{:S(2)}) async-start(bf16[8,1024,128]{2,1,0:T(8,128)(2,1)} %bitcast.97), calls=%async_computation.11 | async-start | bytes 4194304 | tf_op jit(solution)/shard_map/all_to_all | solution.py:726
  425.6 25.7 %attention_backward.1 = (f32[4,197,512]{2,1,0:T(8,128)}, bf16[8,1056,128]{2,1,0:T(8,128)(2,1)}) custom-call(s32[3]{0:T(128)} %pad_add_fusion.spot_ref.refs_0_, bf16[4,197,512]{2,1,0:T(8,128)(2,1)} %reshape.156.tokens_ref.refs_1_, bf16[4,197,512]{2,1,0:T(8,128)(2,1)} %reshape.193.refs_2_, f32[4,512]{1,0:T(4,128)} %pad_maximum_fusion.7.norms_ref.refs_3_, ...), custom_call_target="tpu_custom_call" | custom-call | flops 8999999488 | bytes 12000000 | tf_op jit(solution)/shard_map/attention_backward/pallas_call | solution.py:660
  456.2 25.3 %all-to-all-done.12 = bf16[8,1056,128]{2,1,0:T(8,128)(2,1)} async-done(((bf16[8,1056,128]{2,1,0:T(8,128)(2,1)}), bf16[8,1056,128]{2,1,0:T(8,128)(2,1)}, u32[]{:S(2)}, u32[]{:S(2)}) %all-to-all-start.12) | async-done | bytes 2162720 | tf_op jit(solution)/shard_map/all_to_all | solution.py:726
  481.6 5.3 all-to-all-start.13
  514.8 10.5 %mix.1 = bf16[4,197,512]{2,1,0:T(8,128)(2,1)} custom-call(f32[4,197,512]{2,1,0:T(8,128)} %get-tuple-element.93.refs_9_.resid_ref, s32[4,197,6]{2,1,0:T(8,128)} %reshape.207.refs_6_.slot_ref, f32[4,197,2]{2,1,0:T(8,128)} %copy.43.gates_ref, bf16[2304,512]{1,0:T(8,128)(2,1)} %bitcast.48.refs_10_.rest_0_, bf16[1152,512]{1,0:T(8,128)(2,1)} %bitcast.101), custom_call_target="tpu_custom_call" | custom-call | flops 6000000000 | bytes 6000000 | tf_op jit(solution)/shard_map/mix/pallas_call | solution.py:529
  527.5 10.0 %collective-permute-done.8 = bf16[1056,128]{1,0:T(8,128)(2,1)S(1)} collective-permute-done((bf16[1056,128]{1,0:T(8,128)(2,1)S(1)}, bf16[1056,128]{1,0:T(8,128)(2,1)S(1)}, u32[]{:S(2)}, u32[]{:S(2)}) %collective-permute-start.8) | collective-permute-done | bytes 270368 | tf_op jit(solution)/shard_map/ppermute | solution.py:735
  537.6 10.1 %collective-permute-done.9 = bf16[1056,128]{1,0:T(8,128)(2,1)S(1)} collective-permute-done((bf16[1056,128]{1,0:T(8,128)(2,1)S(1)}, bf16[1056,128]{1,0:T(8,128)(2,1)S(1)}, u32[]{:S(2)}, u32[]{:S(2)}) %collective-permute-start.9) | collective-permute-done | bytes 270368 | tf_op jit(solution)/shard_map/ppermute | solution.py:735
  (141 shorter events, 123.0 us)
Async XLA Ops:
  8.0 68.8 %all-gather.24.cloned.1.call-start = ((), (), s32[]{:S(2)}) async-start(), calls=%async_computation.19 | async-start | bytes 4136960 | tf_op jit(solution)/shard_map/all_gather | solution.py:751
  11.8 10.4 %collective-permute-start.1 = (bf16[1024,128]{1,0:T(8,128)(2,1)S(1)}, bf16[1024,128]{1,0:T(8,128)(2,1)S(1)}, u32[]{:S(2)}, u32[]{:S(2)}) collective-permute-start(bf16[1024,128]{1,0:T(8,128)(2,1)S(1)} %get-tuple-element.119), channel_id=1, source_target_pairs={{0,4},{1,5},{2,6},{3,7},{4,0},{5,1},{6,2},{7,3},{8,12},{9,13},{10,... | collective-permute-start | bytes 786440 | tf_op jit(solution)/shard_map/ppermute | solution.py:732
  12.4 14.2 %collective-permute-start.2 = (bf16[1024,128]{1,0:T(8,128)(2,1)S(1)}, bf16[1024,128]{1,0:T(8,128)(2,1)S(1)}, u32[]{:S(2)}, u32[]{:S(2)}) collective-permute-start(bf16[1024,128]{1,0:T(8,128)(2,1)S(1)} %get-tuple-element.119), channel_id=1, source_target_pairs={{0,6},{1,7},{2,4},{3,5},{4,2},{5,3},{6,0},{7,1},{8,14},{9,15},{10,... | collective-permute-start | bytes 786440 | tf_op jit(solution)/shard_map/ppermute | solution.py:732
  14.8 13.1 %collective-permute-start = (bf16[1024,128]{1,0:T(8,128)(2,1)S(1)}, bf16[1024,128]{1,0:T(8,128)(2,1)S(1)}, u32[]{:S(2)}, u32[]{:S(2)}) collective-permute-start(bf16[1024,128]{1,0:T(8,128)(2,1)S(1)} %get-tuple-element.119), channel_id=1, source_target_pairs={{0,2},{1,3},{2,0},{3,1},{4,6},{5,7},{6,4},{7,5},{8,10},{9,11},{10,... | collective-permute-start | bytes 786440 | tf_op jit(solution)/shard_map/ppermute | solution.py:732
  28.1 29.4 %all-to-all-start = ((bf16[8,1024,128]{2,1,0:T(8,128)(2,1)}), bf16[8,1024,128]{2,1,0:T(8,128)(2,1)S(1)}, u32[]{:S(2)}, u32[]{:S(2)}) async-start(bf16[8,1024,128]{2,1,0:T(8,128)(2,1)} %get-tuple-element.64), calls=%async_computation | async-start | bytes 4194304 | tf_op jit(solution)/shard_map/all_to_all | solution.py:726
  32.3 9.4 %collective-permute-start.3 = (bf16[4,1024,128]{2,1,0:T(8,128)(2,1)S(1)}, bf16[4,1024,128]{2,1,0:T(8,128)(2,1)}, u32[]{:S(2)}, u32[]{:S(2)}) collective-permute-start(bf16[4,1024,128]{2,1,0:T(8,128)(2,1)S(1)} %pad_maximum_fusion.2.weights_a_ref.refs_4_), channel_id=1, source_target_pairs={{0,1},{1,0},{2,3},{3,2},{4,5},{5,4},{6,7},{7,6},{8,9},{9,8},{10,11... | collective-permute-start | bytes 3145736 | tf_op jit(solution)/shard_map/ppermute | solution.py:732
  58.9 32.0 %all-to-all-start.1 = ((bf16[8,288,512]{2,1,0:T(8,128)(2,1)}), bf16[8,288,512]{2,1,0:T(8,128)(2,1)S(1)}, u32[]{:S(2)}, u32[]{:S(2)}) async-start(bf16[8,288,512]{2,1,0:T(8,128)(2,1)} %bitcast.94), calls=%async_computation.1 | async-start | bytes 4718592 | tf_op jit(solution)/shard_map/all_to_all | solution.py:726
  90.9 35.4 %all-to-all-start.2 = ((bf16[8,1024,128]{2,1,0:T(8,128)(2,1)}), bf16[8,1024,128]{2,1,0:T(8,128)(2,1)}, u32[]{:S(2)}, u32[]{:S(2)}) async-start(bf16[8,1024,128]{2,1,0:T(8,128)(2,1)} %get-tuple-element.70), calls=%async_computation.2 | async-start | bytes 4194304 | tf_op jit(solution)/shard_map/all_to_all | solution.py:726
  96.9 28.1 %collective-permute-start.6 = (bf16[576,512]{1,0:T(8,128)(2,1)S(1)}, bf16[576,512]{1,0:T(8,128)(2,1)S(1)}, u32[]{:S(2)}, u32[]{:S(2)}) collective-permute-start(bf16[576,512]{1,0:T(8,128)(2,1)S(1)} %bitcast.104), channel_id=1, source_target_pairs={{0,16},{8,24},{16,0},{24,8},{1,17},{9,25},{17,1},{25,9},{2,18},{10... | collective-permute-start | bytes 1769480 | tf_op jit(solution)/shard_map/ppermute | solution.py:735
  99.5 26.8 %collective-permute-start.5 = (bf16[576,512]{1,0:T(8,128)(2,1)}, bf16[576,512]{1,0:T(8,128)(2,1)S(1)}, u32[]{:S(2)}, u32[]{:S(2)}) collective-permute-start(bf16[576,512]{1,0:T(8,128)(2,1)} %bitcast.22), channel_id=1, source_target_pairs={{0,8},{8,0},{16,24},{24,16},{1,9},{9,1},{17,25},{25,17},{2,10},{10... | collective-permute-start | bytes 1769480 | tf_op jit(solution)/shard_map/ppermute | solution.py:735
  127.2 32.2 %all-to-all-start.3 = ((bf16[8,288,512]{2,1,0:T(8,128)(2,1)}), bf16[8,288,512]{2,1,0:T(8,128)(2,1)S(1)}, u32[]{:S(2)}, u32[]{:S(2)}) async-start(bf16[8,288,512]{2,1,0:T(8,128)(2,1)} %bitcast.92), calls=%async_computation.3 | async-start | bytes 4718592 | tf_op jit(solution)/shard_map/all_to_all | solution.py:726
  131.4 16.2 %collective-permute-start.4 = (bf16[576,512]{1,0:T(8,128)(2,1)S(1)}, bf16[576,512]{1,0:T(8,128)(2,1)S(1)}, u32[]{:S(2)}, u32[]{:S(2)}) collective-permute-start(bf16[576,512]{1,0:T(8,128)(2,1)S(1)} %bitcast.106), channel_id=1, source_target_pairs={{0,8},{8,0},{16,24},{24,16},{1,9},{9,1},{17,25},{25,17},{2,10},{10... | collective-permute-start | bytes 1769480 | tf_op jit(solution)/shard_map/ppermute | solution.py:735
  133.3 28.1 %collective-permute-start.7 = (bf16[576,512]{1,0:T(8,128)(2,1)}, bf16[576,512]{1,0:T(8,128)(2,1)}, u32[]{:S(2)}, u32[]{:S(2)}) collective-permute-start(bf16[576,512]{1,0:T(8,128)(2,1)} %bitcast.22), channel_id=1, source_target_pairs={{0,24},{8,16},{16,8},{24,0},{1,25},{9,17},{17,9},{25,1},{2,26},{10... | collective-permute-start | bytes 1769480 | tf_op jit(solution)/shard_map/ppermute | solution.py:735
  161.3 52.7 %all-to-all-start.4 = ((bf16[8,2048,128]{2,1,0:T(8,128)(2,1)}), bf16[8,2048,128]{2,1,0:T(8,128)(2,1)}, u32[]{:S(2)}, u32[]{:S(2)}) async-start(bf16[8,2048,128]{2,1,0:T(8,128)(2,1)} %pack_weights.3), calls=%async_computation.4 | async-start | bytes 8388608 | tf_op jit(solution)/shard_map/all_to_all | solution.py:726
  166.3 61.8 %all-gather.14.cloned.1.call-start = ((), (), s32[]{:S(2)}) async-start(), calls=%async_computation.14 | async-start | bytes 3538944 | tf_op jit(solution)/shard_map/all_gather | solution.py:797
  214.1 29.2 %all-to-all-start.5 = ((bf16[8,1024,128]{2,1,0:T(8,128)(2,1)}), bf16[8,1024,128]{2,1,0:T(8,128)(2,1)S(1)}, u32[]{:S(2)}, u32[]{:S(2)}) async-start(bf16[8,1024,128]{2,1,0:T(8,128)(2,1)} %bitcast.100), calls=%async_computation.5 | async-start | bytes 4194304 | tf_op jit(solution)/shard_map/all_to_all | solution.py:726
  244.7 32.9 %all-to-all-start.6 = ((bf16[8,288,512]{2,1,0:T(8,128)(2,1)}), bf16[8,288,512]{2,1,0:T(8,128)(2,1)}, u32[]{:S(2)}, u32[]{:S(2)}) async-start(bf16[8,288,512]{2,1,0:T(8,128)(2,1)} %bitcast.91), calls=%async_computation.6 | async-start | bytes 4718592 | tf_op jit(solution)/shard_map/all_to_all | solution.py:726
  249.5 123.6 %all-gather.18.cloned.1.call-start = ((), (), s32[]{:S(2)}) async-start(), calls=%async_computation.16 | async-start | bytes 6291456 | tf_op jit(solution)/shard_map/all_gather | solution.py:738
  280.9 29.4 %all-to-all-start.7 = ((bf16[8,1024,128]{2,1,0:T(8,128)(2,1)}), bf16[8,1024,128]{2,1,0:T(8,128)(2,1)S(1)}, u32[]{:S(2)}, u32[]{:S(2)}) async-start(bf16[8,1024,128]{2,1,0:T(8,128)(2,1)} %bitcast.98), calls=%async_computation.7 | async-start | bytes 4194304 | tf_op jit(solution)/shard_map/all_to_all | solution.py:726
  311.6 48.6 %all-to-all-start.8 = ((bf16[16,144,512]{2,1,0:T(8,128)(2,1)}), bf16[16,144,512]{2,1,0:T(8,128)(2,1)}, u32[]{:S(2)}, u32[]{:S(2)}) async-start(bf16[16,144,512]{2,1,0:T(8,128)(2,1)} %pad_maximum_fusion), calls=%async_computation.8 | async-start | bytes 4718592 | tf_op jit(solution)/shard_map/all_to_all | solution.py:729
  317.6 171.6 %all-gather.20.cloned.1.call-start = ((), (), s32[]{:S(2)}) async-start(), calls=%async_computation.17 | async-start | bytes 6291456 | tf_op jit(solution)/shard_map/all_gather | solution.py:738
  360.3 33.4 %all-to-all-start.9 = ((bf16[8,1024,128]{2,1,0:T(8,128)(2,1)}), bf16[8,1024,128]{2,1,0:T(8,128)(2,1)S(1)}, u32[]{:S(2)}, u32[]{:S(2)}) async-start(bf16[8,1024,128]{2,1,0:T(8,128)(2,1)} %bitcast.99), calls=%async_computation.9 | async-start | bytes 4194304 | tf_op jit(solution)/shard_map/all_to_all | solution.py:726
  393.6 22.9 %all-to-all-start.10 = ((bf16[16,72,512]{2,1,0:T(8,128)(2,1)}), bf16[16,72,512]{2,1,0:T(8,128)(2,1)}, u32[]{:S(2)}, u32[]{:S(2)}) async-start(bf16[16,72,512]{2,1,0:T(8,128)(2,1)} %bitcast.55), calls=%async_computation.10 | async-start | bytes 2359296 | tf_op jit(solution)/shard_map/all_to_all | solution.py:729
  399.9 103.0 %all-gather.16.cloned.1.call-start = ((), (), s32[]{:S(2)}) async-start(), calls=%async_computation.15 | async-start | bytes 6291456 | tf_op jit(solution)/shard_map/all_gather | solution.py:738
  416.5 34.7 %all-to-all-start.11 = ((bf16[8,1024,128]{2,1,0:T(8,128)(2,1)}), bf16[8,1024,128]{2,1,0:T(8,128)(2,1)S(1)}, u32[]{:S(2)}, u32[]{:S(2)}) async-start(bf16[8,1024,128]{2,1,0:T(8,128)(2,1)} %bitcast.97), calls=%async_computation.11 | async-start | bytes 4194304 | tf_op jit(solution)/shard_map/all_to_all | solution.py:726
  451.3 30.3 %all-to-all-start.12 = ((bf16[8,1056,128]{2,1,0:T(8,128)(2,1)}), bf16[8,1056,128]{2,1,0:T(8,128)(2,1)}, u32[]{:S(2)}, u32[]{:S(2)}) async-start(bf16[8,1056,128]{2,1,0:T(8,128)(2,1)} %get-tuple-element.99), calls=%async_computation.12 | async-start | bytes 4325376 | tf_op jit(solution)/shard_map/all_to_all | solution.py:726
  455.6 31.3 %copy-start.16 = (f32[788,2]{0,1:T(2,128)S(1)}, f32[788,2]{0,1:T(2,128)}, u32[]{:S(2)}) copy-start(f32[788,2]{0,1:T(2,128)} %param.14) | copy-start | bytes 18916
  455.7 94.2 %all-gather.22.cloned.1.call-start = ((), (), s32[]{:S(2)}) async-start(), calls=%async_computation.18 | async-start | bytes 6291456 | tf_op jit(solution)/shard_map/all_gather | solution.py:738
  481.6 32.2 %all-to-all-start.13 = ((bf16[16,72,512]{2,1,0:T(8,128)(2,1)}), bf16[16,72,512]{2,1,0:T(8,128)(2,1)S(1)}, u32[]{:S(2)}, u32[]{:S(2)}) async-start(bf16[16,72,512]{2,1,0:T(8,128)(2,1)} %bitcast.59), calls=%async_computation.13 | async-start | bytes 2359296 | tf_op jit(solution)/shard_map/all_to_all | solution.py:729
  509.1 18.5 %collective-permute-start.10 = (bf16[1056,128]{1,0:T(8,128)(2,1)S(1)}, bf16[1056,128]{1,0:T(8,128)(2,1)S(1)}, u32[]{:S(2)}, u32[]{:S(2)}) collective-permute-start(bf16[1056,128]{1,0:T(8,128)(2,1)S(1)} %pad_maximum_fusion.3), channel_id=1, source_target_pairs={{0,24},{8,16},{16,8},{24,0},{1,25},{9,17},{17,9},{25,1},{2,26},{10... | collective-permute-start | bytes 811016 | tf_op jit(solution)/shard_map/ppermute | solution.py:735
  509.2 28.4 %collective-permute-start.8 = (bf16[1056,128]{1,0:T(8,128)(2,1)S(1)}, bf16[1056,128]{1,0:T(8,128)(2,1)S(1)}, u32[]{:S(2)}, u32[]{:S(2)}) collective-permute-start(bf16[1056,128]{1,0:T(8,128)(2,1)S(1)} %pad_maximum_fusion.3), channel_id=1, source_target_pairs={{0,8},{8,0},{16,24},{24,16},{1,9},{9,1},{17,25},{25,17},{2,10},{10... | collective-permute-start | bytes 811016 | tf_op jit(solution)/shard_map/ppermute | solution.py:735
  509.8 37.9 %collective-permute-start.9 = (bf16[1056,128]{1,0:T(8,128)(2,1)S(1)}, bf16[1056,128]{1,0:T(8,128)(2,1)S(1)}, u32[]{:S(2)}, u32[]{:S(2)}) collective-permute-start(bf16[1056,128]{1,0:T(8,128)(2,1)S(1)} %pad_maximum_fusion.3), channel_id=1, source_target_pairs={{0,16},{8,24},{16,0},{24,8},{1,17},{9,25},{17,1},{25,9},{2,18},{10... | collective-permute-start | bytes 811016 | tf_op jit(solution)/shard_map/ppermute | solution.py:735
  (22 other events, 145.8 us)
Sparse Core Ops, SparseCore 0:
  11.8 64.9 all-gather.23
  251.8 56.4 all-gather.17
  320.0 70.4 all-gather.19
  402.0 57.5 all-gather.15
  461.0 83.8 all-gather.21
Sparse Core Ops, SparseCore 1:
  168.3 59.7 all-gather.13

commit v3 on v2

--- a/solution.py
+++ b/solution.py
@@ -120,7 +120,7 @@
     )(own, routes, routes.T)
 
 
-def grad_slots_kernel(plane, own_ref, sent_ref, *gd_refs):
+def grad_slots_kernel(plane, group, own_ref, sent_ref, gd_ref):
     rows = sent_ref.shape[1] - 2 * HEADER
     features = sent_ref.shape[2]
     header = jnp.concatenate(
@@ -136,22 +136,18 @@
     ]
     hot = [(ids_t == routes[k]).astype(f32) for k in range(TOP)]
     count = dot(sum(hot).astype(bf16), one_hot(before < after))
-    slots = []
+    per = plane * SLOTS
+    place = lax.broadcasted_iota(jnp.int32, (per, rows), 0)
+    here = []
     for k in range(TOP):
         rank = jnp.sum(hot[k] * count, axis=0, keepdims=True).astype(jnp.int32)
-        q = routes[k] // plane
-        slot = ((q // 2) * plane + routes[k] % plane) * SLOTS + rank
-        slots.append(jnp.where(q % 2 == own_ref[0], slot, -1))
-    cot = sent_ref[0, 2 * HEADER :, :]
-    per = plane * SLOTS
-    for g, gd_ref in enumerate(gd_refs):
-        place = lax.broadcasted_iota(jnp.int32, (per, rows), 0) + g * per
-        here = [place == slot for slot in slots]
-        gate = sum(jnp.where(here[k], gates[k], 0.0) for k in range(TOP))
-        picked = dot(one_hot(here[0] | here[1]), cot)
-        weighed = jnp.sum(gate, axis=1, keepdims=True) * picked
-        for p in range(plane):
-            gd_ref[p, 0] = weighed[p * SLOTS : (p + 1) * SLOTS, :].astype(bf16)
+        mine = routes[k] // plane == 2 * group + own_ref[0]
+        here.append(place == jnp.where(mine, routes[k] % plane * SLOTS + rank, -1))
+    gate = sum(jnp.where(here[k], gates[k], 0.0) for k in range(TOP))
+    picked = dot(one_hot(here[0] | here[1]), sent_ref[0, 2 * HEADER :, :])
+    weighed = jnp.sum(gate, axis=1, keepdims=True) * picked
+    for p in range(plane):
+        gd_ref[p, 0] = weighed[p * SLOTS : (p + 1) * SLOTS, :].astype(bf16)
 
 
 HEADER = 8
@@ -167,21 +163,18 @@
     return jnp.concatenate([lines[:, :features], lines[:, features:], cot], axis=0)
 
 
-def grad_slots(own, sent, plane, groups):
+def grad_slots(own, sent, plane, group):
     chunks, rows, features = sent.shape
     shape = (plane, chunks, SLOTS, features)
     return pl.pallas_call(
-        functools.partial(grad_slots_kernel, plane),
+        functools.partial(grad_slots_kernel, plane, group),
         grid_spec=pltpu.PrefetchScalarGridSpec(
             num_scalar_prefetch=1,
             grid=(chunks,),
             in_specs=[pl.BlockSpec((1, rows, features), lambda i, own: (own[1] ^ i, 0, 0))],
-            out_specs=[
-                pl.BlockSpec((plane, 1, SLOTS, features), lambda i, own: (0, i, 0, 0))
-            ]
-            * groups,
+            out_specs=pl.BlockSpec((plane, 1, SLOTS, features), lambda i, own: (0, i, 0, 0)),
         ),
-        out_shape=[jax.ShapeDtypeStruct(shape, bf16)] * groups,
+        out_shape=jax.ShapeDtypeStruct(shape, bf16),
         compiler_params=pltpu.CompilerParams(vmem_limit_bytes=VMEM_LIMIT),
         cost_estimate=pl.CostEstimate(flops=8_000_000_000, bytes_accessed=10_000_000, transcendentals=0),
         name="grad_slots",
@@ -780,12 +773,12 @@
             planes * plane * SLOTS, features
         )
 
-    gd_sent = grad_slots(own_and_plane, sent_all, plane, groups)
-    first_in = in_plane(after(packed[0][0], same_core))
+    gd_sent = [grad_slots(own_and_plane, sent_all, plane, g) for g in range(groups)]
+    first_in = in_plane(packed[0][0])
     moved = in_plane(after(x, first_in).reshape(plane, -1, features))
-    first_out = in_plane(after(packed[0][1], (moved, gd_sent)))
     mine, other = quarter(moved, 0), quarter(moved, groups)
     nearest, far_mine = along(other, 1), along(mine, 2)
+    first_out = in_plane(after(packed[0][1], (moved, gd_sent[0])))
     xs = [[mine, nearest, far_mine, along(other, 3)]]
     gd_parts = [v.reshape(plane, planes * SLOTS, features) for v in gd_sent]
     gds = [by_plane(in_plane(after(gd_parts[0], (first_out, nearest, far_mine, packed[1:]))))]
@@ -815,13 +808,14 @@
         return values
 
     held = (first_in, first_out)
-    before = (gds[0], xs[0], nears)
+    before = (gds[0], first_out, xs[0], nears)
     grads, swaps, gx_back, y_back = [], [], [], []
+    last = groups - 1
     for g in range(groups):
         grad, gx, y = expert(far_and_own, xs[g], gds[g], held, wide, narrow, deep, hidden)
         grads.append([])
         swaps.append([])
-        if g < groups - 1:
+        if g < last:
             held = tuple(in_plane(after(v, before)) for v in packed[g + 1])
             grads[g].append(in_plane(after(grad[0], held)))
             swaps[g].append(with_near(grads[g][0]))
@@ -839,18 +833,17 @@
             if g:
                 put(1, g - 1, True, ())
                 put(0, g - 1, False, ())
-            before = to_tokens([after_blocks(gx)], grads[g][0])
+            before = to_tokens([after_blocks(gx)], grads[g][-1])
             gx_back.append(before)
             grads[g].append(in_plane(after(grad[1], before)))
             before = grads[g][1]
             last_y = y
 
-    last = groups - 1
     grad_input, grads_w = attention_back(
         spot, tokens3, cot3, norms, weights, slots3, proj, att, resid, gx_back, wide, narrow
     )
     count = grads_w.shape[1] - 2 * TAIL
-    swaps[last].append(with_near(after(grads[last][1], grads_w)))
+    swaps[last].append(with_near(grads[last][1]))
     grads_w = in_plane(after(grads_w, before))
     y_back.append(to_tokens([last_y], grads_w))
     for g in range(last):
@@ -861,16 +854,26 @@
     mixed = mix(after_blocks(resid), slots3, gates3, y_back).reshape(rows, features)
     put(1, last, False, mixed)
     (out_in,), (out_out,) = out_blocks
-    summed = jnp.sum(grads_w.astype(f32), axis=0)
-    tail = summed[count : count + TAIL] + summed[count + TAIL :]
-    high = lax.reduce_precision(tail, 8, 7)
-    block = jnp.concatenate(
-        [summed[:count].astype(bf16), high.astype(bf16), (tail - high).astype(bf16)], axis=0
-    )
-    terms = after([block] + [along(block, k) for k in range(1, planes)], mixed)
-    terms = [v.astype(f32) for v in terms]
-    block = (terms[0] + terms[1]) + (terms[2] + terms[3])
-    grads_n = (block[count : count + TAIL] + block[count + TAIL :]).reshape(4, features)
+
+    def low_rows(values):
+        tail = values[count : count + TAIL]
+        high = lax.reduce_precision(tail, 8, 7)
+        rest = lax.reduce_precision(tail - high, 8, 7)
+        kept = lax.reduce_precision(values[:count], 8, 7)
+        return jnp.concatenate([kept, high, rest], axis=0).astype(bf16)
+
+    def both_parts(values):
+        values = values.astype(f32)
+        return jnp.concatenate(
+            [values[:count], values[count : count + TAIL] + values[count + TAIL :]], axis=0
+        )
+
+    block = low_rows(both_parts(jnp.sum(grads_w.astype(f32), axis=0)))
+    for k in (1, 2):
+        block = both_parts(block) + both_parts(along(block, k))
+        block = low_rows(block) if k == 1 else block
+    block = after(block, mixed)
+    grads_n = block[count:].reshape(4, features)
     grad_qkv = block[: 3 * qkv_deep].reshape(3, qkv_deep, LANES)
     grad_attn_out = jnp.concatenate(
         [

time: 572 us -> 566 us (0.990)
  the two profiles are of different devices: /device:TPU:10 before, /device:TPU:0 now
where the time goes in v3:
time: 566 us; the launch traced here: 556 us
  waiting for transfers between devices  240 us (42%)
  Pallas kernels  189 us (33%)
  starting transfers between devices  70.1 us (12%)
  local copies, waits for them, and re-layouts  24.7 us (4%)
  other arithmetic  16.6 us (3%)
  between operations  16.2 us (3%)
    all_to_all x11, waiting for transfers between devices, in_plane(): return lax.all_to_all(values, ('wide', 'narrow'), 0, 0, tiled=True)  124 us
    pallas_call x2, Pallas kernels, expert(): pl.pallas_call(functools.partial(expert_kernel, deep, hidden, len(xs), ti...  69.4 us
    ppermute x6, waiting for transfers between devices, along(): lax.ppermute(values, ('pair', 'parity'), [(i, i ^ k) for i in range(plane...  55.9 us
    all_to_all x11, starting transfers between devices, in_plane(): return lax.all_to_all(values, ('wide', 'narrow'), 0, 0, tiled=True)  44.4 us
    pallas_call x8, Pallas kernels, place(): pl.pallas_call(place_kernel, grid_spec=pltpu.PrefetchScalarGridSpec(num_s...  33 us
    all_to_all x3, waiting for transfers between devices, in_pair(): lax.all_to_all(values, ('parity', 'wide', 'narrow'), 0, 0, tiled=True)  31.3 us
    pallas_call x1, Pallas kernels, attention_back(): pl.pallas_call(functools.partial(backward_kernel, wide, narrow, len(backs...  25.7 us
    all_gather x1, waiting for transfers between devices, owned_on_device(): lax.all_gather(with_header(routes, gates, grad_out), ('pair', 'parity'),...  19.3 us
  transfers between devices with their start and end apart: 30, of which 18 were waited for; matrix products, arithmetic and copies ran while one was open for 6% of the time, Pallas kernels for 33%

profile of v3, /device:TPU:0, one launch (start us, length us, event | category | flops | bytes accessed | tf_op | source)
XLA Modules:
  0.0 556.3 jit_solution(9091068490912922066)
XLA Ops:
  16.3 6.9 %pack_weights.2 = (bf16[8,1024,128]{2,1,0:T(8,128)(2,1)}, bf16[8,1024,128]{2,1,0:T(8,128)(2,1)}) custom-call(s32[1]{0:T(128)} %bitcast.17.first_ref, bf16[32,256,512]{2,1,0:T(8,128)(2,1)} %w_in_ref.3, bf16[32,512,256]{2,1,0:T(8,128)(2,1)} %w_out_ref.3), custom_call_target="tpu_custom_call" | custom-call | bytes 9000000 | tf_op jit(solution)/shard_map/pack_weights/pallas_call | solution.py:327
  23.2 4.3 all-to-all-start
  40.8 15.1 %attention_forward.1 = (bf16[4,197,1536]{2,1,0:T(8,128)(2,1)}, bf16[4,197,512]{2,1,0:T(8,128)(2,1)}, f32[4,197,512]{2,1,0:T(8,128)}, bf16[2304,512]{1,0:T(8,128)(2,1)}) custom-call(s32[3]{0:T(128)} %pad_add_fusion.spot_ref.refs_0_, bf16[4,197,512]{2,1,0:T(8,128)(2,1)} %reshape.156.tokens_ref.refs_1_, f32[4,512]{1,0:T(4,128)} %pad_maximum_fusion.8.norms_ref.refs_3_, ...), custom_call_target="tpu_custom_call" | custom-call | flops 6000000000 | bytes 9000000 | tf_op jit(solution)/shard_map/attention_forward/pallas_call | solution.py:283
  61.5 19.3 %all-gather.24.cloned.1.call-done.sent_ref = bf16[4,804,512]{2,1,0:T(8,128)(2,1)} async-done(((bf16[1,804,512]{2,1,0:T(8,128)(2,1)}), bf16[4,804,512]{2,1,0:T(8,128)(2,1)}) %all-gather.24.cloned.1.call-update) | async-done | bytes 3293200 | tf_op jit(solution)/shard_map/all_gather | solution.py:744
  80.8 9.2 %grad_slots.3 = bf16[8,4,72,512]{3,2,1,0:T(8,128)(2,1)} custom-call(s32[2]{0:T(128)} %pad_add_fusion.3.own_ref, bf16[4,804,512]{2,1,0:T(8,128)(2,1)} %all-gather.24.cloned.1.call-done.sent_ref), custom_call_target="tpu_custom_call" | custom-call | flops 8000000000 | bytes 10000000 | tf_op jit(solution)/shard_map/grad_slots/pallas_call | solution.py:169
  90.0 4.4 all-to-all-start.2
  99.0 6.7 %pack_weights.3 = bf16[8,2048,128]{2,1,0:T(8,128)(2,1)} custom-call(s32[1]{0:T(128)} %bitcast.32.first_ref, bf16[32,256,512]{2,1,0:T(8,128)(2,1)} %w_in_ref.3, bf16[32,512,256]{2,1,0:T(8,128)(2,1)} %w_out_ref.3), custom_call_target="tpu_custom_call" | custom-call | bytes 9000000 | tf_op jit(solution)/shard_map/pack_weights/pallas_call | solution.py:327
  105.8 19.0 %collective-permute-done.6.refs_2_ = bf16[576,512]{1,0:T(8,128)(2,1)S(1)} collective-permute-done((bf16[576,512]{1,0:T(8,128)(2,1)S(1)}, bf16[576,512]{1,0:T(8,128)(2,1)S(1)}, u32[]{:S(2)}, u32[]{:S(2)}) %collective-permute-start.6) | collective-permute-done | bytes 589856 | tf_op jit(solution)/shard_map/ppermute | solution.py:728
  132.6 13.1 %collective-permute-done.4 = bf16[576,512]{1,0:T(8,128)(2,1)S(1)} collective-permute-done((bf16[576,512]{1,0:T(8,128)(2,1)S(1)}, bf16[576,512]{1,0:T(8,128)(2,1)S(1)}, u32[]{:S(2)}, u32[]{:S(2)}) %collective-permute-start.4) | collective-permute-done | bytes 589856 | tf_op jit(solution)/shard_map/ppermute | solution.py:728
  146.8 11.7 %all-to-all-done.3 = bf16[8,288,512]{2,1,0:T(8,128)(2,1)S(1)} async-done(((bf16[8,288,512]{2,1,0:T(8,128)(2,1)}), bf16[8,288,512]{2,1,0:T(8,128)(2,1)S(1)}, u32[]{:S(2)}, u32[]{:S(2)}) %all-to-all-start.3) | async-done | bytes 2359328 | tf_op jit(solution)/shard_map/all_to_all | solution.py:719
  160.1 4.6 all-to-all-start.4
  165.5 34.7 %expert.2 = (bf16[2,4,1024,128]{3,2,1,0:T(8,128)(2,1)}, bf16[2,4,1024,128]{3,2,1,0:T(8,128)(2,1)}, bf16[1152,512]{1,0:T(8,128)(2,1)}, bf16[1152,512]{1,0:T(8,128)(2,1)}) custom-call(s32[2]{0:T(128)} %pad_add_fusion.2.where_ref, bf16[576,512]{1,0:T(8,128)(2,1)} %bitcast.104, bf16[576,512]{1,0:T(8,128)(2,1)} %copy-done.24, bf16[576,512]{1,0:T(8,128)(2,1)} %copy-done.23, ...), custom_call_target="tpu_custom_call" | custom-call | flops 24159191040 | bytes 20000000 | tf_op jit(solution)/shard_map/expert/pallas_call | solution.py:437
  200.2 12.6 %all-to-all-done.4 = bf16[8,2048,128]{2,1,0:T(8,128)(2,1)} async-done(((bf16[8,2048,128]{2,1,0:T(8,128)(2,1)}), bf16[8,2048,128]{2,1,0:T(8,128)(2,1)}, u32[]{:S(2)}, u32[]{:S(2)}) %all-to-all-start.4) | async-done | bytes 4194336 | tf_op jit(solution)/shard_map/all_to_all | solution.py:719
  216.4 9.2 %grad_slots.2 = bf16[8,4,72,512]{3,2,1,0:T(8,128)(2,1)} custom-call(s32[2]{0:T(128)} %pad_add_fusion.3.own_ref, bf16[4,804,512]{2,1,0:T(8,128)(2,1)} %all-gather.24.cloned.1.call-done.sent_ref), custom_call_target="tpu_custom_call" | custom-call | flops 8000000000 | bytes 10000000 | tf_op jit(solution)/shard_map/grad_slots/pallas_call | solution.py:169
  225.6 4.7 all-gather.14.cloned.1.call-done
  230.3 11.7 %all-to-all-done.5 = bf16[8,1024,128]{2,1,0:T(8,128)(2,1)S(1)} async-done(((bf16[8,1024,128]{2,1,0:T(8,128)(2,1)}), bf16[8,1024,128]{2,1,0:T(8,128)(2,1)S(1)}, u32[]{:S(2)}, u32[]{:S(2)}) %all-to-all-start.5) | async-done | bytes 2097184 | tf_op jit(solution)/shard_map/all_to_all | solution.py:719
  243.4 4.4 all-to-all-start.6
  253.3 23.0 %all-to-all-done.6 = bf16[8,288,512]{2,1,0:T(8,128)(2,1)} async-done(((bf16[8,288,512]{2,1,0:T(8,128)(2,1)}), bf16[8,288,512]{2,1,0:T(8,128)(2,1)}, u32[]{:S(2)}, u32[]{:S(2)}) %all-to-all-start.6) | async-done | bytes 2359328 | tf_op jit(solution)/shard_map/all_to_all | solution.py:719
  286.3 22.7 %all-to-all-done.7 = bf16[8,1024,128]{2,1,0:T(8,128)(2,1)S(1)} async-done(((bf16[8,1024,128]{2,1,0:T(8,128)(2,1)}), bf16[8,1024,128]{2,1,0:T(8,128)(2,1)S(1)}, u32[]{:S(2)}, u32[]{:S(2)}) %all-to-all-start.7) | async-done | bytes 2097184 | tf_op jit(solution)/shard_map/all_to_all | solution.py:719
  310.4 4.5 all-to-all-start.8
  315.6 34.7 %expert.3 = (bf16[2,4,1024,128]{3,2,1,0:T(8,128)(2,1)}, bf16[2,4,1024,128]{3,2,1,0:T(8,128)(2,1)}, bf16[1152,512]{1,0:T(8,128)(2,1)}, bf16[1152,512]{1,0:T(8,128)(2,1)}) custom-call(s32[2]{0:T(128)} %pad_add_fusion.2.where_ref, bf16[1152,512]{1,0:T(8,128)(2,1)} %pad_maximum_fusion.1.refs_0_, bf16[2,1152,512]{2,1,0:T(8,128)(2,1)} %bitcast.116, ...), custom_call_target="tpu_custom_call" | custom-call | flops 24159191040 | bytes 20000000 | tf_op jit(solution)/shard_map/expert/pallas_call | solution.py:437
  350.4 12.0 %all-to-all-done.8 = bf16[16,144,512]{2,1,0:T(8,128)(2,1)} async-done(((bf16[16,144,512]{2,1,0:T(8,128)(2,1)}), bf16[16,144,512]{2,1,0:T(8,128)(2,1)}, u32[]{:S(2)}, u32[]{:S(2)}) %all-to-all-start.8) | async-done | bytes 2359328 | tf_op jit(solution)/shard_map/all_to_all | solution.py:722
  374.8 16.8 %all-to-all-done.9 = bf16[8,1024,128]{2,1,0:T(8,128)(2,1)S(1)} async-done(((bf16[8,1024,128]{2,1,0:T(8,128)(2,1)}), bf16[8,1024,128]{2,1,0:T(8,128)(2,1)S(1)}, u32[]{:S(2)}, u32[]{:S(2)}) %all-to-all-start.9) | async-done | bytes 2097184 | tf_op jit(solution)/shard_map/all_to_all | solution.py:719
  391.6 4.4 all-to-all-start.10
  396.6 19.3 %all-to-all-done.10 = bf16[16,72,512]{2,1,0:T(8,128)(2,1)} async-done(((bf16[16,72,512]{2,1,0:T(8,128)(2,1)}), bf16[16,72,512]{2,1,0:T(8,128)(2,1)}, u32[]{:S(2)}, u32[]{:S(2)}) %all-to-all-start.10) | async-done | bytes 1179680 | tf_op jit(solution)/shard_map/all_to_all | solution.py:722
  421.8 25.7 %attention_backward.1 = (f32[4,197,512]{2,1,0:T(8,128)}, bf16[8,1056,128]{2,1,0:T(8,128)(2,1)}) custom-call(s32[3]{0:T(128)} %pad_add_fusion.spot_ref.refs_0_, bf16[4,197,512]{2,1,0:T(8,128)(2,1)} %reshape.156.tokens_ref.refs_1_, bf16[4,197,512]{2,1,0:T(8,128)(2,1)} %reshape.193.refs_2_, f32[4,512]{1,0:T(4,128)} %pad_maximum_fusion.8.norms_ref.refs_3_, ...), custom_call_target="tpu_custom_call" | custom-call | flops 8999999488 | bytes 12000000 | tf_op jit(solution)/shard_map/attention_backward/pallas_call | solution.py:653
  447.5 4.4 all-to-all-start.12
  452.4 25.8 %all-to-all-done.12 = bf16[8,1056,128]{2,1,0:T(8,128)(2,1)} async-done(((bf16[8,1056,128]{2,1,0:T(8,128)(2,1)}), bf16[8,1056,128]{2,1,0:T(8,128)(2,1)}, u32[]{:S(2)}, u32[]{:S(2)}) %all-to-all-start.12) | async-done | bytes 2162720 | tf_op jit(solution)/shard_map/all_to_all | solution.py:719
  481.2 4.4 all-to-all-start.13
  485.6 9.8 %collective-permute-done.8 = bf16[1056,128]{1,0:T(8,128)(2,1)S(1)} collective-permute-done((bf16[1056,128]{1,0:T(8,128)(2,1)S(1)}, bf16[1056,128]{1,0:T(8,128)(2,1)S(1)}, u32[]{:S(2)}, u32[]{:S(2)}) %collective-permute-start.8) | collective-permute-done | bytes 270368 | tf_op jit(solution)/shard_map/ppermute | solution.py:728
  516.1 13.6 %collective-permute-done.9 = bf16[1056,128]{1,0:T(8,128)(2,1)S(1)} collective-permute-done((bf16[1056,128]{1,0:T(8,128)(2,1)S(1)}, bf16[1056,128]{1,0:T(8,128)(2,1)S(1)}, u32[]{:S(2)}, u32[]{:S(2)}) %collective-permute-start.9) | collective-permute-done | bytes 270368 | tf_op jit(solution)/shard_map/ppermute | solution.py:728
  529.8 10.5 %mix.1 = bf16[4,197,512]{2,1,0:T(8,128)(2,1)} custom-call(f32[4,197,512]{2,1,0:T(8,128)} %get-tuple-element.83.refs_9_.resid_ref, s32[4,197,6]{2,1,0:T(8,128)} %reshape.207.refs_6_.slot_ref, f32[4,197,2]{2,1,0:T(8,128)} %copy.43.gates_ref, bf16[2304,512]{1,0:T(8,128)(2,1)} %bitcast.48.refs_10_.rest_0_, bf16[1152,512]{1,0:T(8,128)(2,1)} %bitcast.60.rest_1_), custom_call_target="tpu_custom_call" | custom-call | flops 6000000000 | bytes 6000000 | tf_op jit(solution)/shard_map/mix/pallas_call | solution.py:522
  (158 shorter events, 117.0 us)
Async XLA Ops:
  8.0 72.7 %all-gather.24.cloned.1.call-start = ((), (), s32[]{:S(2)}) async-start(), calls=%async_computation.19 | async-start | bytes 4136960 | tf_op jit(solution)/shard_map/all_gather | solution.py:744
  11.8 15.8 %collective-permute-start.1 = (bf16[1024,128]{1,0:T(8,128)(2,1)S(1)}, bf16[1024,128]{1,0:T(8,128)(2,1)S(1)}, u32[]{:S(2)}, u32[]{:S(2)}) collective-permute-start(bf16[1024,128]{1,0:T(8,128)(2,1)S(1)} %get-tuple-element.115), channel_id=1, source_target_pairs={{0,4},{1,5},{2,6},{3,7},{4,0},{5,1},{6,2},{7,3},{8,12},{9,13},{10,... | collective-permute-start | bytes 786440 | tf_op jit(solution)/shard_map/ppermute | solution.py:725
  14.8 13.2 %collective-permute-start.2 = (bf16[1024,128]{1,0:T(8,128)(2,1)S(1)}, bf16[1024,128]{1,0:T(8,128)(2,1)S(1)}, u32[]{:S(2)}, u32[]{:S(2)}) collective-permute-start(bf16[1024,128]{1,0:T(8,128)(2,1)S(1)} %get-tuple-element.115), channel_id=1, source_target_pairs={{0,6},{1,7},{2,4},{3,5},{4,2},{5,3},{6,0},{7,1},{8,14},{9,15},{10,... | collective-permute-start | bytes 786440 | tf_op jit(solution)/shard_map/ppermute | solution.py:725
  16.3 13.1 %collective-permute-start = (bf16[1024,128]{1,0:T(8,128)(2,1)S(1)}, bf16[1024,128]{1,0:T(8,128)(2,1)S(1)}, u32[]{:S(2)}, u32[]{:S(2)}) collective-permute-start(bf16[1024,128]{1,0:T(8,128)(2,1)S(1)} %get-tuple-element.115), channel_id=1, source_target_pairs={{0,2},{1,3},{2,0},{3,1},{4,6},{5,7},{6,4},{7,5},{8,10},{9,11},{10,... | collective-permute-start | bytes 786440 | tf_op jit(solution)/shard_map/ppermute | solution.py:725
  23.2 32.7 %all-to-all-start = ((bf16[8,1024,128]{2,1,0:T(8,128)(2,1)}), bf16[8,1024,128]{2,1,0:T(8,128)(2,1)S(1)}, u32[]{:S(2)}, u32[]{:S(2)}) async-start(bf16[8,1024,128]{2,1,0:T(8,128)(2,1)} %get-tuple-element.56), calls=%async_computation | async-start | bytes 4194304 | tf_op jit(solution)/shard_map/all_to_all | solution.py:719
  27.5 12.6 %copy-start.19 = (f32[512]{0:T(512)S(1)}, f32[512]{0:T(512)}, u32[]{:S(2)}) copy-start(f32[512]{0:T(512)} %param.19) | copy-start | bytes 6148
  31.3 9.4 %collective-permute-start.3 = (bf16[4,1024,128]{2,1,0:T(8,128)(2,1)S(1)}, bf16[4,1024,128]{2,1,0:T(8,128)(2,1)}, u32[]{:S(2)}, u32[]{:S(2)}) collective-permute-start(bf16[4,1024,128]{2,1,0:T(8,128)(2,1)S(1)} %pad_maximum_fusion.2.weights_a_ref.refs_4_), channel_id=1, source_target_pairs={{0,1},{1,0},{2,3},{3,2},{4,5},{5,4},{6,7},{7,6},{8,9},{9,8},{10,11... | collective-permute-start | bytes 3145736 | tf_op jit(solution)/shard_map/ppermute | solution.py:725
  57.2 32.7 %all-to-all-start.1 = ((bf16[8,288,512]{2,1,0:T(8,128)(2,1)}), bf16[8,288,512]{2,1,0:T(8,128)(2,1)S(1)}, u32[]{:S(2)}, u32[]{:S(2)}) async-start(bf16[8,288,512]{2,1,0:T(8,128)(2,1)} %bitcast.93), calls=%async_computation.1 | async-start | bytes 4718592 | tf_op jit(solution)/shard_map/all_to_all | solution.py:719
  90.0 35.3 %all-to-all-start.2 = ((bf16[8,1024,128]{2,1,0:T(8,128)(2,1)}), bf16[8,1024,128]{2,1,0:T(8,128)(2,1)}, u32[]{:S(2)}, u32[]{:S(2)}) async-start(bf16[8,1024,128]{2,1,0:T(8,128)(2,1)} %get-tuple-element.60), calls=%async_computation.2 | async-start | bytes 4194304 | tf_op jit(solution)/shard_map/all_to_all | solution.py:719
  95.6 29.3 %collective-permute-start.6 = (bf16[576,512]{1,0:T(8,128)(2,1)S(1)}, bf16[576,512]{1,0:T(8,128)(2,1)S(1)}, u32[]{:S(2)}, u32[]{:S(2)}) collective-permute-start(bf16[576,512]{1,0:T(8,128)(2,1)S(1)} %bitcast.103), channel_id=1, source_target_pairs={{0,16},{8,24},{16,0},{24,8},{1,17},{9,25},{17,1},{25,9},{2,18},{10... | collective-permute-start | bytes 1769480 | tf_op jit(solution)/shard_map/ppermute | solution.py:728
  97.5 27.8 %collective-permute-start.5 = (bf16[576,512]{1,0:T(8,128)(2,1)}, bf16[576,512]{1,0:T(8,128)(2,1)S(1)}, u32[]{:S(2)}, u32[]{:S(2)}) collective-permute-start(bf16[576,512]{1,0:T(8,128)(2,1)} %bitcast.22), channel_id=1, source_target_pairs={{0,8},{8,0},{16,24},{24,16},{1,9},{9,1},{17,25},{25,17},{2,10},{10... | collective-permute-start | bytes 1769480 | tf_op jit(solution)/shard_map/ppermute | solution.py:728
  126.1 32.4 %all-to-all-start.3 = ((bf16[8,288,512]{2,1,0:T(8,128)(2,1)}), bf16[8,288,512]{2,1,0:T(8,128)(2,1)S(1)}, u32[]{:S(2)}, u32[]{:S(2)}) async-start(bf16[8,288,512]{2,1,0:T(8,128)(2,1)} %bitcast.91), calls=%async_computation.3 | async-start | bytes 4718592 | tf_op jit(solution)/shard_map/all_to_all | solution.py:719
  130.0 15.7 %collective-permute-start.4 = (bf16[576,512]{1,0:T(8,128)(2,1)S(1)}, bf16[576,512]{1,0:T(8,128)(2,1)S(1)}, u32[]{:S(2)}, u32[]{:S(2)}) collective-permute-start(bf16[576,512]{1,0:T(8,128)(2,1)S(1)} %bitcast.105), channel_id=1, source_target_pairs={{0,8},{8,0},{16,24},{24,16},{1,9},{9,1},{17,25},{25,17},{2,10},{10... | collective-permute-start | bytes 1769480 | tf_op jit(solution)/shard_map/ppermute | solution.py:728
  130.5 29.5 %collective-permute-start.7 = (bf16[576,512]{1,0:T(8,128)(2,1)}, bf16[576,512]{1,0:T(8,128)(2,1)}, u32[]{:S(2)}, u32[]{:S(2)}) collective-permute-start(bf16[576,512]{1,0:T(8,128)(2,1)} %bitcast.22), channel_id=1, source_target_pairs={{0,24},{8,16},{16,8},{24,0},{1,25},{9,17},{17,9},{25,1},{2,26},{10... | collective-permute-start | bytes 1769480 | tf_op jit(solution)/shard_map/ppermute | solution.py:728
  160.1 52.7 %all-to-all-start.4 = ((bf16[8,2048,128]{2,1,0:T(8,128)(2,1)}), bf16[8,2048,128]{2,1,0:T(8,128)(2,1)}, u32[]{:S(2)}, u32[]{:S(2)}) async-start(bf16[8,2048,128]{2,1,0:T(8,128)(2,1)} %pack_weights.3), calls=%async_computation.4 | async-start | bytes 8388608 | tf_op jit(solution)/shard_map/all_to_all | solution.py:719
  164.7 65.7 %all-gather.14.cloned.1.call-start = ((), (), s32[]{:S(2)}) async-start(), calls=%async_computation.14 | async-start | bytes 3538944 | tf_op jit(solution)/shard_map/all_gather | solution.py:790
  212.8 29.2 %all-to-all-start.5 = ((bf16[8,1024,128]{2,1,0:T(8,128)(2,1)}), bf16[8,1024,128]{2,1,0:T(8,128)(2,1)S(1)}, u32[]{:S(2)}, u32[]{:S(2)}) async-start(bf16[8,1024,128]{2,1,0:T(8,128)(2,1)} %bitcast.100), calls=%async_computation.5 | async-start | bytes 4194304 | tf_op jit(solution)/shard_map/all_to_all | solution.py:719
  243.4 32.9 %all-to-all-start.6 = ((bf16[8,288,512]{2,1,0:T(8,128)(2,1)}), bf16[8,288,512]{2,1,0:T(8,128)(2,1)}, u32[]{:S(2)}, u32[]{:S(2)}) async-start(bf16[8,288,512]{2,1,0:T(8,128)(2,1)} %bitcast.95), calls=%async_computation.6 | async-start | bytes 4718592 | tf_op jit(solution)/shard_map/all_to_all | solution.py:719
  247.8 122.8 %all-gather.18.cloned.1.call-start = ((), (), s32[]{:S(2)}) async-start(), calls=%async_computation.16 | async-start | bytes 6291456 | tf_op jit(solution)/shard_map/all_gather | solution.py:731
  279.7 29.4 %all-to-all-start.7 = ((bf16[8,1024,128]{2,1,0:T(8,128)(2,1)}), bf16[8,1024,128]{2,1,0:T(8,128)(2,1)S(1)}, u32[]{:S(2)}, u32[]{:S(2)}) async-start(bf16[8,1024,128]{2,1,0:T(8,128)(2,1)} %bitcast.98), calls=%async_computation.7 | async-start | bytes 4194304 | tf_op jit(solution)/shard_map/all_to_all | solution.py:719
  310.4 51.9 %all-to-all-start.8 = ((bf16[16,144,512]{2,1,0:T(8,128)(2,1)}), bf16[16,144,512]{2,1,0:T(8,128)(2,1)}, u32[]{:S(2)}, u32[]{:S(2)}) async-start(bf16[16,144,512]{2,1,0:T(8,128)(2,1)} %pad_maximum_fusion), calls=%async_computation.8 | async-start | bytes 4718592 | tf_op jit(solution)/shard_map/all_to_all | solution.py:722
  314.9 183.2 %all-gather.20.cloned.1.call-start = ((), (), s32[]{:S(2)}) async-start(), calls=%async_computation.17 | async-start | bytes 6291456 | tf_op jit(solution)/shard_map/all_gather | solution.py:731
  362.4 29.2 %all-to-all-start.9 = ((bf16[8,1024,128]{2,1,0:T(8,128)(2,1)}), bf16[8,1024,128]{2,1,0:T(8,128)(2,1)S(1)}, u32[]{:S(2)}, u32[]{:S(2)}) async-start(bf16[8,1024,128]{2,1,0:T(8,128)(2,1)} %bitcast.99), calls=%async_computation.9 | async-start | bytes 4194304 | tf_op jit(solution)/shard_map/all_to_all | solution.py:719
  391.6 24.3 %all-to-all-start.10 = ((bf16[16,72,512]{2,1,0:T(8,128)(2,1)}), bf16[16,72,512]{2,1,0:T(8,128)(2,1)}, u32[]{:S(2)}, u32[]{:S(2)}) async-start(bf16[16,72,512]{2,1,0:T(8,128)(2,1)} %bitcast.55), calls=%async_computation.10 | async-start | bytes 2359296 | tf_op jit(solution)/shard_map/all_to_all | solution.py:722
  396.0 115.9 %all-gather.16.cloned.1.call-start = ((), (), s32[]{:S(2)}) async-start(), calls=%async_computation.15 | async-start | bytes 6291456 | tf_op jit(solution)/shard_map/all_gather | solution.py:731
  396.6 23.3 %copy-start.4 = (bf16[788,512]{1,0:T(8,128)(2,1)S(1)}, bf16[788,512]{1,0:T(8,128)(2,1)}, u32[]{:S(2)}) copy-start(bf16[788,512]{1,0:T(8,128)(2,1)} %param.13) | copy-start | bytes 2420740
  415.9 31.6 %all-to-all-start.11 = ((bf16[8,1024,128]{2,1,0:T(8,128)(2,1)}), bf16[8,1024,128]{2,1,0:T(8,128)(2,1)S(1)}, u32[]{:S(2)}, u32[]{:S(2)}) async-start(bf16[8,1024,128]{2,1,0:T(8,128)(2,1)} %bitcast.97), calls=%async_computation.11 | async-start | bytes 4194304 | tf_op jit(solution)/shard_map/all_to_all | solution.py:719
  447.5 30.8 %all-to-all-start.12 = ((bf16[8,1056,128]{2,1,0:T(8,128)(2,1)}), bf16[8,1056,128]{2,1,0:T(8,128)(2,1)}, u32[]{:S(2)}, u32[]{:S(2)}) async-start(bf16[8,1056,128]{2,1,0:T(8,128)(2,1)} %get-tuple-element.89), calls=%async_computation.12 | async-start | bytes 4325376 | tf_op jit(solution)/shard_map/all_to_all | solution.py:719
  451.8 92.8 %all-gather.22.cloned.1.call-start = ((), (), s32[]{:S(2)}) async-start(), calls=%async_computation.18 | async-start | bytes 6291456 | tf_op jit(solution)/shard_map/all_gather | solution.py:731
  480.3 15.2 %collective-permute-start.8 = (bf16[1056,128]{1,0:T(8,128)(2,1)S(1)}, bf16[1056,128]{1,0:T(8,128)(2,1)S(1)}, u32[]{:S(2)}, u32[]{:S(2)}) collective-permute-start(bf16[1056,128]{1,0:T(8,128)(2,1)S(1)} %get-tuple-element.113), channel_id=1, source_target_pairs={{0,8},{8,0},{16,24},{24,16},{1,9},{9,1},{17,25},{25,17},{2,10},{10... | collective-permute-start | bytes 811016 | tf_op jit(solution)/shard_map/ppermute | solution.py:728
  481.2 48.6 %all-to-all-start.13 = ((bf16[16,72,512]{2,1,0:T(8,128)(2,1)}), bf16[16,72,512]{2,1,0:T(8,128)(2,1)}, u32[]{:S(2)}, u32[]{:S(2)}) async-start(bf16[16,72,512]{2,1,0:T(8,128)(2,1)} %bitcast.59), calls=%async_computation.13 | async-start | bytes 2359296 | tf_op jit(solution)/shard_map/all_to_all | solution.py:722
  495.8 33.9 %collective-permute-start.9 = (bf16[1056,128]{1,0:T(8,128)(2,1)S(1)}, bf16[1056,128]{1,0:T(8,128)(2,1)S(1)}, u32[]{:S(2)}, u32[]{:S(2)}) collective-permute-start(bf16[1056,128]{1,0:T(8,128)(2,1)S(1)} %get-tuple-element.110), channel_id=1, source_target_pairs={{0,16},{8,24},{16,0},{24,8},{1,17},{9,25},{17,1},{25,9},{2,18},{10... | collective-permute-start | bytes 811016 | tf_op jit(solution)/shard_map/ppermute | solution.py:728
  (23 other events, 111.1 us)
Sparse Core Ops, SparseCore 0:
  11.8 68.8 all-gather.23
  250.2 58.2 all-gather.17
  317.3 72.1 all-gather.19
  398.1 58.7 all-gather.15
  458.2 80.2 all-gather.21
Sparse Core Ops, SparseCore 1:
  166.7 63.6 all-gather.13

commit v4 on v3

--- a/solution.py
+++ b/solution.py
@@ -824,14 +824,14 @@
             grads[g].append(in_plane(after_blocks(after(grad[1], gds[g + 1]))))
             swaps[g].append(with_near(grads[g][1]))
             gds[g + 1] = after(gds[g + 1], grads[g][1])
-            before = to_tokens([gx, y], grads[g][1])
+            put(1, g, True, ())
+            before = to_tokens(after_blocks([gx, y]), grads[g][1])
             y_back.append(before)
             gx_back.append(before)
         else:
             grads[g].append(in_plane(after(grad[0], before)))
             swaps[g].append(with_near(grads[g][0]))
             if g:
-                put(1, g - 1, True, ())
                 put(0, g - 1, False, ())
             before = to_tokens([after_blocks(gx)], grads[g][-1])
             gx_back.append(before)

time: 566 us -> 572 us (1.011)
  blocking collectives: 0 us -> 29.2 us
  waiting for transfers between devices: 240 us -> 223 us
    all_to_all x0 -> x1, blocking collectives: none -> 29.2 us  [in_plane(): return lax.all_to_all(values, ('wide', 'narrow'), 0, 0, tiled=True)]
    all_to_all x11 -> x10, waiting for transfers between devices: 124 us -> 107 us  [in_plane(): return lax.all_to_all(values, ('wide', 'narrow'), 0, 0, tiled=True)]
    all_to_all x11 -> x10, starting transfers between devices: 44.4 us -> 40.7 us  [in_plane(): return lax.all_to_all(values, ('wide', 'narrow'), 0, 0, tiled=True)]
  transfers between devices with their start and end apart: 30 -> 29, of which waited for: 18 -> 17; matrix products, arithmetic and copies ran while one was open for 6% -> 6% of each run, Pallas kernels for 33% -> 33%
where the time goes in v4:
time: 572 us; the launch traced here: 562 us
  waiting for transfers between devices  223 us (39%)
  Pallas kernels  189 us (33%)
  starting transfers between devices  64.8 us (11%)
  blocking collectives  29.2 us (5%)
  local copies, waits for them, and re-layouts  24.8 us (4%)
  between operations  16.2 us (3%)
  other arithmetic  15.5 us (3%)
    all_to_all x10, waiting for transfers between devices, in_plane(): return lax.all_to_all(values, ('wide', 'narrow'), 0, 0, tiled=True)  107 us
    pallas_call x2, Pallas kernels, expert(): pl.pallas_call(functools.partial(expert_kernel, deep, hidden, len(xs), ti...  69.4 us
    ppermute x6, waiting for transfers between devices, along(): lax.ppermute(values, ('pair', 'parity'), [(i, i ^ k) for i in range(plane...  56.7 us
    all_to_all x10, starting transfers between devices, in_plane(): return lax.all_to_all(values, ('wide', 'narrow'), 0, 0, tiled=True)  40.7 us
    pallas_call x8, Pallas kernels, place(): pl.pallas_call(place_kernel, grid_spec=pltpu.PrefetchScalarGridSpec(num_s...  33.1 us
    all_to_all x3, waiting for transfers between devices, in_pair(): lax.all_to_all(values, ('parity', 'wide', 'narrow'), 0, 0, tiled=True)  32.3 us
    all_to_all x1, blocking collectives, in_plane(): return lax.all_to_all(values, ('wide', 'narrow'), 0, 0, tiled=True)  29.2 us
    pallas_call x1, Pallas kernels, attention_back(): pl.pallas_call(functools.partial(backward_kernel, wide, narrow, len(backs...  25.7 us
  transfers between devices with their start and end apart: 29, of which 17 were waited for; matrix products, arithmetic and copies ran while one was open for 6% of the time, Pallas kernels for 33%

profile of v4, /device:TPU:0, one launch (start us, length us, event | category | flops | bytes accessed | tf_op | source)
XLA Modules:
  0.0 562.2 jit_solution(1987880771647846856)
XLA Ops:
  16.3 6.8 %pack_weights.2 = (bf16[8,1024,128]{2,1,0:T(8,128)(2,1)}, bf16[8,1024,128]{2,1,0:T(8,128)(2,1)}) custom-call(s32[1]{0:T(128)} %bitcast.17.first_ref, bf16[32,256,512]{2,1,0:T(8,128)(2,1)} %w_in_ref.3, bf16[32,512,256]{2,1,0:T(8,128)(2,1)} %w_out_ref.3), custom_call_target="tpu_custom_call" | custom-call | bytes 9000000 | tf_op jit(solution)/shard_map/pack_weights/pallas_call | solution.py:327
  23.1 4.3 all-to-all-start
  40.8 15.1 %attention_forward.1 = (bf16[4,197,1536]{2,1,0:T(8,128)(2,1)}, bf16[4,197,512]{2,1,0:T(8,128)(2,1)}, f32[4,197,512]{2,1,0:T(8,128)}, bf16[2304,512]{1,0:T(8,128)(2,1)}) custom-call(s32[3]{0:T(128)} %pad_add_fusion.spot_ref.refs_0_, bf16[4,197,512]{2,1,0:T(8,128)(2,1)} %reshape.156.tokens_ref.refs_1_, f32[4,512]{1,0:T(4,128)} %pad_maximum_fusion.8.norms_ref.refs_3_, ...), custom_call_target="tpu_custom_call" | custom-call | flops 6000000000 | bytes 9000000 | tf_op jit(solution)/shard_map/attention_forward/pallas_call | solution.py:283
  61.4 19.4 %all-gather.24.cloned.1.call-done.sent_ref = bf16[4,804,512]{2,1,0:T(8,128)(2,1)} async-done(((bf16[1,804,512]{2,1,0:T(8,128)(2,1)}), bf16[4,804,512]{2,1,0:T(8,128)(2,1)}) %all-gather.24.cloned.1.call-update) | async-done | bytes 3293200 | tf_op jit(solution)/shard_map/all_gather | solution.py:744
  80.8 9.2 %grad_slots.3 = bf16[8,4,72,512]{3,2,1,0:T(8,128)(2,1)} custom-call(s32[2]{0:T(128)} %pad_add_fusion.3.own_ref, bf16[4,804,512]{2,1,0:T(8,128)(2,1)} %all-gather.24.cloned.1.call-done.sent_ref), custom_call_target="tpu_custom_call" | custom-call | flops 8000000000 | bytes 10000000 | tf_op jit(solution)/shard_map/grad_slots/pallas_call | solution.py:169
  90.0 4.3 all-to-all-start.2
  99.0 6.7 %pack_weights.3 = bf16[8,2048,128]{2,1,0:T(8,128)(2,1)} custom-call(s32[1]{0:T(128)} %bitcast.32.first_ref, bf16[32,256,512]{2,1,0:T(8,128)(2,1)} %w_in_ref.3, bf16[32,512,256]{2,1,0:T(8,128)(2,1)} %w_out_ref.3), custom_call_target="tpu_custom_call" | custom-call | bytes 9000000 | tf_op jit(solution)/shard_map/pack_weights/pallas_call | solution.py:327
  105.7 19.0 %collective-permute-done.6.refs_2_ = bf16[576,512]{1,0:T(8,128)(2,1)S(1)} collective-permute-done((bf16[576,512]{1,0:T(8,128)(2,1)S(1)}, bf16[576,512]{1,0:T(8,128)(2,1)S(1)}, u32[]{:S(2)}, u32[]{:S(2)}) %collective-permute-start.6) | collective-permute-done | bytes 589856 | tf_op jit(solution)/shard_map/ppermute | solution.py:728
  132.5 13.2 %collective-permute-done.4 = bf16[576,512]{1,0:T(8,128)(2,1)S(1)} collective-permute-done((bf16[576,512]{1,0:T(8,128)(2,1)S(1)}, bf16[576,512]{1,0:T(8,128)(2,1)S(1)}, u32[]{:S(2)}, u32[]{:S(2)}) %collective-permute-start.4) | collective-permute-done | bytes 589856 | tf_op jit(solution)/shard_map/ppermute | solution.py:728
  146.8 11.7 %all-to-all-done.3 = bf16[8,288,512]{2,1,0:T(8,128)(2,1)S(1)} async-done(((bf16[8,288,512]{2,1,0:T(8,128)(2,1)}), bf16[8,288,512]{2,1,0:T(8,128)(2,1)S(1)}, u32[]{:S(2)}, u32[]{:S(2)}) %all-to-all-start.3) | async-done | bytes 2359328 | tf_op jit(solution)/shard_map/all_to_all | solution.py:719
  160.1 4.6 all-to-all-start.4
  165.5 34.7 %expert.2 = (bf16[2,4,1024,128]{3,2,1,0:T(8,128)(2,1)}, bf16[2,4,1024,128]{3,2,1,0:T(8,128)(2,1)}, bf16[1152,512]{1,0:T(8,128)(2,1)}, bf16[1152,512]{1,0:T(8,128)(2,1)}) custom-call(s32[2]{0:T(128)} %pad_add_fusion.2.where_ref, bf16[576,512]{1,0:T(8,128)(2,1)} %bitcast.106, bf16[576,512]{1,0:T(8,128)(2,1)} %copy-done.26, bf16[576,512]{1,0:T(8,128)(2,1)} %copy-done.25, ...), custom_call_target="tpu_custom_call" | custom-call | flops 24159191040 | bytes 20000000 | tf_op jit(solution)/shard_map/expert/pallas_call | solution.py:437
  200.2 12.6 %all-to-all-done.4 = bf16[8,2048,128]{2,1,0:T(8,128)(2,1)} async-done(((bf16[8,2048,128]{2,1,0:T(8,128)(2,1)}), bf16[8,2048,128]{2,1,0:T(8,128)(2,1)}, u32[]{:S(2)}, u32[]{:S(2)}) %all-to-all-start.4) | async-done | bytes 4194336 | tf_op jit(solution)/shard_map/all_to_all | solution.py:719
  216.4 9.2 %grad_slots.2 = bf16[8,4,72,512]{3,2,1,0:T(8,128)(2,1)} custom-call(s32[2]{0:T(128)} %pad_add_fusion.3.own_ref, bf16[4,804,512]{2,1,0:T(8,128)(2,1)} %all-gather.24.cloned.1.call-done.sent_ref), custom_call_target="tpu_custom_call" | custom-call | flops 8000000000 | bytes 10000000 | tf_op jit(solution)/shard_map/grad_slots/pallas_call | solution.py:169
  229.2 12.8 %all-to-all-done.5 = bf16[8,1024,128]{2,1,0:T(8,128)(2,1)S(1)} async-done(((bf16[8,1024,128]{2,1,0:T(8,128)(2,1)}), bf16[8,1024,128]{2,1,0:T(8,128)(2,1)S(1)}, u32[]{:S(2)}, u32[]{:S(2)}) %all-to-all-start.5) | async-done | bytes 2097184 | tf_op jit(solution)/shard_map/all_to_all | solution.py:719
  243.4 4.4 all-to-all-start.6
  253.3 23.0 %all-to-all-done.6 = bf16[8,288,512]{2,1,0:T(8,128)(2,1)} async-done(((bf16[8,288,512]{2,1,0:T(8,128)(2,1)}), bf16[8,288,512]{2,1,0:T(8,128)(2,1)}, u32[]{:S(2)}, u32[]{:S(2)}) %all-to-all-start.6) | async-done | bytes 2359328 | tf_op jit(solution)/shard_map/all_to_all | solution.py:719
  279.7 29.2 %all_to_all.70 = bf16[8,1024,128]{2,1,0:T(8,128)(2,1)} all-to-all(bf16[8,1024,128]{2,1,0:T(8,128)(2,1)S(1)} %bitcast.100), channel_id=1, replica_groups=mesh['pair'=2,'parity'=2,'wide'=2,'narrow'=4] {'wide','narrow'}, dimensions={0} | all-to-all | bytes 4194304 | tf_op jit(solution)/shard_map/all_to_all | solution.py:719
  308.8 4.2 place_grads.9.refs_0_
  319.2 34.7 %expert.3 = (bf16[2,4,1024,128]{3,2,1,0:T(8,128)(2,1)}, bf16[2,4,1024,128]{3,2,1,0:T(8,128)(2,1)}, bf16[1152,512]{1,0:T(8,128)(2,1)}, bf16[1152,512]{1,0:T(8,128)(2,1)}) custom-call(s32[2]{0:T(128)} %pad_add_fusion.2.where_ref, bf16[1152,512]{1,0:T(8,128)(2,1)} %pad_maximum_fusion.1.refs_0_, bf16[2,1152,512]{2,1,0:T(8,128)(2,1)} %bitcast.118, ...), custom_call_target="tpu_custom_call" | custom-call | flops 24159191040 | bytes 20000000 | tf_op jit(solution)/shard_map/expert/pallas_call | solution.py:437
  353.9 12.3 %all-to-all-done.8 = bf16[16,144,512]{2,1,0:T(8,128)(2,1)S(1)} async-done(((bf16[16,144,512]{2,1,0:T(8,128)(2,1)}), bf16[16,144,512]{2,1,0:T(8,128)(2,1)S(1)}, u32[]{:S(2)}, u32[]{:S(2)}) %all-to-all-start.8) | async-done | bytes 2359328 | tf_op jit(solution)/shard_map/all_to_all | solution.py:722
  376.1 20.8 %all-to-all-done.9 = bf16[8,1024,128]{2,1,0:T(8,128)(2,1)S(1)} async-done(((bf16[8,1024,128]{2,1,0:T(8,128)(2,1)}), bf16[8,1024,128]{2,1,0:T(8,128)(2,1)S(1)}, u32[]{:S(2)}, u32[]{:S(2)}) %all-to-all-start.9) | async-done | bytes 2097184 | tf_op jit(solution)/shard_map/all_to_all | solution.py:719
  396.9 4.4 all-to-all-start.10
  401.9 20.0 %all-to-all-done.10 = bf16[16,72,512]{2,1,0:T(8,128)(2,1)} async-done(((bf16[16,72,512]{2,1,0:T(8,128)(2,1)}), bf16[16,72,512]{2,1,0:T(8,128)(2,1)}, u32[]{:S(2)}, u32[]{:S(2)}) %all-to-all-start.10) | async-done | bytes 1179680 | tf_op jit(solution)/shard_map/all_to_all | solution.py:722
  427.7 25.7 %attention_backward.1 = (f32[4,197,512]{2,1,0:T(8,128)}, bf16[8,1056,128]{2,1,0:T(8,128)(2,1)}) custom-call(s32[3]{0:T(128)} %pad_add_fusion.spot_ref.refs_0_, bf16[4,197,512]{2,1,0:T(8,128)(2,1)} %reshape.156.tokens_ref.refs_1_, bf16[4,197,512]{2,1,0:T(8,128)(2,1)} %reshape.193.refs_2_, f32[4,512]{1,0:T(4,128)} %pad_maximum_fusion.8.norms_ref.refs_3_, ...), custom_call_target="tpu_custom_call" | custom-call | flops 8999999488 | bytes 12000000 | tf_op jit(solution)/shard_map/attention_backward/pallas_call | solution.py:653
  453.4 4.4 all-to-all-start.12
  458.4 25.8 %all-to-all-done.12 = bf16[8,1056,128]{2,1,0:T(8,128)(2,1)} async-done(((bf16[8,1056,128]{2,1,0:T(8,128)(2,1)}), bf16[8,1056,128]{2,1,0:T(8,128)(2,1)}, u32[]{:S(2)}, u32[]{:S(2)}) %all-to-all-start.12) | async-done | bytes 2162720 | tf_op jit(solution)/shard_map/all_to_all | solution.py:719
  487.1 4.4 all-to-all-start.13
  491.6 9.8 %collective-permute-done.8 = bf16[1056,128]{1,0:T(8,128)(2,1)S(1)} collective-permute-done((bf16[1056,128]{1,0:T(8,128)(2,1)S(1)}, bf16[1056,128]{1,0:T(8,128)(2,1)S(1)}, u32[]{:S(2)}, u32[]{:S(2)}) %collective-permute-start.8) | collective-permute-done | bytes 270368 | tf_op jit(solution)/shard_map/ppermute | solution.py:728
  507.5 4.3 place_grads.11.refs_0_
  521.4 14.2 %collective-permute-done.9 = bf16[1056,128]{1,0:T(8,128)(2,1)S(1)} collective-permute-done((bf16[1056,128]{1,0:T(8,128)(2,1)S(1)}, bf16[1056,128]{1,0:T(8,128)(2,1)S(1)}, u32[]{:S(2)}, u32[]{:S(2)}) %collective-permute-start.9) | collective-permute-done | bytes 270368 | tf_op jit(solution)/shard_map/ppermute | solution.py:728
  535.8 10.5 %mix.1 = bf16[4,197,512]{2,1,0:T(8,128)(2,1)} custom-call(f32[4,197,512]{2,1,0:T(8,128)} %get-tuple-element.91.refs_9_.resid_ref, s32[4,197,6]{2,1,0:T(8,128)} %reshape.207.refs_6_.slot_ref, f32[4,197,2]{2,1,0:T(8,128)} %copy.43.gates_ref, bf16[2304,512]{1,0:T(8,128)(2,1)} %bitcast.92, bf16[1152,512]{1,0:T(8,128)(2,1)} %bitcast.60.rest_1_), custom_call_target="tpu_custom_call" | custom-call | flops 6000000000 | bytes 6000000 | tf_op jit(solution)/shard_map/mix/pallas_call | solution.py:522
  (161 shorter events, 110.4 us)
Async XLA Ops:
  8.0 72.7 %all-gather.24.cloned.1.call-start = ((), (), s32[]{:S(2)}) async-start(), calls=%async_computation.19 | async-start | bytes 4136960 | tf_op jit(solution)/shard_map/all_gather | solution.py:744
  11.8 15.7 %collective-permute-start.1 = (bf16[1024,128]{1,0:T(8,128)(2,1)S(1)}, bf16[1024,128]{1,0:T(8,128)(2,1)S(1)}, u32[]{:S(2)}, u32[]{:S(2)}) collective-permute-start(bf16[1024,128]{1,0:T(8,128)(2,1)S(1)} %get-tuple-element.123), channel_id=1, source_target_pairs={{0,4},{1,5},{2,6},{3,7},{4,0},{5,1},{6,2},{7,3},{8,12},{9,13},{10,... | collective-permute-start | bytes 786440 | tf_op jit(solution)/shard_map/ppermute | solution.py:725
  14.8 13.2 %collective-permute-start.2 = (bf16[1024,128]{1,0:T(8,128)(2,1)S(1)}, bf16[1024,128]{1,0:T(8,128)(2,1)S(1)}, u32[]{:S(2)}, u32[]{:S(2)}) collective-permute-start(bf16[1024,128]{1,0:T(8,128)(2,1)S(1)} %get-tuple-element.123), channel_id=1, source_target_pairs={{0,6},{1,7},{2,4},{3,5},{4,2},{5,3},{6,0},{7,1},{8,14},{9,15},{10,... | collective-permute-start | bytes 786440 | tf_op jit(solution)/shard_map/ppermute | solution.py:725
  16.3 13.1 %collective-permute-start = (bf16[1024,128]{1,0:T(8,128)(2,1)S(1)}, bf16[1024,128]{1,0:T(8,128)(2,1)S(1)}, u32[]{:S(2)}, u32[]{:S(2)}) collective-permute-start(bf16[1024,128]{1,0:T(8,128)(2,1)S(1)} %get-tuple-element.123), channel_id=1, source_target_pairs={{0,2},{1,3},{2,0},{3,1},{4,6},{5,7},{6,4},{7,5},{8,10},{9,11},{10,... | collective-permute-start | bytes 786440 | tf_op jit(solution)/shard_map/ppermute | solution.py:725
  23.1 32.7 %all-to-all-start = ((bf16[8,1024,128]{2,1,0:T(8,128)(2,1)}), bf16[8,1024,128]{2,1,0:T(8,128)(2,1)S(1)}, u32[]{:S(2)}, u32[]{:S(2)}) async-start(bf16[8,1024,128]{2,1,0:T(8,128)(2,1)} %get-tuple-element.60), calls=%async_computation | async-start | bytes 4194304 | tf_op jit(solution)/shard_map/all_to_all | solution.py:719
  27.5 12.7 %copy-start.21 = (f32[512]{0:T(512)S(1)}, f32[512]{0:T(512)}, u32[]{:S(2)}) copy-start(f32[512]{0:T(512)} %param.19) | copy-start | bytes 6148
  27.5 12.7 %copy-start.22 = (f32[512]{0:T(512)S(1)}, f32[512]{0:T(512)}, u32[]{:S(2)}) copy-start(f32[512]{0:T(512)} %param.18) | copy-start | bytes 6148
  31.3 9.4 %collective-permute-start.3 = (bf16[4,1024,128]{2,1,0:T(8,128)(2,1)S(1)}, bf16[4,1024,128]{2,1,0:T(8,128)(2,1)}, u32[]{:S(2)}, u32[]{:S(2)}) collective-permute-start(bf16[4,1024,128]{2,1,0:T(8,128)(2,1)S(1)} %pad_maximum_fusion.2.weights_a_ref.refs_4_), channel_id=1, source_target_pairs={{0,1},{1,0},{2,3},{3,2},{4,5},{5,4},{6,7},{7,6},{8,9},{9,8},{10,11... | collective-permute-start | bytes 3145736 | tf_op jit(solution)/shard_map/ppermute | solution.py:725
  57.2 32.8 %all-to-all-start.1 = ((bf16[8,288,512]{2,1,0:T(8,128)(2,1)}), bf16[8,288,512]{2,1,0:T(8,128)(2,1)S(1)}, u32[]{:S(2)}, u32[]{:S(2)}) async-start(bf16[8,288,512]{2,1,0:T(8,128)(2,1)} %bitcast.94), calls=%async_computation.1 | async-start | bytes 4718592 | tf_op jit(solution)/shard_map/all_to_all | solution.py:719
  90.0 35.3 %all-to-all-start.2 = ((bf16[8,1024,128]{2,1,0:T(8,128)(2,1)}), bf16[8,1024,128]{2,1,0:T(8,128)(2,1)}, u32[]{:S(2)}, u32[]{:S(2)}) async-start(bf16[8,1024,128]{2,1,0:T(8,128)(2,1)} %get-tuple-element.64), calls=%async_computation.2 | async-start | bytes 4194304 | tf_op jit(solution)/shard_map/all_to_all | solution.py:719
  95.5 29.3 %collective-permute-start.6 = (bf16[576,512]{1,0:T(8,128)(2,1)S(1)}, bf16[576,512]{1,0:T(8,128)(2,1)S(1)}, u32[]{:S(2)}, u32[]{:S(2)}) collective-permute-start(bf16[576,512]{1,0:T(8,128)(2,1)S(1)} %bitcast.105), channel_id=1, source_target_pairs={{0,16},{8,24},{16,0},{24,8},{1,17},{9,25},{17,1},{25,9},{2,18},{10... | collective-permute-start | bytes 1769480 | tf_op jit(solution)/shard_map/ppermute | solution.py:728
  97.4 27.8 %collective-permute-start.5 = (bf16[576,512]{1,0:T(8,128)(2,1)}, bf16[576,512]{1,0:T(8,128)(2,1)S(1)}, u32[]{:S(2)}, u32[]{:S(2)}) collective-permute-start(bf16[576,512]{1,0:T(8,128)(2,1)} %bitcast.22), channel_id=1, source_target_pairs={{0,8},{8,0},{16,24},{24,16},{1,9},{9,1},{17,25},{25,17},{2,10},{10... | collective-permute-start | bytes 1769480 | tf_op jit(solution)/shard_map/ppermute | solution.py:728
  126.0 32.4 %all-to-all-start.3 = ((bf16[8,288,512]{2,1,0:T(8,128)(2,1)}), bf16[8,288,512]{2,1,0:T(8,128)(2,1)S(1)}, u32[]{:S(2)}, u32[]{:S(2)}) async-start(bf16[8,288,512]{2,1,0:T(8,128)(2,1)} %bitcast.93), calls=%async_computation.3 | async-start | bytes 4718592 | tf_op jit(solution)/shard_map/all_to_all | solution.py:719
  129.9 15.7 %collective-permute-start.4 = (bf16[576,512]{1,0:T(8,128)(2,1)S(1)}, bf16[576,512]{1,0:T(8,128)(2,1)S(1)}, u32[]{:S(2)}, u32[]{:S(2)}) collective-permute-start(bf16[576,512]{1,0:T(8,128)(2,1)S(1)} %bitcast.107), channel_id=1, source_target_pairs={{0,8},{8,0},{16,24},{24,16},{1,9},{9,1},{17,25},{25,17},{2,10},{10... | collective-permute-start | bytes 1769480 | tf_op jit(solution)/shard_map/ppermute | solution.py:728
  130.5 29.6 %collective-permute-start.7 = (bf16[576,512]{1,0:T(8,128)(2,1)}, bf16[576,512]{1,0:T(8,128)(2,1)}, u32[]{:S(2)}, u32[]{:S(2)}) collective-permute-start(bf16[576,512]{1,0:T(8,128)(2,1)} %bitcast.22), channel_id=1, source_target_pairs={{0,24},{8,16},{16,8},{24,0},{1,25},{9,17},{17,9},{25,1},{2,26},{10... | collective-permute-start | bytes 1769480 | tf_op jit(solution)/shard_map/ppermute | solution.py:728
  160.1 52.7 %all-to-all-start.4 = ((bf16[8,2048,128]{2,1,0:T(8,128)(2,1)}), bf16[8,2048,128]{2,1,0:T(8,128)(2,1)}, u32[]{:S(2)}, u32[]{:S(2)}) async-start(bf16[8,2048,128]{2,1,0:T(8,128)(2,1)} %pack_weights.3), calls=%async_computation.4 | async-start | bytes 8388608 | tf_op jit(solution)/shard_map/all_to_all | solution.py:719
  164.6 64.6 %all-gather.14.cloned.1.call-start = ((), (), s32[]{:S(2)}) async-start(), calls=%async_computation.14 | async-start | bytes 3538944 | tf_op jit(solution)/shard_map/all_gather | solution.py:790
  212.8 29.2 %all-to-all-start.5 = ((bf16[8,1024,128]{2,1,0:T(8,128)(2,1)}), bf16[8,1024,128]{2,1,0:T(8,128)(2,1)S(1)}, u32[]{:S(2)}, u32[]{:S(2)}) async-start(bf16[8,1024,128]{2,1,0:T(8,128)(2,1)} %bitcast.102), calls=%async_computation.5 | async-start | bytes 4194304 | tf_op jit(solution)/shard_map/all_to_all | solution.py:719
  243.4 32.9 %all-to-all-start.6 = ((bf16[8,288,512]{2,1,0:T(8,128)(2,1)}), bf16[8,288,512]{2,1,0:T(8,128)(2,1)}, u32[]{:S(2)}, u32[]{:S(2)}) async-start(bf16[8,288,512]{2,1,0:T(8,128)(2,1)} %bitcast.97), calls=%async_computation.6 | async-start | bytes 4718592 | tf_op jit(solution)/shard_map/all_to_all | solution.py:719
  247.8 124.1 %all-gather.18.cloned.1.call-start = ((), (), s32[]{:S(2)}) async-start(), calls=%async_computation.16 | async-start | bytes 6291456 | tf_op jit(solution)/shard_map/all_gather | solution.py:731
  314.7 51.5 %all-to-all-start.8 = ((bf16[16,144,512]{2,1,0:T(8,128)(2,1)}), bf16[16,144,512]{2,1,0:T(8,128)(2,1)S(1)}, u32[]{:S(2)}, u32[]{:S(2)}) async-start(bf16[16,144,512]{2,1,0:T(8,128)(2,1)} %pad_maximum_fusion), calls=%async_computation.8 | async-start | bytes 4718592 | tf_op jit(solution)/shard_map/all_to_all | solution.py:722
  318.5 185.0 %all-gather.20.cloned.1.call-start = ((), (), s32[]{:S(2)}) async-start(), calls=%async_computation.17 | async-start | bytes 6291456 | tf_op jit(solution)/shard_map/all_gather | solution.py:731
  367.6 29.2 %all-to-all-start.9 = ((bf16[8,1024,128]{2,1,0:T(8,128)(2,1)}), bf16[8,1024,128]{2,1,0:T(8,128)(2,1)S(1)}, u32[]{:S(2)}, u32[]{:S(2)}) async-start(bf16[8,1024,128]{2,1,0:T(8,128)(2,1)} %bitcast.101), calls=%async_computation.9 | async-start | bytes 4194304 | tf_op jit(solution)/shard_map/all_to_all | solution.py:719
  396.9 25.0 %all-to-all-start.10 = ((bf16[16,72,512]{2,1,0:T(8,128)(2,1)}), bf16[16,72,512]{2,1,0:T(8,128)(2,1)}, u32[]{:S(2)}, u32[]{:S(2)}) async-start(bf16[16,72,512]{2,1,0:T(8,128)(2,1)} %bitcast.55), calls=%async_computation.10 | async-start | bytes 2359296 | tf_op jit(solution)/shard_map/all_to_all | solution.py:722
  401.3 116.0 %all-gather.16.cloned.1.call-start = ((), (), s32[]{:S(2)}) async-start(), calls=%async_computation.15 | async-start | bytes 6291456 | tf_op jit(solution)/shard_map/all_gather | solution.py:731
  401.8 24.0 %copy-start.3 = (bf16[788,512]{1,0:T(8,128)(2,1)S(1)}, bf16[788,512]{1,0:T(8,128)(2,1)}, u32[]{:S(2)}) copy-start(bf16[788,512]{1,0:T(8,128)(2,1)} %param.13) | copy-start | bytes 2420740
  421.8 31.6 %all-to-all-start.11 = ((bf16[8,1024,128]{2,1,0:T(8,128)(2,1)}), bf16[8,1024,128]{2,1,0:T(8,128)(2,1)S(1)}, u32[]{:S(2)}, u32[]{:S(2)}) async-start(bf16[8,1024,128]{2,1,0:T(8,128)(2,1)} %bitcast.99), calls=%async_computation.11 | async-start | bytes 4194304 | tf_op jit(solution)/shard_map/all_to_all | solution.py:719
  453.4 30.8 %all-to-all-start.12 = ((bf16[8,1056,128]{2,1,0:T(8,128)(2,1)}), bf16[8,1056,128]{2,1,0:T(8,128)(2,1)}, u32[]{:S(2)}, u32[]{:S(2)}) async-start(bf16[8,1056,128]{2,1,0:T(8,128)(2,1)} %get-tuple-element.97), calls=%async_computation.12 | async-start | bytes 4325376 | tf_op jit(solution)/shard_map/all_to_all | solution.py:719
  457.8 92.8 %all-gather.22.cloned.1.call-start = ((), (), s32[]{:S(2)}) async-start(), calls=%async_computation.18 | async-start | bytes 6291456 | tf_op jit(solution)/shard_map/all_gather | solution.py:731
  486.3 15.2 %collective-permute-start.8 = (bf16[1056,128]{1,0:T(8,128)(2,1)S(1)}, bf16[1056,128]{1,0:T(8,128)(2,1)S(1)}, u32[]{:S(2)}, u32[]{:S(2)}) collective-permute-start(bf16[1056,128]{1,0:T(8,128)(2,1)S(1)} %get-tuple-element.121), channel_id=1, source_target_pairs={{0,8},{8,0},{16,24},{24,16},{1,9},{9,1},{17,25},{25,17},{2,10},{10... | collective-permute-start | bytes 811016 | tf_op jit(solution)/shard_map/ppermute | solution.py:728
  487.1 48.6 %all-to-all-start.13 = ((bf16[16,72,512]{2,1,0:T(8,128)(2,1)}), bf16[16,72,512]{2,1,0:T(8,128)(2,1)}, u32[]{:S(2)}, u32[]{:S(2)}) async-start(bf16[16,72,512]{2,1,0:T(8,128)(2,1)} %bitcast.59), calls=%async_computation.13 | async-start | bytes 2359296 | tf_op jit(solution)/shard_map/all_to_all | solution.py:722
  501.7 33.9 %collective-permute-start.9 = (bf16[1056,128]{1,0:T(8,128)(2,1)S(1)}, bf16[1056,128]{1,0:T(8,128)(2,1)S(1)}, u32[]{:S(2)}, u32[]{:S(2)}) collective-permute-start(bf16[1056,128]{1,0:T(8,128)(2,1)S(1)} %get-tuple-element.118), channel_id=1, source_target_pairs={{0,16},{8,24},{16,0},{24,8},{1,17},{9,25},{17,1},{25,9},{2,18},{10... | collective-permute-start | bytes 811016 | tf_op jit(solution)/shard_map/ppermute | solution.py:728
  (24 other events, 106.0 us)
Sparse Core Ops, SparseCore 0:
  11.8 68.8 all-gather.23
  250.1 57.1 all-gather.17
  320.9 72.1 all-gather.19
  403.3 58.7 all-gather.15
  463.5 79.5 all-gather.21
Sparse Core Ops, SparseCore 1:
  166.6 62.5 all-gather.13
